TPU v7x, 32 devices: a whole 2x2x4 slice. The times are simulated.
32 devices in a mesh: grp: 2 (over x), dp: 4 (over y, core), tp: 4 (over z).
Axes of the slice: x: 2, y: 2, z: 4, core: 2. Of those that a mesh axis runs over, the one named last changes fastest.
Arguments:
- query: bfloat16 [256, 6144], P(('grp', 'dp'), 'tp'), parts along dimension 0, may hold values from -200 to 200
- key_value_new: bfloat16 [256, 2048], P(('grp', 'dp'), 'tp'), parts along dimension 0, may hold values from -6 to 6
- key_value_cache: bfloat16 [256, 160, 2048], P(('grp', 'dp'), None, 'tp'), parts along dimension 0, may hold values from -7 to 7
- cache_len: int32 [256], P(('grp', 'dp')), parts along dimension 0, may hold values from 2 to 160, as said below
- out_proj: bfloat16 [6144, 6144], P('tp', 'dp'), may hold values from -0.078125 to 0.078125
- residual: bfloat16 [256, 6144], P('grp', 'dp'), parts along dimension 0, may hold values from -80 to 80
- norm_gain: float32 [6144], P('dp'), may hold values from 0.5 to 1.5
- routes: int32 [256, 2], P('grp'), parts along dimension 0, may hold values from 0 to 3, all different within a row; in each aligned block of 128 rows (0 to 127, 128 to 255, ...) at most 96 rows name the same one
- route_weight: float32 [256, 2], P('grp'), parts along dimension 0, may hold values from 0.25 to 1
- w_gate: bfloat16 [6144, 32768], P(None, ('dp', 'tp')), may hold values from -0.078125 to 0.078125
- w_up: bfloat16 [6144, 32768], P(None, ('dp', 'tp')), may hold values from -0.078125 to 0.078125
- w_down: bfloat16 [32768, 6144], P(('dp', 'tp')), may hold values from -0.09375 to 0.09375
Outputs:
- attended: bfloat16 [256, 6144], P(('grp', 'tp'), 'dp'), parts along dimension 0
- expert_mix: bfloat16 [256, 6144], P(('grp', 'tp'), 'dp'), parts along dimension 0
There are 2 independent parts, one for each index of `grp`. A program takes and returns all parts, laid end to end along the dimension named above; an argument that names none is the same for every part. Nothing has to cross between parts.
Inputs may be any that keep to these rules, and one draw needn't show every extreme that they name: `cache_len`: in every block of 32 requests of one index of dp, one request has exactly 160. `routes`: each request names 2 different experts; no expert is named by more than 96 requests, a bound that some block reaches.
All inputs are finite; a program needn't handle non-finite values.
Results may differ from a plain program's by a relative error of at most 0.017.
Values may be sent and summed in bfloat16 or wider, within the bound.
No kernel may reach another device: no remote copies, remote signals or barrier semaphores. Data moves between devices by JAX's collectives and lax.ppermute only.
A program may use at most 256 MiB of HBM per device.

v0:
```python
import jax
import jax.numpy as jnp
from jax import lax
from jax.sharding import PartitionSpec as P

D = 6144
QUERY_HEADS = 48
KEY_VALUE_HEADS = 8
HEAD_SIZE = 128
EXPERTS = 4
TOP = 2


EPS = 1e-05


def attend(query_heads, fresh_entry, cache_tensor, lengths):
    scale = 1.0 / HEAD_SIZE**0.5
    keys = cache_tensor[:, :, :, 0, :]
    value_rows = cache_tensor[:, :, :, 1, :]
    s_cache = (
        jnp.einsum("rkgd,rckd->rkgc", query_heads, keys, preferred_element_type=jnp.float32) * scale
    )
    s_self = (
        jnp.einsum(
            "rkgd,rkd->rkg",
            query_heads,
            fresh_entry[:, :, 0, :],
            preferred_element_type=jnp.float32,
        )
        * scale
    )
    positions = jnp.arange(cache_tensor.shape[1], dtype=jnp.int32)
    valid = (positions[None, :] < lengths[:, None])[:, None, None, :]
    s_cache = jnp.where(valid, s_cache, -jnp.inf)
    top = jnp.maximum(jnp.max(s_cache, axis=-1), s_self)
    e_cache = jnp.where(valid, jnp.exp(s_cache - top[..., None]), 0.0)
    e_self = jnp.exp(s_self - top)
    total = jnp.sum(e_cache, axis=-1) + e_self
    p_cache = (e_cache / total[..., None]).astype(jnp.bfloat16)
    p_self = (e_self / total).astype(jnp.bfloat16)
    ctx = jnp.einsum("rkgc,rckd->rkgd", p_cache, value_rows, preferred_element_type=jnp.float32)
    ctx = ctx + p_self.astype(jnp.float32)[..., None] * fresh_entry[:, :, None, 1, :].astype(
        jnp.float32
    )
    return ctx.astype(jnp.bfloat16).reshape(query_heads.shape[0], -1)


def make_slots(routes, experts, capacity):
    flat = routes.reshape(-1)
    count = flat.shape[0]
    onehot = (flat[:, None] == jnp.arange(experts, dtype=jnp.int32)[None, :]).astype(jnp.int32)
    rank = jnp.cumsum(onehot, axis=0) - onehot
    slot = jnp.sum(rank * onehot, axis=1)
    owner = jnp.arange(count, dtype=jnp.int32) // routes.shape[1]
    table = jnp.full((experts, capacity), routes.shape[0], jnp.int32).at[flat, slot].set(owner)
    return (flat, slot, table)


def expert_ffn(rows_in, wg, wu, wd):
    gate = jnp.dot(rows_in, wg, preferred_element_type=jnp.float32)
    up = jnp.dot(rows_in, wu, preferred_element_type=jnp.float32)
    hidden = (jax.nn.silu(gate) * up).astype(jnp.bfloat16)
    return jnp.dot(hidden, wd, preferred_element_type=jnp.float32)


def send_back(part_out):
    return lax.all_to_all(
        part_out[None].astype(jnp.bfloat16), "dp", split_axis=2, concat_axis=0, tiled=True
    ).astype(jnp.float32)


def body(
    query,
    key_value_new,
    key_value_cache,
    cache_len,
    out_proj,
    residual,
    norm_gain,
    routes,
    route_weight,
    w_gate,
    w_up,
    w_down,
):
    n_dp = lax.axis_size("dp")
    n_tp = lax.axis_size("tp")
    rows_here = query.shape[0]
    kv_here = key_value_new.shape[1] // (2 * HEAD_SIZE)
    head_groups = QUERY_HEADS // KEY_VALUE_HEADS
    query_heads = query.reshape(rows_here, kv_here, head_groups, HEAD_SIZE)
    fresh_entry = key_value_new.reshape(rows_here, kv_here, 2, HEAD_SIZE)
    cache_tensor = key_value_cache.reshape(
        rows_here, key_value_cache.shape[1], kv_here, 2, HEAD_SIZE
    )
    context = attend(query_heads, fresh_entry, cache_tensor, cache_len)
    partial_proj = jnp.dot(
        lax.all_gather(context, "dp", axis=0, tiled=True),
        out_proj,
        preferred_element_type=jnp.float32,
    )
    total_rows = partial_proj.shape[0]
    share = total_rows // n_tp
    tensor_index = lax.axis_index("tp")
    stream = residual.astype(jnp.float32)
    proj = lax.psum(partial_proj.astype(jnp.bfloat16), "tp").astype(jnp.float32)
    x = stream + proj
    squares = lax.psum(jnp.sum(x * x, axis=1), "dp")
    normed = (x * lax.rsqrt(squares / D + EPS)[:, None] * norm_gain[None, :]).astype(jnp.bfloat16)
    attended = lax.dynamic_slice_in_dim(x, tensor_index * share, share, 0).astype(jnp.bfloat16)
    capacity = 3 * total_rows // 4
    owners = n_dp // EXPERTS
    flat, slot, table = make_slots(routes, EXPERTS, capacity)
    picked = jnp.take(normed, table, axis=0, mode="fill", fill_value=0)
    outgoing = jnp.repeat(picked, owners, axis=0)
    part_out = expert_ffn(
        lax.all_to_all(outgoing, "dp", split_axis=0, concat_axis=2, tiled=True)[0],
        w_gate,
        w_up,
        w_down,
    )
    back = send_back(part_out)
    per_expert = jnp.sum(back.reshape(EXPERTS, owners, capacity, back.shape[2]), axis=1)
    gathered = per_expert[flat, slot]
    weighted = gathered * route_weight.reshape(-1)[:, None]
    combined = jnp.sum(weighted.reshape(total_rows, TOP, back.shape[2]), axis=1)
    expert_mix = lax.psum_scatter(
        combined.astype(jnp.bfloat16), "tp", scatter_dimension=0, tiled=True
    )
    return (attended, expert_mix)


def solution(mesh):
    in_specs = (
        P(("grp", "dp"), "tp"),
        P(("grp", "dp"), "tp"),
        P(("grp", "dp"), None, "tp"),
        P(("grp", "dp")),
        P("tp", "dp"),
        P("grp", "dp"),
        P("dp"),
        P("grp", None),
        P("grp", None),
        P(None, ("dp", "tp")),
        P(None, ("dp", "tp")),
        P(("dp", "tp"), None),
    )
    out_specs = (P(("grp", "tp"), "dp"), P(("grp", "tp"), "dp"))
    return jax.shard_map(body, mesh=mesh, in_specs=in_specs, out_specs=out_specs, check_vma=False)
```

profile of v0, /device:TPU:0, one launch (start us, length us, event | category | flops | bytes accessed | tf_op | source)
XLA Modules:
  0.0 260.1 jit_solution(10105563833841051826)
XLA Ops:
  7.2 0.0 all-reduce.2.cloned.1.call-start
  7.2 8.3 %reshape.120 = bf16[32,160,2,2,128]{4,3,2,1,0:T(2,128)(2,1)} reshape(bf16[32,160,512]{2,1,0:T(8,128)(2,1)} %param.14) | data formatting | bytes 10485760 | tf_op jit(solution)/shard_map/reshape | solution.py:94
  15.6 17.5 %fusion.30 = (bf16[32,160,2,1,128]{4,3,2,1,0:T(2,128)(2,1)}, bf16[32,160,2,1,128]{4,3,2,1,0:T(2,128)(2,1)}) fusion(bf16[32,160,2,2,128]{4,3,2,1,0:T(2,128)(2,1)} %reshape.120), kind=kLoop, calls=%fused_computation.69 | loop fusion | bytes 10485760 | tf_op jit(solution)/shard_map/slice | solution.py:19
  33.1 0.0 copy-done.2
  33.1 0.1 reshape.119
  33.2 0.0 copy-done.7
  33.3 0.1 iota_compare_fusion
  33.3 0.0 copy-done.3
  33.4 0.2 fusion.19
  33.6 4.1 %fusion.31 = (f32[32,2,6]{2,1,0:T(2,128)S(1)}, f32[32,2,6,160]{3,2,1,0:T(8,128)S(1)}) fusion(bf16[32,2,6,128]{3,2,1,0:T(8,128)(2,1)S(1)} %reshape.119, bf16[32,160,2,1,128]{4,3,2,1,0:T(2,128)(2,1)} %get-tuple-element.4, pred[32,160]{1,0:T(8,128)(4,1)S(1)} %iota_compare_fusion), kind=kOutput, calls=%fused_computation.70 | convolution fusion | flops 15912576 | bytes 2972160 | tf_op jit(solution)/shard_map/rkgd,rckd->rkgc/dot_general | solution.py:22
  37.7 0.3 fusion.13
  38.0 0.1 fusion.21
  38.1 3.4 %fusion.7 = bf16[32,2,6,128]{3,2,1,0:T(8,128)(2,1)S(1)} fusion(bf16[32,160,2,1,128]{4,3,2,1,0:T(2,128)(2,1)} %get-tuple-element.5, f32[32,2,6,160]{3,2,1,0:T(8,128)S(1)} %get-tuple-element.11, f32[32,2,6]{2,1,0:T(2,128)S(1)} %get-tuple-element.7, f32[32,2,6]{2,1,0:T(2,128)S(1)} %multiply_maximum_fusion, pred[32,160]{1,0:T(8,128)(4,1)S(1)} %iota_compare_fusion, ...), kind=kOutput, calls=%fused_computation.18 | convolution fusion | flops 16121856 | bytes 3008000 | tf_op jit(solution)/shard_map/rkgc,rckd->rkgd/dot_general | solution.py:42
  41.5 0.1 reshape.122
  41.6 7.9 %all_gather.3 = bf16[128,1536]{1,0:T(8,128)(2,1)S(1)} all-gather(bf16[32,1536]{1,0:T(8,128)(2,1)S(1)} %reshape.122), channel_id=1, replica_groups=mesh['grp'=2,'dp'=4,'tp'=4] {'dp'}, dimensions={0}, use_global_device_ids=true | all-gather | bytes 491520 | tf_op jit(solution)/shard_map/all_gather | solution.py:99
  49.5 3.9 %convolution_convert_fusion.1 = bf16[128,1536]{1,0:T(8,128)(2,1)} fusion(bf16[128,1536]{1,0:T(8,128)(2,1)S(1)} %all_gather.3, bf16[1536,1536]{1,0:T(8,128)(2,1)} %param.16), kind=kOutput, calls=%fused_computation.9 | convolution fusion | flops 604176384 | bytes 5505024 | tf_op jit(solution)/shard_map/dot_general | solution.py:98
  53.4 0.0 all-reduce.2.cloned.1.call-update
  53.4 0.0 copy-done.5
  53.5 0.1 copy.70
  53.6 0.1 reshape.123
  53.7 0.1 eq.29
  53.9 0.1 eq.25
  54.0 1.2 reduce-window.6
  55.2 0.1 slice.34
  55.3 0.1 copy.73
  55.5 0.1 copy.74
  55.6 0.1 add_bitcast_fusion
  55.7 11.4 %scatter_fusion = s32[4,96]{1,0:T(4,128)S(1)} fusion(s32[4,96]{1,0:T(4,128)S(1)} %broadcast_in_dim.50, s32[256]{0:T(256)S(1)} %bitcast.78, s32[256]{0:T(256)S(1)} %and_select_fusion), kind=kCustom, calls=%fused_computation.2 | custom fusion | bytes 5120 | tf_op jit(solution)/shard_map/scatter | solution.py:56
  67.2 0.1 reshape.130
  67.3 24.4 %all-reduce.2.cloned.1.call-done = bf16[128,1536]{1,0:T(8,128)(2,1)} async-done(((bf16[128,1536]{1,0:T(8,128)(2,1)}), bf16[128,1536]{1,0:T(8,128)(2,1)}) %all-reduce.2.cloned.1.call-update) | async-done | bytes 393232 | tf_op jit(solution)/shard_map/psum | solution.py:107
  91.6 0.0 copy-done
  91.6 1.2 multiply_reduce_fusion.1
  92.8 5.7 %psum.15 = f32[128]{0:T(128)S(1)} all-reduce(f32[128]{0:T(128)S(1)} %multiply_reduce_fusion.1), channel_id=1, replica_groups=mesh['grp'=2,'dp'=4,'tp'=4] {'dp'}, use_global_device_ids=true, to_apply=%region_8.9 | all-reduce | flops 128 | bytes 1024 | tf_op jit(solution)/shard_map/psum | solution.py:109
  98.5 0.0 copy-done.4
  98.5 1.2 multiply_convert_fusion
  99.7 2.2 gather_fusion
  101.9 0.1 broadcast_select_fusion
  102.1 18.3 %all_to_all.24 = bf16[4,96,1536]{2,1,0:T(8,128)(2,1)S(1)} all-to-all(bf16[4,96,1536]{2,1,0:T(8,128)(2,1)S(1)} %broadcast_select_fusion), channel_id=1, replica_groups=mesh['grp'=2,'dp'=4,'tp'=4] {'dp'}, dimensions={0} | all-to-all | bytes 2359296 | tf_op jit(solution)/shard_map/all_to_all | solution.py:118
  120.4 0.9 copy.75
  121.3 0.2 copy.86
  121.5 10.3 %fusion.32 = f32[96,2048]{1,0:T(8,128)S(1)} fusion(bf16[96,6144]{1,0:T(8,128)(2,1)S(1)} %bitcast.75, bf16[6144,2048]{1,0:T(8,128)(2,1)} %param.21), kind=kOutput, calls=%fused_computation.71 | convolution fusion | flops 2415919104 | bytes 27131904 | tf_op jit(solution)/shard_map/dot_general | solution.py:61
  131.8 19.7 %fusion = bf16[1,96,6144]{2,1,0:T(8,128)(2,1)S(1)} fusion(bf16[2048,6144]{1,0:T(8,128)(2,1)} %param.23, bf16[96,6144]{1,0:T(8,128)(2,1)S(1)} %bitcast.76, bf16[6144,2048]{1,0:T(8,128)(2,1)} %param.22, f32[96,2048]{1,0:T(8,128)S(1)} %fusion.32), kind=kOutput, calls=%fused_computation.4 | convolution fusion | flops 4833607680 | bytes 53477376 | tf_op jit(solution)/shard_map/dot_general | solution.py:64
  151.5 5.1 %copy.76 = bf16[1,96,6144]{1,0,2:T(2,128)(2,1)} copy(bf16[1,96,6144]{2,1,0:T(8,128)(2,1)S(1)} %fusion) | data formatting | bytes 2359296 | tf_op jit(solution)/shard_map/convert_element_type | solution.py:69
  156.6 0.5 broadcast.159
  157.2 34.6 %reduce = bf16[6144,96]{1,0:T(8,128)(2,1)S(1)} reduce(bf16[6144,1,96]{2,1,0:T(2,128)(2,1)} %bitcast.79, bf16[]{:T(256)} %broadcast.159), dimensions={1}, to_apply=%bitcast.58.reduce_sub_computation | reduce | bytes 2359298
  191.7 0.0 copy-start.6
  191.7 3.3 %reshape.152 = bf16[4,2,73728]{2,1,0:T(2,128)(2,1)} reshape(bf16[6144,96]{1,0:T(8,128)(2,1)S(1)} %reduce) | data formatting | bytes 2359296
  195.1 3.5 %all-to-all-start.1 = ((bf16[4,2,73728]{2,1,0:T(2,128)(2,1)}), bf16[4,2,73728]{2,1,0:T(2,128)(2,1)S(1)}, u32[]{:S(2)}, u32[]{:S(2)}) async-start(bf16[4,2,73728]{2,1,0:T(2,128)(2,1)} %reshape.152), calls=%async_computation.1 | async-start | bytes 2359296 | tf_op jit(solution)/shard_map/all_to_all | solution.py:68
  198.6 0.0 reduce-scatter.2.cloned.1.call-start
  198.6 0.0 copy-done.6
  198.6 0.1 copy.79
  198.8 15.7 %all-to-all-done.1 = bf16[4,2,73728]{2,1,0:T(2,128)(2,1)S(1)} async-done(((bf16[4,2,73728]{2,1,0:T(2,128)(2,1)}), bf16[4,2,73728]{2,1,0:T(2,128)(2,1)S(1)}, u32[]{:S(2)}, u32[]{:S(2)}) %all-to-all-start.1) | async-done | bytes 1179680 | tf_op jit(solution)/shard_map/all_to_all | solution.py:68
  214.4 3.3 %reshape.153 = bf16[6144,1,96]{2,1,0:T(2,128)(2,1)} reshape(bf16[4,2,73728]{2,1,0:T(2,128)(2,1)S(1)} %all-to-all-done.1) | data formatting | bytes 2359296
  217.7 6.1 %copy.77 = bf16[1,96,6144]{2,1,0:T(8,128)(2,1)S(1)} copy(bf16[1,96,6144]{1,0,2:T(2,128)(2,1)} %bitcast.80) | data formatting | bytes 2359296 | tf_op jit(solution)/shard_map/all_to_all | solution.py:68
  223.8 0.2 reduce_sum.55
  224.1 0.2 copy.106
  224.2 4.0 %gather_fusion.1 = f32[256,1536]{1,0:T(8,128)} fusion(f32[4,96,1536]{2,1,0:T(8,128)S(1)} %bitcast.74, s32[256]{0:T(256)S(1)} %bitcast.77), kind=kCustom, calls=%fused_computation.1 | custom fusion | bytes 3147776 | tf_op jit(solution)/shard_map/gather | solution.py:125
  228.2 2.3 gather.11
  230.5 2.9 %multiply_reduce_fusion = bf16[128,1536]{1,0:T(8,128)(2,1)} fusion(f32[128,2,1536]{2,1,0:T(2,128)S(1)} %gather.11, f32[128,2]{1,0:T(8,128)S(1)} %copy.79), kind=kLoop, calls=%fused_computation.13 | loop fusion | flops 589824 | bytes 1967104 | tf_op jit(solution)/shard_map/reduce_sum | solution.py:127
  233.4 0.0 reduce-scatter.2.cloned.1.call-update
  233.5 0.0 copy-done.1
  233.5 0.1 convert_add_fusion
  233.6 0.7 dynamic-slice_convert_fusion
  234.2 19.0 %reduce-scatter.2.cloned.1.call-done = bf16[32,1536]{1,0:T(8,128)(2,1)} async-done(((bf16[128,1536]{1,0:T(8,128)(2,1)}), bf16[32,1536]{1,0:T(8,128)(2,1)}) %reduce-scatter.2.cloned.1.call-update) | async-done | bytes 98320 | tf_op jit(solution)/shard_map/reduce_scatter | solution.py:128
  (22 shorter events, 0.2 us)
Async XLA Ops:
  7.2 84.5 %all-reduce.2.cloned.1.call-start = ((), (), s32[]{:S(2)}) async-start(), calls=%async_computation.3 | async-start | bytes 786432 | tf_op jit(solution)/shard_map/psum | solution.py:107
  15.5 17.6 %copy-start.2 = (bf16[32,1536]{1,0:T(8,128)(2,1)S(1)}, bf16[32,1536]{1,0:T(8,128)(2,1)}, u32[]{:S(2)}) copy-start(bf16[32,1536]{1,0:T(8,128)(2,1)} %param.12) | copy-start | bytes 294916
  15.6 17.7 %copy-start.7 = (s32[32]{0:T(128)S(1)}, s32[32]{0:T(128)}, u32[]{:S(2)}) copy-start(s32[32]{0:T(128)} %param.15) | copy-start | bytes 388
  15.6 17.8 %copy-start.3 = (bf16[32,512]{1,0:T(8,128)(2,1)S(1)}, bf16[32,512]{1,0:T(8,128)(2,1)}, u32[]{:S(2)}) copy-start(bf16[32,512]{1,0:T(8,128)(2,1)} %param.13) | copy-start | bytes 98308
  49.5 3.9 %copy-start.5 = (s32[128,2]{0,1:T(2,128)S(1)}, s32[128,2]{0,1:T(2,128)}, u32[]{:S(2)}) copy-start(s32[128,2]{0,1:T(2,128)} %param.19) | copy-start | bytes 3076
  53.4 38.2 %copy-start = (bf16[128,1536]{1,0:T(8,128)(2,1)S(1)}, bf16[128,1536]{1,0:T(8,128)(2,1)}, u32[]{:S(2)}) copy-start(bf16[128,1536]{1,0:T(8,128)(2,1)} %param.17) | copy-start | bytes 1179652
  53.4 45.1 %copy-start.4 = (f32[1536]{0:T(1024)S(1)}, f32[1536]{0:T(1024)}, u32[]{:S(2)}) copy-start(f32[1536]{0:T(1024)} %param.18) | copy-start | bytes 18436
  191.7 6.9 %copy-start.6 = (f32[128,2]{0,1:T(2,128)S(1)}, f32[128,2]{0,1:T(2,128)}, u32[]{:S(2)}) copy-start(f32[128,2]{0,1:T(2,128)} %param.20) | copy-start | bytes 3076
  195.1 19.4 %all-to-all-start.1 = ((bf16[4,2,73728]{2,1,0:T(2,128)(2,1)}), bf16[4,2,73728]{2,1,0:T(2,128)(2,1)S(1)}, u32[]{:S(2)}, u32[]{:S(2)}) async-start(bf16[4,2,73728]{2,1,0:T(2,128)(2,1)} %reshape.152), calls=%async_computation.1 | async-start | bytes 2359296 | tf_op jit(solution)/shard_map/all_to_all | solution.py:68
  198.6 54.7 %reduce-scatter.2.cloned.1.call-start = ((), (), s32[]{:S(2)}) async-start(), calls=%async_computation.4 | async-start | bytes 491520 | tf_op jit(solution)/shard_map/reduce_scatter | solution.py:128
  228.2 5.3 %copy-start.1 = (bf16[128,1536]{1,0:T(8,128)(2,1)S(1)}, bf16[128,1536]{1,0:T(8,128)(2,1)}, u32[]{:S(2)}) copy-start(bf16[128,1536]{1,0:T(8,128)(2,1)} %all-reduce.2.cloned.1.call-done) | copy-start | bytes 1179652
Sparse Core Ops, SparseCore 0:
  53.6 38.0 all-reduce.1
  233.6 19.6 reduce-scatter.1
where the time goes:
time: 261 us; the launch traced here: 260 us
  local copies, waits for them, and re-layouts  67.5 us (26%)
  waiting for transfers between devices  59.1 us (23%)
  other arithmetic  42.2 us (16%)
  matrix products  41.5 us (16%)
  blocking collectives  31.9 us (12%)
  between operations  14.3 us (5%)
  starting transfers between devices  3.61 us (1%)
    unnamed x2, other arithmetic  34.6 us
    psum x1, waiting for transfers between devices, body(): proj = lax.psum(partial_proj.astype(jnp.bfloat16), 'tp').astype(jnp.float32)  24.4 us
    dot_general x1, matrix products, expert_ffn(): return jnp.dot(hidden, wd, preferred_element_type=jnp.float32)  19.7 us
    reduce_scatter x1, waiting for transfers between devices, body(): lax.psum_scatter(combined.astype(jnp.bfloat16), 'tp', scatter_dimension=0...  19 us
    all_to_all x1, blocking collectives, body(): lax.all_to_all(outgoing, 'dp', split_axis=0, concat_axis=2, tiled=True)[0]  18.3 us
    slice x1, local copies, waits for them, and re-layouts, attend(): keys = cache_tensor[:, :, :, 0, :]  17.5 us
    all_to_all x1, waiting for transfers between devices, send_back(): lax.all_to_all(part_out[None].astype(jnp.bfloat16), 'dp', split_axis=2, c...  15.7 us
    scatter x1, local copies, waits for them, and re-layouts, make_slots(): jnp.full((experts, capacity), routes.shape[0], jnp.int32).at[flat, slot]  11.4 us
  transfers between devices with their start and end apart: 3, of which 3 were waited for; matrix products, arithmetic and copies ran while one was open for 6% of the time, Pallas kernels for 0%

commit v1 on v0

v1 whole, which is shorter than its diff:
```python
import functools

import jax
import jax.numpy as jnp
from jax import lax
from jax.experimental import pallas as pl
from jax.experimental.pallas import tpu as pltpu
from jax.sharding import PartitionSpec as P

QUERY_HEADS = 48
KEY_VALUE_HEADS = 8
HEAD_SIZE = 128
EXPERTS = 4
EPS = 1e-05
MIB = 1 << 20
VM = pltpu.VMEM
f32, bf16 = jnp.float32, jnp.bfloat16


def swap(x, axis, k):
    n = lax.axis_size(axis)
    return lax.ppermute(x, axis, [(i, i ^ k) for i in range(n)])


def whole(n):
    return [pl.BlockSpec(memory_space=VM) for _ in range(n)]


def attend_kernel(kv, group, len_ref, q_ref, new_ref, cache_ref, out_ref):
    batch, slots = cache_ref.shape[0], cache_ref.shape[1]
    first = pl.program_id(0) * batch
    scale = 1.0 / HEAD_SIZE**0.5
    pos = lax.broadcasted_iota(jnp.int32, (1, 8, slots), 2)
    valid = jnp.concatenate([pos < len_ref[first + b] for b in range(batch)], axis=0)
    for h in range(kv):
        lo = 2 * h * HEAD_SIZE
        q = q_ref[:, h]
        keys = cache_ref[:, :, lo : lo + HEAD_SIZE]
        vals = cache_ref[:, :, lo + HEAD_SIZE : lo + 2 * HEAD_SIZE]
        new_k = new_ref[:, :, lo : lo + HEAD_SIZE].astype(f32)
        new_v = new_ref[:, :, lo + HEAD_SIZE : lo + 2 * HEAD_SIZE].astype(f32)
        s = lax.dot_general(q, keys, (((2,), (2,)), ((0,), (0,))), preferred_element_type=f32)
        s = jnp.where(valid, s * scale, -jnp.inf)
        s_new = jnp.sum(q.astype(f32) * new_k, axis=2, keepdims=True) * scale
        top = jnp.maximum(jnp.max(s, axis=2, keepdims=True), s_new)
        e = jnp.exp(s - top)
        e_new = jnp.exp(s_new - top)
        inv = 1.0 / (jnp.sum(e, axis=2, keepdims=True) + e_new)
        p = (e * inv).astype(bf16)
        p_new = (e_new * inv).astype(bf16).astype(f32)
        ctx = lax.dot_general(p, vals, (((2,), (1,)), ((0,), (0,))), preferred_element_type=f32)
        ctx = ctx + p_new * new_v
        out_ref[:, h] = ctx.astype(bf16)


def attend(query, key_value_new, cache, cache_len):
    rows, slots, width = cache.shape
    kv = width // (2 * HEAD_SIZE)
    group = QUERY_HEADS // KEY_VALUE_HEADS
    q = query.reshape(rows, kv, group, HEAD_SIZE)
    q = jnp.pad(q, ((0, 0), (0, 0), (0, 8 - group), (0, 0)))
    new = key_value_new.reshape(rows, 1, width)
    batch = 8
    out = pl.pallas_call(
        functools.partial(attend_kernel, kv, group),
        out_shape=jax.ShapeDtypeStruct((rows, kv, 8, HEAD_SIZE), bf16),
        grid_spec=pltpu.PrefetchScalarGridSpec(
            num_scalar_prefetch=1,
            grid=(rows // batch,),
            in_specs=[
                pl.BlockSpec((batch, kv, 8, HEAD_SIZE), lambda i, n: (i, 0, 0, 0)),
                pl.BlockSpec((batch, 1, width), lambda i, n: (i, 0, 0)),
                pl.BlockSpec((batch, slots, width), lambda i, n: (i, 0, 0)),
            ],
            out_specs=pl.BlockSpec((batch, kv, 8, HEAD_SIZE), lambda i, n: (i, 0, 0, 0)),
        ),
        compiler_params=pltpu.CompilerParams(vmem_limit_bytes=24 * MIB),
        name="attention",
    )(cache_len, q, new, cache)
    return out[:, :, :group].reshape(rows, kv * group * HEAD_SIZE)


def project_kernel(n_dp, n_tp, place_ref, *refs):
    ctx = refs[:n_dp]
    w_ref, res_ref = refs[n_dp], refs[n_dp + 1]
    outs = refs[n_dp + 2 : n_dp + 2 + n_tp]
    held, prod = refs[n_dp + 2 + n_tp :]
    j, t = place_ref[0], place_ref[1]
    rows = ctx[0].shape[0]
    share = outs[0].shape[0]
    for k in range(n_dp):
        held[pl.ds(pl.multiple_of((j ^ k) * rows, rows), rows), :] = ctx[k][...]
    prod[...] = jnp.dot(held[...], w_ref[...], preferred_element_type=f32)
    mine = pl.ds(pl.multiple_of(t * share, share), share)
    outs[0][...] = prod[mine, :] + res_ref[mine, :].astype(f32)
    for k in range(1, n_tp):
        outs[k][...] = prod[pl.ds(pl.multiple_of((t ^ k) * share, share), share), :].astype(bf16)


def project(place, ctx, out_proj, residual, n_tp):
    n_dp = len(ctx)
    total, width = residual.shape
    share = total // n_tp
    depth = out_proj.shape[0]
    return pl.pallas_call(
        functools.partial(project_kernel, n_dp, n_tp),
        out_shape=[jax.ShapeDtypeStruct((share, width), f32 if k == 0 else bf16) for k in range(n_tp)],
        in_specs=[pl.BlockSpec(memory_space=pltpu.SMEM)] + whole(n_dp + 2),
        out_specs=whole(n_tp),
        scratch_shapes=[VM((total, depth), bf16), VM((total, width), f32)],
        compiler_params=pltpu.CompilerParams(vmem_limit_bytes=24 * MIB),
        name="projection",
    )(place, *ctx, out_proj, residual)


def chunk_of(width):
    return 512 if width % 512 == 0 else width


def gate_up_stream(j, ks, x_refs, g_refs, wg, wu, buf_g, buf_u, sem, add, after_start):
    depth, step = buf_g.shape[0], buf_g.shape[1]
    width = x_refs[0].shape[1]
    chunks = [(i, c) for i in range(len(ks)) for c in range(width // step)]

    def copies(n):
        i, c = chunks[n]
        slot = n % depth
        rows = pl.ds(pl.multiple_of((j ^ ks[i]) * width + c * step, 128), step)
        return (
            pltpu.make_async_copy(wg.at[rows, :], buf_g.at[slot], sem.at[0, slot]),
            pltpu.make_async_copy(wu.at[rows, :], buf_u.at[slot], sem.at[1, slot]),
        )

    for n in range(min(depth, len(chunks))):
        for c in copies(n):
            c.start()
    after_start()
    for n in range(len(chunks)):
        i, c = chunks[n]
        cols = slice(c * step, (c + 1) * step)
        x = x_refs[i][:, cols].astype(f32)
        xs = (x * g_refs[i][:, cols]).astype(bf16)
        sq = x * x
        part = sum(sq[:, l : l + 128] for l in range(0, step, 128))
        one, two = copies(n)
        slot = n % depth
        one.wait()
        g = jnp.dot(xs, buf_g[slot], preferred_element_type=f32)
        two.wait()
        u = jnp.dot(xs, buf_u[slot], preferred_element_type=f32)
        add(n == 0, g, u, part)
        if n + depth < len(chunks):
            for c in copies(n + depth):
                c.start()


def first_kernel(ks, place_ref, *refs):
    n = len(ks)
    x_refs, g_refs = refs[:n], refs[n : 2 * n]
    wg, wu, acc_g, acc_u, sq, buf_g, buf_u, sem = refs[2 * n :]

    def add(fresh, g, u, part):
        acc_g[...] = g if fresh else acc_g[...] + g
        acc_u[...] = u if fresh else acc_u[...] + u
        sq[...] = part if fresh else sq[...] + part

    gate_up_stream(place_ref[0], ks, x_refs, g_refs, wg, wu, buf_g, buf_u, sem, add, lambda: None)


def first_part(place, ks, xs, gains, w_gate, w_up):
    rows, width = xs[0].shape
    hidden = w_gate.shape[1]
    step = chunk_of(width)
    return pl.pallas_call(
        functools.partial(first_kernel, ks),
        out_shape=[
            jax.ShapeDtypeStruct((rows, hidden), f32),
            jax.ShapeDtypeStruct((rows, hidden), f32),
            jax.ShapeDtypeStruct((rows, 128), f32),
        ],
        in_specs=[pl.BlockSpec(memory_space=pltpu.SMEM)] + whole(2 * len(ks)) + [pl.BlockSpec(memory_space=pl.ANY)] * 2,
        out_specs=whole(3),
        scratch_shapes=[
            VM((3, step, hidden), bf16),
            VM((3, step, hidden), bf16),
            pltpu.SemaphoreType.DMA((2, 3)),
        ],
        compiler_params=pltpu.CompilerParams(vmem_limit_bytes=28 * MIB),
        name="gate_up_first",
    )(place, *xs, *gains, w_gate, w_up)


def down_copies(j, blocks, wd, buf, sem, width):
    step = buf.shape[2]
    depth = buf.shape[0]
    chunks = [(i, c) for i in range(len(blocks)) for c in range(width // step)]

    def copy(n):
        i, c = chunks[n]
        cols = pl.ds(pl.multiple_of((j ^ blocks[i]) * width + c * step, 128), step)
        return pltpu.make_async_copy(wd.at[:, cols], buf.at[n % depth], sem.at[n % depth])

    def start():
        for n in range(min(depth, len(chunks))):
            copy(n).start()

    def run(h, put):
        for n in range(len(chunks)):
            i, c = chunks[n]
            copy(n).wait()
            put(i, slice(c * step, (c + 1) * step), jnp.dot(h, buf[n % depth], preferred_element_type=f32))
            if n + depth < len(chunks):
                copy(n + depth).start()

    return start, run


def second_kernel(ks, blocks, model, place_ref, *refs):
    n, m = len(ks), len(blocks)
    x_refs, g_refs = refs[:n], refs[n : 2 * n]
    in_g, in_u, in_sq, weight, wg, wu, wd = refs[2 * n : 2 * n + 7]
    outs = refs[2 * n + 7 : 2 * n + 7 + m]
    h_ref, acc_g, acc_u, sq, buf_g, buf_u, buf_d, sem, sem_d = refs[2 * n + 7 + m :]
    j = place_ref[0]
    start, run = down_copies(j, blocks, wd, buf_d, sem_d, outs[0].shape[1])

    def add(fresh, g, u, part):
        acc_g[...] = (in_g if fresh else acc_g)[...] + g
        acc_u[...] = (in_u if fresh else acc_u)[...] + u
        sq[...] = (in_sq if fresh else sq)[...] + part

    gate_up_stream(j, ks, x_refs, g_refs, wg, wu, buf_g, buf_u, sem, add, start)
    scale = lax.rsqrt(jnp.sum(sq[...], axis=1, keepdims=True) / model + EPS)
    g = acc_g[...] * scale
    u = acc_u[...] * (scale * weight[...])
    h_ref[...] = (g / (1.0 + jnp.exp(-g)) * u).astype(bf16)

    def put(i, cols, value):
        outs[i][:, cols] = value.astype(bf16)

    run(h_ref[...], put)


def second_part(place, ks, blocks, xs, gains, acc_g, acc_u, sq, weight, w_gate, w_up, w_down):
    rows, width = xs[0].shape
    hidden = w_gate.shape[1]
    step = chunk_of(width)
    res = pl.pallas_call(
        functools.partial(second_kernel, ks, blocks, w_down.shape[1]),
        out_shape=[jax.ShapeDtypeStruct((rows, width), bf16) for _ in blocks]
        + [jax.ShapeDtypeStruct((rows, hidden), bf16)],
        in_specs=[pl.BlockSpec(memory_space=pltpu.SMEM)]
        + whole(2 * len(ks) + 4)
        + [pl.BlockSpec(memory_space=pl.ANY)] * 3,
        out_specs=whole(len(blocks) + 1),
        scratch_shapes=[
            VM((rows, hidden), f32),
            VM((rows, hidden), f32),
            VM((rows, 128), f32),
            VM((3, step, hidden), bf16),
            VM((3, step, hidden), bf16),
            VM((3, hidden, step), bf16),
            pltpu.SemaphoreType.DMA((2, 3)),
            pltpu.SemaphoreType.DMA((3,)),
        ],
        compiler_params=pltpu.CompilerParams(vmem_limit_bytes=44 * MIB),
        name="gate_up_second",
    )(place, *xs, *gains, acc_g, acc_u, sq, weight, w_gate, w_up, w_down)
    return res[:-1], res[-1]


def down_kernel(blocks, added, place_ref, h_ref, *refs):
    n_add = sum(added)
    adds = iter(refs[:n_add])
    adds = [next(adds) if a else None for a in added]
    wd = refs[n_add]
    outs = refs[n_add + 1 : n_add + 1 + len(blocks)]
    buf, sem = refs[n_add + 1 + len(blocks) :]
    start, run = down_copies(place_ref[0], blocks, wd, buf, sem, outs[0].shape[1])
    start()

    def put(i, cols, value):
        if adds[i] is not None:
            value = value + adds[i][:, cols].astype(f32)
        outs[i][:, cols] = value.astype(outs[i].dtype)

    run(h_ref[...], put)


def down_part(place, blocks, h, adds, types, w_down, width):
    rows, hidden = h.shape
    step = chunk_of(width)
    given = [a for a in adds if a is not None]
    return pl.pallas_call(
        functools.partial(down_kernel, blocks, [a is not None for a in adds]),
        out_shape=[jax.ShapeDtypeStruct((rows, width), t) for t in types],
        in_specs=[pl.BlockSpec(memory_space=pltpu.SMEM)] + whole(1 + len(given)) + [pl.BlockSpec(memory_space=pl.ANY)],
        out_specs=whole(len(blocks)),
        scratch_shapes=[VM((4, hidden, step), bf16), pltpu.SemaphoreType.DMA((4,))],
        compiler_params=pltpu.CompilerParams(vmem_limit_bytes=28 * MIB),
        name="down",
    )(place, h, *given, w_down)


def gather_dp(x):
    n = lax.axis_size("dp")
    far = {k: swap(x, "dp", k) for k in range(2, n, 2)}
    out = [None] * n
    out[0], out[1] = x, swap(x, "dp", 1)
    for k in range(2, n, 2):
        out[k] = far[k]
        out[k + 1] = swap(far[k], "dp", 1)
    return out


def body(
    query,
    key_value_new,
    key_value_cache,
    cache_len,
    out_proj,
    residual,
    norm_gain,
    routes,
    route_weight,
    w_gate,
    w_up,
    w_down,
):
    n_dp = lax.axis_size("dp")
    n_tp = lax.axis_size("tp")
    j, t = lax.axis_index("dp"), lax.axis_index("tp")
    place = jnp.stack([j, t]).astype(jnp.int32)
    total, width = residual.shape
    share = total // n_tp

    gains = gather_dp(norm_gain[None, :])
    expert = j // (n_dp // EXPERTS)
    weight = jnp.sum(jnp.where(routes == expert, route_weight, 0.0), axis=1, keepdims=True)

    context = attend(query, key_value_new, key_value_cache, cache_len)
    parts = project(place, gather_dp(context), out_proj, residual, n_tp)
    x = parts[0]
    for k in range(1, n_tp):
        x = x + swap(parts[k], "tp", k).astype(f32)
    attended = x.astype(bf16)

    others = [attended] + [swap(attended, "tp", k) for k in range(1, n_tp)]
    stacked = jnp.zeros((n_tp, share, width), bf16)
    for k in range(n_tp):
        stacked = lax.dynamic_update_slice(stacked, others[k][None], (t ^ k, 0, 0))
    mine = stacked.reshape(total, width)

    xs = gather_dp(mine)
    near, far = (0, 1), tuple(range(2, n_dp))
    acc_g, acc_u, sq = first_part(place, near, [xs[k] for k in near], [gains[k] for k in near], w_gate, w_up)
    odd = tuple(range(3, n_dp, 2))
    even = tuple(range(2, n_dp, 2))
    out_odd, h = second_part(
        place, far, odd, [xs[k] for k in far], [gains[k] for k in far], acc_g, acc_u, sq, weight, w_gate, w_up, w_down
    )
    crossed = [swap(o, "dp", 1) for o in out_odd]
    sums = down_part(place, even, h, crossed, [bf16] * len(even), w_down, width)
    arrived = [swap(s, "dp", k) for s, k in zip(sums, even)]
    near_out = down_part(place, (1, 0), h, [None, None], [bf16, f32], w_down, width)
    mix = near_out[1] + swap(near_out[0], "dp", 1).astype(f32)
    for a in arrived:
        mix = mix + a.astype(f32)
    blocks = mix.reshape(n_tp, share, width)
    result = lax.dynamic_index_in_dim(blocks, t, 0, keepdims=False)
    for k in range(1, n_tp):
        piece = lax.dynamic_index_in_dim(blocks, t ^ k, 0, keepdims=False).astype(bf16)
        result = result + swap(piece, "tp", k).astype(f32)
    return (attended, result.astype(bf16))


def solution(mesh):
    in_specs = (
        P(("grp", "dp"), "tp"),
        P(("grp", "dp"), "tp"),
        P(("grp", "dp"), None, "tp"),
        P(("grp", "dp")),
        P("tp", "dp"),
        P("grp", "dp"),
        P("dp"),
        P("grp", None),
        P("grp", None),
        P(None, ("dp", "tp")),
        P(None, ("dp", "tp")),
        P(("dp", "tp"), None),
    )
    out_specs = (P(("grp", "tp"), "dp"), P(("grp", "tp"), "dp"))
    return jax.shard_map(body, mesh=mesh, in_specs=in_specs, out_specs=out_specs, check_vma=False)
```

time: 261 us -> 127 us (0.49)
  local copies, waits for them, and re-layouts: 67.5 us -> 17.6 us
  matrix products: 41.5 us -> 0 us
  other arithmetic: 42.2 us -> 1.63 us
  Pallas kernels: 0 us -> 36.4 us
  blocking collectives: 31.9 us -> 0 us
  starting transfers between devices: 3.61 us -> 21 us
  between operations: 14.3 us -> 0.82 us
  waiting for transfers between devices: 59.1 us -> 49.2 us
    ppermute x0 -> x21, waiting for transfers between devices: none -> 49.2 us  [swap(): return lax.ppermute(x, axis, [(i, i ^ k) for i in range(n)])]
    dot_general x6 -> x0, matrix products: 41.5 us -> none  [the longest x1 19.7 us: expert_ffn(): return jnp.dot(hidden, wd, preferred_element_type=jnp.float32)]
    pallas_call x0 -> x6, Pallas kernels: none -> 36.4 us  [the longest x1 12.8 us: second_part(): pl.pallas_call(functools.partial(second_kernel, ks, blocks, w_down.shape[...]
    unnamed x2 -> x0, other arithmetic: 34.6 us -> none
    psum x1 -> x0, waiting for transfers between devices: 24.4 us -> none  [body(): proj = lax.psum(partial_proj.astype(jnp.bfloat16), 'tp').astype(jnp.float32)]
    ppermute x0 -> x21, starting transfers between devices: none -> 21 us  [swap(): return lax.ppermute(x, axis, [(i, i ^ k) for i in range(n)])]
    reduce_scatter x1 -> x0, waiting for transfers between devices: 19 us -> none  [body(): lax.psum_scatter(combined.astype(jnp.bfloat16), 'tp', scatter_dimension=0...]
    all_to_all x1 -> x0, blocking collectives: 18.3 us -> none  [body(): lax.all_to_all(outgoing, 'dp', split_axis=0, concat_axis=2, tiled=True)[0]]
  transfers between devices with their start and end apart: 3 -> 21, of which waited for: 3 -> 12; matrix products, arithmetic and copies ran while one was open for 6% -> 1% of each run, Pallas kernels for 0% -> 14%
where the time goes in v1:
time: 127 us
  waiting for transfers between devices  49.2 us (39%)
  Pallas kernels  36.4 us (29%)
  starting transfers between devices  21 us (17%)
  local copies, waits for them, and re-layouts  17.6 us (14%)
  other arithmetic  1.63 us (1%)
    ppermute x21, waiting for transfers between devices, swap(): return lax.ppermute(x, axis, [(i, i ^ k) for i in range(n)])  49.2 us
    ppermute x21, starting transfers between devices, swap(): return lax.ppermute(x, axis, [(i, i ^ k) for i in range(n)])  21 us
    unnamed x12, local copies, waits for them, and re-layouts  14.6 us
    pallas_call x1, Pallas kernels, second_part(): pl.pallas_call(functools.partial(second_kernel, ks, blocks, w_down.shape[...  12.8 us
    pallas_call x1, Pallas kernels, first_part(): pl.pallas_call(functools.partial(first_kernel, ks), out_shape=[jax.ShapeD...  9.59 us
    pallas_call x2, Pallas kernels, down_part(): pl.pallas_call(functools.partial(down_kernel, blocks, [a is not None for...  7.85 us
    pallas_call x1, Pallas kernels, attend(): pl.pallas_call(functools.partial(attend_kernel, kv, group), out_shape=jax...  4.69 us
  transfers between devices with their start and end apart: 21, of which 12 were waited for; matrix products, arithmetic and copies ran while one was open for 1% of the time, Pallas kernels for 14%

profile of v1, /device:TPU:0, one launch (start us, length us, event | category | flops | bytes accessed | tf_op | source)
XLA Modules:
  0.0 126.6 jit_solution(12342011627199465097)
XLA Ops:
  0.6 0.8 copy.15.new_ref
  1.4 1.0 reshape.22
  2.5 0.0 copy-start.1
  2.5 2.5 %copy-done.1 = bf16[32,160,512]{2,1,0:T(8,128)(2,1)S(1)} copy-done((bf16[32,160,512]{2,1,0:T(8,128)(2,1)S(1)}, bf16[32,160,512]{2,1,0:T(8,128)(2,1)}, u32[]{:S(2)}) %copy-start.1) | copy-done | bytes 5242904
  5.0 0.7 copy-done.4
  5.7 4.7 %attention.1 = bf16[32,2,8,128]{3,2,1,0:T(8,128)(2,1)S(1)} custom-call(s32[32]{0:T(128)S(1)} %copy-done.4, bf16[32,2,8,128]{3,2,1,0:T(8,128)(2,1)S(1)} %pad.4.q_ref, bf16[32,1,512]{2,1,0:T(2,128)(2,1)S(1)} %copy.15.new_ref, bf16[32,160,512]{2,1,0:T(8,128)(2,1)S(1)} %copy-done.1), custom_call_target="tpu_custom_call" | custom-call | tf_op jit(solution)/shard_map/attention/pallas_call | solution.py:64
  10.3 0.1 reshape.24.refs_0_
  10.5 3.0 %collective-permute-start.1 = (bf16[32,1536]{1,0:T(8,128)(2,1)S(1)}, bf16[32,1536]{1,0:T(8,128)(2,1)S(1)}, u32[]{:S(2)}, u32[]{:S(2)}) collective-permute-start(bf16[32,1536]{1,0:T(8,128)(2,1)S(1)} %reshape.24.refs_0_), channel_id=1, source_target_pairs={{0,8},{4,12},{8,0},{12,4},{1,9},{5,13},{9,1},{13,5},{2,10},{6,14},... | collective-permute-start | bytes 294920 | tf_op jit(solution)/shard_map/ppermute | solution.py:22
  13.5 0.0 collective-permute-start
  13.5 2.8 %collective-permute-done.1.refs_2_ = bf16[32,1536]{1,0:T(8,128)(2,1)S(1)} collective-permute-done((bf16[32,1536]{1,0:T(8,128)(2,1)S(1)}, bf16[32,1536]{1,0:T(8,128)(2,1)S(1)}, u32[]{:S(2)}, u32[]{:S(2)}) %collective-permute-start.1) | collective-permute-done | bytes 98336 | tf_op jit(solution)/shard_map/ppermute | solution.py:22
  16.3 0.0 collective-permute-start.2
  16.3 0.1 pad_add_fusion.place_ref
  16.4 0.0 collective-permute-done.refs_1_
  16.4 1.2 collective-permute-done.2.refs_3_
  17.6 2.3 %copy-done.2 = bf16[1536,1536]{1,0:T(8,128)(2,1)S(1)} copy-done((bf16[1536,1536]{1,0:T(8,128)(2,1)S(1)}, bf16[1536,1536]{1,0:T(8,128)(2,1)}, u32[]{:S(2)}) %copy-start.2) | copy-done | bytes 4718616
  20.0 1.0 copy-done.3
  20.9 1.4 %projection.1 = (f32[32,1536]{1,0:T(8,128)S(1)}, bf16[32,1536]{1,0:T(8,128)(2,1)S(1)}, bf16[32,1536]{1,0:T(8,128)(2,1)S(1)}, bf16[32,1536]{1,0:T(8,128)(2,1)S(1)}) custom-call(s32[2]{0:T(128)S(1)} %pad_add_fusion.place_ref, bf16[32,1536]{1,0:T(8,128)(2,1)S(1)} %reshape.24.refs_0_, bf16[32,1536]{1,0:T(8,128)(2,1)S(1)} %collective-permute-done.refs_1_, ...), custom_call_target="tpu_custom_call" | custom-call | tf_op jit(solution)/shard_map/projection/pallas_call | solution.py:105
  22.3 1.9 %collective-permute-start.3 = (bf16[32,1536]{1,0:T(8,128)(2,1)S(1)}, bf16[32,1536]{1,0:T(8,128)(2,1)S(1)}, u32[]{:S(2)}, u32[]{:S(2)}) collective-permute-start(bf16[32,1536]{1,0:T(8,128)(2,1)S(1)} %get-tuple-element.14), channel_id=1, source_target_pairs={{0,1},{1,0},{2,3},{3,2},{4,5},{5,4},{6,7},{7,6},{8,9},{9,8},{10,11... | collective-permute-start | bytes 294920 | tf_op jit(solution)/shard_map/ppermute | solution.py:22
  24.3 2.6 %collective-permute-start.4 = (bf16[32,1536]{1,0:T(8,128)(2,1)S(1)}, bf16[32,1536]{1,0:T(8,128)(2,1)S(1)}, u32[]{:S(2)}, u32[]{:S(2)}) collective-permute-start(bf16[32,1536]{1,0:T(8,128)(2,1)S(1)} %get-tuple-element.15), channel_id=1, source_target_pairs={{0,2},{1,3},{2,0},{3,1},{4,6},{5,7},{6,4},{7,5},{8,10},{9,11},{10,... | collective-permute-start | bytes 294920 | tf_op jit(solution)/shard_map/ppermute | solution.py:22
  26.9 0.0 collective-permute-start.5
  26.9 0.5 collective-permute-done.3
  27.4 7.5 %collective-permute-done.4 = bf16[32,1536]{1,0:T(8,128)(2,1)S(1)} collective-permute-done((bf16[32,1536]{1,0:T(8,128)(2,1)S(1)}, bf16[32,1536]{1,0:T(8,128)(2,1)S(1)}, u32[]{:S(2)}, u32[]{:S(2)}) %collective-permute-start.4) | collective-permute-done | bytes 98336 | tf_op jit(solution)/shard_map/ppermute | solution.py:22
  34.9 0.0 collective-permute-done.5
  35.0 0.1 bitcast_dynamic-update-slice_fusion.3
  35.0 0.0 copy-start.5
  35.1 1.8 %collective-permute-start.6 = (bf16[32,1536]{1,0:T(8,128)(2,1)S(1)}, bf16[32,1536]{1,0:T(8,128)(2,1)S(1)}, u32[]{:S(2)}, u32[]{:S(2)}) collective-permute-start(bf16[32,1536]{1,0:T(8,128)(2,1)S(1)} %get-tuple-element.25), channel_id=1, source_target_pairs={{0,1},{1,0},{2,3},{3,2},{4,5},{5,4},{6,7},{7,6},{8,9},{9,8},{10,11... | collective-permute-start | bytes 294920 | tf_op jit(solution)/shard_map/ppermute | solution.py:22
  36.9 2.5 %collective-permute-start.8 = (bf16[32,1536]{1,0:T(8,128)(2,1)S(1)}, bf16[32,1536]{1,0:T(8,128)(2,1)S(1)}, u32[]{:S(2)}, u32[]{:S(2)}) collective-permute-start(bf16[32,1536]{1,0:T(8,128)(2,1)S(1)} %get-tuple-element.25), channel_id=1, source_target_pairs={{0,3},{1,2},{2,1},{3,0},{4,7},{5,6},{6,5},{7,4},{8,11},{9,10},{10,... | collective-permute-start | bytes 294920 | tf_op jit(solution)/shard_map/ppermute | solution.py:22
  39.3 0.0 collective-permute-start.7
  39.3 0.7 collective-permute-done.6
  40.0 7.5 %collective-permute-done.7 = bf16[32,1536]{1,0:T(8,128)(2,1)S(1)} collective-permute-done((bf16[32,1536]{1,0:T(8,128)(2,1)S(1)}, bf16[32,1536]{1,0:T(8,128)(2,1)S(1)}, u32[]{:S(2)}, u32[]{:S(2)}) %collective-permute-start.7) | collective-permute-done | bytes 98336 | tf_op jit(solution)/shard_map/ppermute | solution.py:22
  47.5 0.0 collective-permute-done.8
  47.6 1.6 %collective-permute-start.9 = (bf16[128,1536]{1,0:T(8,128)(2,1)S(1)}, bf16[128,1536]{1,0:T(8,128)(2,1)S(1)}, u32[]{:S(2)}, u32[]{:S(2)}) collective-permute-start(bf16[128,1536]{1,0:T(8,128)(2,1)S(1)} %bitcast.29), channel_id=1, source_target_pairs={{0,8},{4,12},{8,0},{12,4},{1,9},{5,13},{9,1},{13,5},{2,10},{6,14},... | collective-permute-start | bytes 1179656 | tf_op jit(solution)/shard_map/ppermute | solution.py:22
  49.1 0.0 collective-permute-start.13
  49.1 8.7 %collective-permute-done.9.refs_0_ = bf16[128,1536]{1,0:T(8,128)(2,1)S(1)} collective-permute-done((bf16[128,1536]{1,0:T(8,128)(2,1)S(1)}, bf16[128,1536]{1,0:T(8,128)(2,1)S(1)}, u32[]{:S(2)}, u32[]{:S(2)}) %collective-permute-start.9) | collective-permute-done | bytes 393248 | tf_op jit(solution)/shard_map/ppermute | solution.py:22
  57.8 0.0 collective-permute-start.10
  57.8 0.7 broadcast_in_dim.30.refs_2_
  58.5 1.5 %collective-permute-start.11 = (f32[1,1536]{1,0:T(1,128)S(1)}, f32[1,1536]{1,0:T(1,128)S(1)}, u32[]{:S(2)}, u32[]{:S(2)}) collective-permute-start(f32[1,1536]{1,0:T(1,128)S(1)} %broadcast_in_dim.30.refs_2_), channel_id=1, source_target_pairs={{0,8},{4,12},{8,0},{12,4},{1,9},{5,13},{9,1},{13,5},{2,10},{6,14},... | collective-permute-start | bytes 18440 | tf_op jit(solution)/shard_map/ppermute | solution.py:22
  60.0 0.2 collective-permute-start.14
  60.3 1.9 %collective-permute-done.11.refs_2_ = f32[1,1536]{1,0:T(1,128)S(1)} collective-permute-done((f32[1,1536]{1,0:T(1,128)S(1)}, f32[1,1536]{1,0:T(1,128)S(1)}, u32[]{:S(2)}, u32[]{:S(2)}) %collective-permute-start.11) | collective-permute-done | bytes 6176 | tf_op jit(solution)/shard_map/ppermute | solution.py:22
  62.1 0.0 collective-permute-start.12
  62.1 0.7 fusion.6
  62.9 0.1 copy.16.refs_7_
  63.0 0.0 collective-permute-done.14.refs_3_
  63.0 0.0 collective-permute-done.13.refs_1_
  63.0 9.6 %gate_up_first.1 = (f32[128,2048]{1,0:T(8,128)S(1)}, f32[128,2048]{1,0:T(8,128)S(1)}, f32[128,128]{1,0:T(8,128)S(1)}) custom-call(s32[2]{0:T(128)S(1)} %pad_add_fusion.place_ref, bf16[128,1536]{1,0:T(8,128)(2,1)S(1)} %bitcast.31, bf16[128,1536]{1,0:T(8,128)(2,1)S(1)} %collective-permute-done.13.refs_1_, f32[1,1536]{1,0:T(1,128)S(1)} %broadcast_in_dim.30.refs_2_, ...), custom_call_target="tpu_custom_call" | custom-call | tf_op jit(solution)/shard_map/gate_up_first/pallas_call | solution.py:174
  72.6 0.0 collective-permute-done.12.refs_3_
  72.6 12.8 %gate_up_second.1 = (bf16[128,1536]{1,0:T(8,128)(2,1)S(1)}, bf16[128,2048]{1,0:T(8,128)(2,1)S(1)}) custom-call(s32[2]{0:T(128)S(1)} %pad_add_fusion.place_ref, bf16[128,1536]{1,0:T(8,128)(2,1)S(1)} %collective-permute-done.9.refs_0_, bf16[128,1536]{1,0:T(8,128)(2,1)S(1)} %collective-permute-done.10.refs_1_, f32[1,1536]{1,0:T(1,128)S(1)} %collective-permute-done.11.refs_2_, ...), custom_call_target="tpu_custom_call" | custom-call | tf_op jit(solution)/shard_map/gate_up_second/pallas_call | solution.py:248
  85.5 0.6 collective-permute-start.16
  86.0 8.2 %copy-done = bf16[2048,6144]{1,0:T(8,128)(2,1)S(1)} copy-done((bf16[2048,6144]{1,0:T(8,128)(2,1)S(1)}, bf16[2048,6144]{1,0:T(8,128)(2,1)}, u32[]{:S(2)}) %copy-start) | copy-done | bytes 25165848
  94.2 5.1 %down.2 = (bf16[128,1536]{1,0:T(8,128)(2,1)S(1)}, f32[128,1536]{1,0:T(8,128)S(1)}) custom-call(s32[2]{0:T(128)S(1)} %pad_add_fusion.place_ref, bf16[128,2048]{1,0:T(8,128)(2,1)S(1)} %get-tuple-element.20.h_ref, bf16[2048,6144]{1,0:T(8,128)(2,1)S(1)} %copy-done), custom_call_target="tpu_custom_call" | custom-call | tf_op jit(solution)/shard_map/down/pallas_call | solution.py:294
  99.3 0.1 collective-permute-start.15
  99.4 0.0 collective-permute-done.16.refs_0_
  99.4 2.8 %down.3 = bf16[128,1536]{1,0:T(8,128)(2,1)S(1)} custom-call(s32[2]{0:T(128)S(1)} %pad_add_fusion.place_ref, bf16[128,2048]{1,0:T(8,128)(2,1)S(1)} %get-tuple-element.20.h_ref, bf16[128,1536]{1,0:T(8,128)(2,1)S(1)} %collective-permute-done.16.refs_0_, bf16[2048,6144]{1,0:T(8,128)(2,1)S(1)} %copy-done), custom_call_target="tpu_custom_call" | custom-call | tf_op jit(solution)/shard_map/down/pallas_call | solution.py:294
  102.2 1.6 %collective-permute-start.17 = (bf16[128,1536]{1,0:T(8,128)(2,1)S(1)}, bf16[128,1536]{1,0:T(8,128)(2,1)S(1)}, u32[]{:S(2)}, u32[]{:S(2)}) collective-permute-start(bf16[128,1536]{1,0:T(8,128)(2,1)S(1)} %down.3), channel_id=1, source_target_pairs={{0,8},{4,12},{8,0},{12,4},{1,9},{5,13},{9,1},{13,5},{2,10},{6,14},... | collective-permute-start | bytes 1179656 | tf_op jit(solution)/shard_map/ppermute | solution.py:22
  103.8 0.0 collective-permute-done.15
  103.8 9.9 %collective-permute-done.17 = bf16[128,1536]{1,0:T(8,128)(2,1)S(1)} collective-permute-done((bf16[128,1536]{1,0:T(8,128)(2,1)S(1)}, bf16[128,1536]{1,0:T(8,128)(2,1)S(1)}, u32[]{:S(2)}, u32[]{:S(2)}) %collective-permute-start.17) | collective-permute-done | bytes 393248 | tf_op jit(solution)/shard_map/ppermute | solution.py:22
  113.7 0.1 convert_add_fusion
  113.9 0.1 collective-permute-start.18
  114.0 2.3 %collective-permute-start.20 = (bf16[32,1536]{1,0:T(8,128)(2,1)S(1)}, bf16[32,1536]{1,0:T(8,128)(2,1)S(1)}, u32[]{:S(2)}, u32[]{:S(2)}) collective-permute-start(bf16[32,1536]{1,0:T(8,128)(2,1)S(1)} %get-tuple-element.27), channel_id=1, source_target_pairs={{0,3},{1,2},{2,1},{3,0},{4,7},{5,6},{6,5},{7,4},{8,11},{9,10},{10,... | collective-permute-start | bytes 294920 | tf_op jit(solution)/shard_map/ppermute | solution.py:22
  116.3 1.2 collective-permute-start.19
  117.5 1.6 %collective-permute-done.18 = bf16[32,1536]{1,0:T(8,128)(2,1)S(1)} collective-permute-done((bf16[32,1536]{1,0:T(8,128)(2,1)S(1)}, bf16[32,1536]{1,0:T(8,128)(2,1)S(1)}, u32[]{:S(2)}, u32[]{:S(2)}) %collective-permute-start.18) | collective-permute-done | bytes 98336 | tf_op jit(solution)/shard_map/ppermute | solution.py:22
  119.0 2.8 %collective-permute-done.20 = bf16[32,1536]{1,0:T(8,128)(2,1)S(1)} collective-permute-done((bf16[32,1536]{1,0:T(8,128)(2,1)S(1)}, bf16[32,1536]{1,0:T(8,128)(2,1)S(1)}, u32[]{:S(2)}, u32[]{:S(2)}) %collective-permute-start.20) | collective-permute-done | bytes 98336 | tf_op jit(solution)/shard_map/ppermute | solution.py:22
  121.8 4.1 %collective-permute-done.19 = bf16[32,1536]{1,0:T(8,128)(2,1)S(1)} collective-permute-done((bf16[32,1536]{1,0:T(8,128)(2,1)S(1)}, bf16[32,1536]{1,0:T(8,128)(2,1)S(1)}, u32[]{:S(2)}, u32[]{:S(2)}) %collective-permute-start.19) | collective-permute-done | bytes 98336 | tf_op jit(solution)/shard_map/ppermute | solution.py:22
  125.9 0.7 fusion.2
  (12 shorter events, 0.1 us)
Async XLA Ops:
  2.5 2.5 %copy-start.1 = (bf16[32,160,512]{2,1,0:T(8,128)(2,1)S(1)}, bf16[32,160,512]{2,1,0:T(8,128)(2,1)}, u32[]{:S(2)}) copy-start(bf16[32,160,512]{2,1,0:T(8,128)(2,1)} %cache_ref.1) | copy-start | bytes 15728644
  5.0 0.7 copy-start.4
  10.5 5.8 %collective-permute-start.1 = (bf16[32,1536]{1,0:T(8,128)(2,1)S(1)}, bf16[32,1536]{1,0:T(8,128)(2,1)S(1)}, u32[]{:S(2)}, u32[]{:S(2)}) collective-permute-start(bf16[32,1536]{1,0:T(8,128)(2,1)S(1)} %reshape.24.refs_0_), channel_id=1, source_target_pairs={{0,8},{4,12},{8,0},{12,4},{1,9},{5,13},{9,1},{13,5},{2,10},{6,14},... | collective-permute-start | bytes 294920 | tf_op jit(solution)/shard_map/ppermute | solution.py:22
  13.5 2.9 %collective-permute-start = (bf16[32,1536]{1,0:T(8,128)(2,1)S(1)}, bf16[32,1536]{1,0:T(8,128)(2,1)S(1)}, u32[]{:S(2)}, u32[]{:S(2)}) collective-permute-start(bf16[32,1536]{1,0:T(8,128)(2,1)S(1)} %reshape.24.refs_0_), channel_id=1, source_target_pairs={{0,4},{4,0},{8,12},{12,8},{1,5},{5,1},{9,13},{13,9},{2,6},{6,2},{1... | collective-permute-start | bytes 294920 | tf_op jit(solution)/shard_map/ppermute | solution.py:22
  16.3 1.3 %collective-permute-start.2 = (bf16[32,1536]{1,0:T(8,128)(2,1)S(1)}, bf16[32,1536]{1,0:T(8,128)(2,1)S(1)}, u32[]{:S(2)}, u32[]{:S(2)}) collective-permute-start(bf16[32,1536]{1,0:T(8,128)(2,1)S(1)} %collective-permute-done.1.refs_2_), channel_id=1, source_target_pairs={{0,4},{4,0},{8,12},{12,8},{1,5},{5,1},{9,13},{13,9},{2,6},{6,2},{1... | collective-permute-start | bytes 294920 | tf_op jit(solution)/shard_map/ppermute | solution.py:22
  17.6 2.3 %copy-start.2 = (bf16[1536,1536]{1,0:T(8,128)(2,1)S(1)}, bf16[1536,1536]{1,0:T(8,128)(2,1)}, u32[]{:S(2)}) copy-start(bf16[1536,1536]{1,0:T(8,128)(2,1)} %refs_4_.2) | copy-start | bytes 14155780
  20.0 1.0 copy-start.3
  22.3 5.1 %collective-permute-start.3 = (bf16[32,1536]{1,0:T(8,128)(2,1)S(1)}, bf16[32,1536]{1,0:T(8,128)(2,1)S(1)}, u32[]{:S(2)}, u32[]{:S(2)}) collective-permute-start(bf16[32,1536]{1,0:T(8,128)(2,1)S(1)} %get-tuple-element.14), channel_id=1, source_target_pairs={{0,1},{1,0},{2,3},{3,2},{4,5},{5,4},{6,7},{7,6},{8,9},{9,8},{10,11... | collective-permute-start | bytes 294920 | tf_op jit(solution)/shard_map/ppermute | solution.py:22
  24.3 10.7 %collective-permute-start.4 = (bf16[32,1536]{1,0:T(8,128)(2,1)S(1)}, bf16[32,1536]{1,0:T(8,128)(2,1)S(1)}, u32[]{:S(2)}, u32[]{:S(2)}) collective-permute-start(bf16[32,1536]{1,0:T(8,128)(2,1)S(1)} %get-tuple-element.15), channel_id=1, source_target_pairs={{0,2},{1,3},{2,0},{3,1},{4,6},{5,7},{6,4},{7,5},{8,10},{9,11},{10,... | collective-permute-start | bytes 294920 | tf_op jit(solution)/shard_map/ppermute | solution.py:22
  26.9 8.1 %collective-permute-start.5 = (bf16[32,1536]{1,0:T(8,128)(2,1)S(1)}, bf16[32,1536]{1,0:T(8,128)(2,1)S(1)}, u32[]{:S(2)}, u32[]{:S(2)}) collective-permute-start(bf16[32,1536]{1,0:T(8,128)(2,1)S(1)} %get-tuple-element.16), channel_id=1, source_target_pairs={{0,3},{1,2},{2,1},{3,0},{4,7},{5,6},{6,5},{7,4},{8,11},{9,10},{10,... | collective-permute-start | bytes 294920 | tf_op jit(solution)/shard_map/ppermute | solution.py:22
  35.0 37.5 %copy-start.5 = (bf16[32,1536]{1,0:T(8,128)(2,1)}, bf16[32,1536]{1,0:T(8,128)(2,1)S(1)}, u32[]{:S(2)}) copy-start(bf16[32,1536]{1,0:T(8,128)(2,1)S(1)} %get-tuple-element.25) | copy-start | bytes 294916
  35.1 5.0 %collective-permute-start.6 = (bf16[32,1536]{1,0:T(8,128)(2,1)S(1)}, bf16[32,1536]{1,0:T(8,128)(2,1)S(1)}, u32[]{:S(2)}, u32[]{:S(2)}) collective-permute-start(bf16[32,1536]{1,0:T(8,128)(2,1)S(1)} %get-tuple-element.25), channel_id=1, source_target_pairs={{0,1},{1,0},{2,3},{3,2},{4,5},{5,4},{6,7},{7,6},{8,9},{9,8},{10,11... | collective-permute-start | bytes 294920 | tf_op jit(solution)/shard_map/ppermute | solution.py:22
  36.9 10.7 %collective-permute-start.8 = (bf16[32,1536]{1,0:T(8,128)(2,1)S(1)}, bf16[32,1536]{1,0:T(8,128)(2,1)S(1)}, u32[]{:S(2)}, u32[]{:S(2)}) collective-permute-start(bf16[32,1536]{1,0:T(8,128)(2,1)S(1)} %get-tuple-element.25), channel_id=1, source_target_pairs={{0,3},{1,2},{2,1},{3,0},{4,7},{5,6},{6,5},{7,4},{8,11},{9,10},{10,... | collective-permute-start | bytes 294920 | tf_op jit(solution)/shard_map/ppermute | solution.py:22
  39.3 8.2 %collective-permute-start.7 = (bf16[32,1536]{1,0:T(8,128)(2,1)S(1)}, bf16[32,1536]{1,0:T(8,128)(2,1)S(1)}, u32[]{:S(2)}, u32[]{:S(2)}) collective-permute-start(bf16[32,1536]{1,0:T(8,128)(2,1)S(1)} %get-tuple-element.25), channel_id=1, source_target_pairs={{0,2},{1,3},{2,0},{3,1},{4,6},{5,7},{6,4},{7,5},{8,10},{9,11},{10,... | collective-permute-start | bytes 294920 | tf_op jit(solution)/shard_map/ppermute | solution.py:22
  47.6 10.2 %collective-permute-start.9 = (bf16[128,1536]{1,0:T(8,128)(2,1)S(1)}, bf16[128,1536]{1,0:T(8,128)(2,1)S(1)}, u32[]{:S(2)}, u32[]{:S(2)}) collective-permute-start(bf16[128,1536]{1,0:T(8,128)(2,1)S(1)} %bitcast.29), channel_id=1, source_target_pairs={{0,8},{4,12},{8,0},{12,4},{1,9},{5,13},{9,1},{13,5},{2,10},{6,14},... | collective-permute-start | bytes 1179656 | tf_op jit(solution)/shard_map/ppermute | solution.py:22
  49.1 13.8 %collective-permute-start.13 = (bf16[128,1536]{1,0:T(8,128)(2,1)S(1)}, bf16[128,1536]{1,0:T(8,128)(2,1)S(1)}, u32[]{:S(2)}, u32[]{:S(2)}) collective-permute-start(bf16[128,1536]{1,0:T(8,128)(2,1)S(1)} %bitcast.30), channel_id=1, source_target_pairs={{0,4},{4,0},{8,12},{12,8},{1,5},{5,1},{9,13},{13,9},{2,6},{6,2},{1... | collective-permute-start | bytes 1179656 | tf_op jit(solution)/shard_map/ppermute | solution.py:22
  57.8 14.8 %collective-permute-start.10 = (bf16[128,1536]{1,0:T(8,128)(2,1)S(1)}, bf16[128,1536]{1,0:T(8,128)(2,1)S(1)}, u32[]{:S(2)}, u32[]{:S(2)}) collective-permute-start(bf16[128,1536]{1,0:T(8,128)(2,1)S(1)} %collective-permute-done.9.refs_0_), channel_id=1, source_target_pairs={{0,4},{4,0},{8,12},{12,8},{1,5},{5,1},{9,13},{13,9},{2,6},{6,2},{1... | collective-permute-start | bytes 1179656 | tf_op jit(solution)/shard_map/ppermute | solution.py:22
  58.5 3.6 %collective-permute-start.11 = (f32[1,1536]{1,0:T(1,128)S(1)}, f32[1,1536]{1,0:T(1,128)S(1)}, u32[]{:S(2)}, u32[]{:S(2)}) collective-permute-start(f32[1,1536]{1,0:T(1,128)S(1)} %broadcast_in_dim.30.refs_2_), channel_id=1, source_target_pairs={{0,8},{4,12},{8,0},{12,4},{1,9},{5,13},{9,1},{13,5},{2,10},{6,14},... | collective-permute-start | bytes 18440 | tf_op jit(solution)/shard_map/ppermute | solution.py:22
  60.0 2.9 %collective-permute-start.14 = (f32[1,1536]{1,0:T(1,128)S(1)}, f32[1,1536]{1,0:T(1,128)S(1)}, u32[]{:S(2)}, u32[]{:S(2)}) collective-permute-start(f32[1,1536]{1,0:T(1,128)S(1)} %broadcast_in_dim.30.refs_2_), channel_id=1, source_target_pairs={{0,4},{4,0},{8,12},{12,8},{1,5},{5,1},{9,13},{13,9},{2,6},{6,2},{1... | collective-permute-start | bytes 18440 | tf_op jit(solution)/shard_map/ppermute | solution.py:22
  62.1 10.5 %collective-permute-start.12 = (f32[1,1536]{1,0:T(1,128)S(1)}, f32[1,1536]{1,0:T(1,128)S(1)}, u32[]{:S(2)}, u32[]{:S(2)}) collective-permute-start(f32[1,1536]{1,0:T(1,128)S(1)} %collective-permute-done.11.refs_2_), channel_id=1, source_target_pairs={{0,4},{4,0},{8,12},{12,8},{1,5},{5,1},{9,13},{13,9},{2,6},{6,2},{1... | collective-permute-start | bytes 18440 | tf_op jit(solution)/shard_map/ppermute | solution.py:22
  85.5 13.9 %collective-permute-start.16 = (bf16[128,1536]{1,0:T(8,128)(2,1)S(1)}, bf16[128,1536]{1,0:T(8,128)(2,1)S(1)}, u32[]{:S(2)}, u32[]{:S(2)}) collective-permute-start(bf16[128,1536]{1,0:T(8,128)(2,1)S(1)} %get-tuple-element.23), channel_id=1, source_target_pairs={{0,4},{4,0},{8,12},{12,8},{1,5},{5,1},{9,13},{13,9},{2,6},{6,2},{1... | collective-permute-start | bytes 1179656 | tf_op jit(solution)/shard_map/ppermute | solution.py:22
  86.0 8.2 %copy-start = (bf16[2048,6144]{1,0:T(8,128)(2,1)S(1)}, bf16[2048,6144]{1,0:T(8,128)(2,1)}, u32[]{:S(2)}) copy-start(bf16[2048,6144]{1,0:T(8,128)(2,1)} %refs_1_.1) | copy-start | bytes 75497472
  99.3 4.5 %collective-permute-start.15 = (bf16[128,1536]{1,0:T(8,128)(2,1)S(1)}, bf16[128,1536]{1,0:T(8,128)(2,1)S(1)}, u32[]{:S(2)}, u32[]{:S(2)}) collective-permute-start(bf16[128,1536]{1,0:T(8,128)(2,1)S(1)} %get-tuple-element.22), channel_id=1, source_target_pairs={{0,4},{4,0},{8,12},{12,8},{1,5},{5,1},{9,13},{13,9},{2,6},{6,2},{1... | collective-permute-start | bytes 1179656 | tf_op jit(solution)/shard_map/ppermute | solution.py:22
  102.2 11.6 %collective-permute-start.17 = (bf16[128,1536]{1,0:T(8,128)(2,1)S(1)}, bf16[128,1536]{1,0:T(8,128)(2,1)S(1)}, u32[]{:S(2)}, u32[]{:S(2)}) collective-permute-start(bf16[128,1536]{1,0:T(8,128)(2,1)S(1)} %down.3), channel_id=1, source_target_pairs={{0,8},{4,12},{8,0},{12,4},{1,9},{5,13},{9,1},{13,5},{2,10},{6,14},... | collective-permute-start | bytes 1179656 | tf_op jit(solution)/shard_map/ppermute | solution.py:22
  113.9 5.1 %collective-permute-start.18 = (bf16[32,1536]{1,0:T(8,128)(2,1)S(1)}, bf16[32,1536]{1,0:T(8,128)(2,1)S(1)}, u32[]{:S(2)}, u32[]{:S(2)}) collective-permute-start(bf16[32,1536]{1,0:T(8,128)(2,1)S(1)} %get-tuple-element.26), channel_id=1, source_target_pairs={{0,1},{1,0},{2,3},{3,2},{4,5},{5,4},{6,7},{7,6},{8,9},{9,8},{10,11... | collective-permute-start | bytes 294920 | tf_op jit(solution)/shard_map/ppermute | solution.py:22
  114.0 7.8 %collective-permute-start.20 = (bf16[32,1536]{1,0:T(8,128)(2,1)S(1)}, bf16[32,1536]{1,0:T(8,128)(2,1)S(1)}, u32[]{:S(2)}, u32[]{:S(2)}) collective-permute-start(bf16[32,1536]{1,0:T(8,128)(2,1)S(1)} %get-tuple-element.27), channel_id=1, source_target_pairs={{0,3},{1,2},{2,1},{3,0},{4,7},{5,6},{6,5},{7,4},{8,11},{9,10},{10,... | collective-permute-start | bytes 294920 | tf_op jit(solution)/shard_map/ppermute | solution.py:22
  116.3 9.7 %collective-permute-start.19 = (bf16[32,1536]{1,0:T(8,128)(2,1)S(1)}, bf16[32,1536]{1,0:T(8,128)(2,1)S(1)}, u32[]{:S(2)}, u32[]{:S(2)}) collective-permute-start(bf16[32,1536]{1,0:T(8,128)(2,1)S(1)} %get-tuple-element.28), channel_id=1, source_target_pairs={{0,2},{1,3},{2,0},{3,1},{4,6},{5,7},{6,4},{7,5},{8,10},{9,11},{10,... | collective-permute-start | bytes 294920 | tf_op jit(solution)/shard_map/ppermute | solution.py:22

commit v2 on v0

v2 whole, which is shorter than its diff:
```python
import functools

import jax
import jax.numpy as jnp
from jax import lax
from jax.experimental import pallas as pl
from jax.experimental.pallas import tpu as pltpu
from jax.sharding import PartitionSpec as P

QUERY_HEADS = 48
KEY_VALUE_HEADS = 8
HEAD_SIZE = 128
EXPERTS = 4
EPS = 1e-05
TAIL = 128
MIB = 1 << 20
VM = pltpu.VMEM
f32, bf16 = jnp.float32, jnp.bfloat16
SMEM_SPEC = pl.BlockSpec(memory_space=pltpu.SMEM)
HBM_SPEC = pl.BlockSpec(memory_space=pltpu.HBM)
VMEM_SPEC = pl.BlockSpec(memory_space=VM)


def swap(x, axis, k):
    n = lax.axis_size(axis)
    return lax.ppermute(x, axis, [(i, i ^ k) for i in range(n)])


def hbm(x):
    return pltpu.with_memory_space_constraint(x, pltpu.HBM)


def cost(nbytes, flops=0):
    return pl.CostEstimate(flops=int(flops), bytes_accessed=int(nbytes), transcendentals=0)


def row_loads(place_ref, mats, ks, outs, sem):
    loads = []
    for i, k in enumerate(ks):
        width = outs[i].shape[0]
        rows = pl.ds(pl.multiple_of((place_ref[0] ^ k) * width, 128), width)
        loads.append(pltpu.make_async_copy(mats[i].at[rows, :], outs[i], sem.at[i]))
    return loads


def col_loads(place_ref, mat, ks, outs, sem):
    loads = []
    for i, k in enumerate(ks):
        width = outs[i].shape[1]
        cols = pl.ds(pl.multiple_of((place_ref[0] ^ k) * width, 128), width)
        loads.append(pltpu.make_async_copy(mat.at[:, cols], outs[i], sem.at[i]))
    return loads


def all_of(loads, act):
    for c in loads:
        getattr(c, act)()


def attend_kernel(kv, group, batch, _, len_hbm, q_hbm, new_hbm, cache_hbm, w_hbm, *refs):
    out_ref, w_ref, len_ref, q_ref, new_ref, cache, q_scr, sem, w_sem, small_sem = refs
    rows, slots = cache.shape[0], cache.shape[1]
    small = [
        pltpu.make_async_copy(a, b, small_sem.at[i])
        for i, (a, b) in enumerate(((q_hbm, q_ref), (new_hbm, new_ref), (len_hbm, len_ref)))
    ]
    all_of(small, "start")
    parts = [pl.ds(i * batch, batch) for i in range(rows // batch)]
    loads = [pltpu.make_async_copy(cache_hbm.at[p], cache.at[p], sem.at[i]) for i, p in enumerate(parts)]
    all_of(loads, "start")
    after = pltpu.make_async_copy(w_hbm, w_ref, w_sem)
    after.start()
    all_of(small, "wait")
    scale = 1.0 / HEAD_SIZE**0.5
    q_scr[...] = jnp.zeros_like(q_scr)
    for h in range(kv):
        for g in range(group):
            lo = (h * group + g) * HEAD_SIZE
            q_scr[h, :, g, :] = q_ref[:, lo : lo + HEAD_SIZE].astype(f32)
    pos = lax.broadcasted_iota(jnp.int32, (1, 8, slots), 2)
    new = new_ref[...].astype(f32)
    for i, p in enumerate(parts):
        base = i * batch
        valid = jnp.concatenate([pos < len_ref[base + b] for b in range(batch)], axis=0)
        loads[i].wait()
        for h in range(kv):
            lo = 2 * h * HEAD_SIZE

            def spread(col):
                return jnp.concatenate(
                    [
                        jnp.broadcast_to(new[base + b : base + b + 1, col : col + HEAD_SIZE][None], (1, 8, HEAD_SIZE))
                        for b in range(batch)
                    ],
                    axis=0,
                )

            q = q_scr[h, p]
            keys = cache[p, :, lo : lo + HEAD_SIZE]
            vals = cache[p, :, lo + HEAD_SIZE : lo + 2 * HEAD_SIZE]
            s = lax.dot_general(
                q.astype(bf16), keys, (((2,), (2,)), ((0,), (0,))), preferred_element_type=f32
            )
            s = jnp.where(valid, s * scale, -jnp.inf)
            s_new = jnp.sum(q * spread(lo), axis=2, keepdims=True) * scale
            top = jnp.maximum(jnp.max(s, axis=2, keepdims=True), s_new)
            e = jnp.exp(s - top)
            e_new = jnp.exp(s_new - top)
            inv = 1.0 / (jnp.sum(e, axis=2, keepdims=True) + e_new)
            probs = (e * inv).astype(bf16)
            p_new = (e_new * inv).astype(bf16).astype(f32)
            ctx = lax.dot_general(probs, vals, (((2,), (1,)), ((0,), (0,))), preferred_element_type=f32)
            q_scr[h, p] = ctx + p_new * spread(lo + HEAD_SIZE)
    for h in range(kv):
        for g in range(group):
            lo = (h * group + g) * HEAD_SIZE
            out_ref[:, lo : lo + HEAD_SIZE] = q_scr[h, :, g, :].astype(bf16)
    after.wait()


def attend(place, query, key_value_new, cache, cache_len, out_proj):
    rows, slots, width = cache.shape
    kv = width // (2 * HEAD_SIZE)
    group = QUERY_HEADS // KEY_VALUE_HEADS
    batch = 8
    return pl.pallas_call(
        functools.partial(attend_kernel, kv, group, batch),
        out_shape=[jax.ShapeDtypeStruct(query.shape, bf16), VM(out_proj.shape, bf16)],
        in_specs=[SMEM_SPEC] + [HBM_SPEC] * 5,
        out_specs=[VMEM_SPEC] * 2,
        scratch_shapes=[
            pltpu.SMEM(cache_len.shape, jnp.int32),
            VM(query.shape, bf16),
            VM(key_value_new.shape, bf16),
            VM(cache.shape, bf16),
            VM((kv, rows, 8, HEAD_SIZE), f32),
            pltpu.SemaphoreType.DMA((rows // batch,)),
            pltpu.SemaphoreType.DMA,
            pltpu.SemaphoreType.DMA((3,)),
        ],
        compiler_params=pltpu.CompilerParams(vmem_limit_bytes=10 * MIB),
        cost_estimate=cost(4 * cache.size, 24 * cache.size),
        name="attention",
    )(place, *[hbm(a) for a in (cache_len, query, key_value_new, cache, out_proj)])


def fetch_kernel(ks, place_ref, token_ref, *refs):
    n = len(ks)
    mats, outs, token_out, sem = refs[:n], refs[n : 2 * n], refs[2 * n], refs[2 * n + 1]
    loads = row_loads(place_ref, mats, ks, outs, sem)
    all_of(loads, "start")
    token_out[...] = token_ref[:8, :128]
    all_of(loads, "wait")


def fetch(place, token, wanted, width):
    ks = [k for _, k in wanted]
    n = len(wanted)
    res = pl.pallas_call(
        functools.partial(fetch_kernel, ks),
        out_shape=[VM((width, m.shape[1]), bf16) for m, _ in wanted] + [jax.ShapeDtypeStruct((8, 128), token.dtype)],
        in_specs=[SMEM_SPEC, VMEM_SPEC] + [HBM_SPEC] * n,
        out_specs=[VMEM_SPEC] * (n + 1),
        scratch_shapes=[pltpu.SemaphoreType.DMA((n,))],
        compiler_params=pltpu.CompilerParams(vmem_limit_bytes=MIB),
        cost_estimate=cost(sum(2 * width * m.shape[1] for m, _ in wanted)),
        name="fetch",
    )(place, token, *[hbm(m) for m, _ in wanted])
    return res[:n], res[n]


def project_kernel(keep, sent, place_ref, *refs):
    n_dp = len(refs) - 5
    ctx, w_ref, keep_ref, send_ref, held, prod = refs[:n_dp], *refs[n_dp:]
    j, t = place_ref[0], place_ref[1]
    rows = ctx[0].shape[0]
    share = keep_ref.shape[0] // len(keep)
    for k in range(n_dp):
        held[pl.ds(pl.multiple_of((j ^ k) * rows, rows), rows), :] = ctx[k][...]
    prod[...] = jnp.dot(held[...], w_ref[...], preferred_element_type=f32)
    for i, k in enumerate(sent):
        block = pl.ds(pl.multiple_of((t ^ k) * share, share), share)
        send_ref[i * share : (i + 1) * share, :] = prod[block, :].astype(bf16)
    for i, k in enumerate(keep):
        block = pl.ds(pl.multiple_of((t ^ k) * share, share), share)
        keep_ref[i * share : (i + 1) * share, :] = prod[block, :]


def project(place, ctx, out_proj, total, keep, sent):
    width = out_proj.shape[1]
    share = total // (len(keep) + len(sent))
    depth = out_proj.shape[0]
    return pl.pallas_call(
        functools.partial(project_kernel, keep, sent),
        out_shape=[
            jax.ShapeDtypeStruct((len(keep) * share, width), f32),
            jax.ShapeDtypeStruct((len(sent) * share, width), bf16),
        ],
        in_specs=[SMEM_SPEC] + [VMEM_SPEC] * (len(ctx) + 1),
        out_specs=[VMEM_SPEC] * 2,
        scratch_shapes=[VM((total, depth), bf16), VM((total, width), f32)],
        compiler_params=pltpu.CompilerParams(vmem_limit_bytes=4 * MIB),
        cost_estimate=cost(2 * out_proj.size, 2 * total * out_proj.size),
        name="projection",
    )(place, *ctx, out_proj)


def sum_kernel(own_ref, got_ref, token_ref, sum_ref, pass_ref):
    total = own_ref[...] + got_ref[...].astype(f32)
    sum_ref[...] = total
    pass_ref[...] = total.astype(bf16)


def pass_kernel(x_ref, token_ref, out_ref):
    out_ref[...] = x_ref[...]


def passed_on(x, token):
    return pl.pallas_call(
        pass_kernel,
        out_shape=jax.ShapeDtypeStruct(x.shape, x.dtype),
        in_specs=[VMEM_SPEC] * 2,
        out_specs=VMEM_SPEC,
        compiler_params=pltpu.CompilerParams(vmem_limit_bytes=2 * MIB),
        name="passed_on",
    )(x, token)


def add_up(own, got, token):
    return pl.pallas_call(
        sum_kernel,
        out_shape=[jax.ShapeDtypeStruct(own.shape, f32), jax.ShapeDtypeStruct(own.shape, bf16)],
        in_specs=[VMEM_SPEC] * 3,
        out_specs=[VMEM_SPEC] * 2,
        compiler_params=pltpu.CompilerParams(vmem_limit_bytes=4 * MIB),
        name="pair_sum",
    )(own, got, token)


def stream_kernel(keep, arrived, place_ref, sum_ref, *refs):
    n = len(arrived)
    got, (res_ref, gain_ref, _, att_ref, msg_ref) = refs[:n], refs[n:]
    share, width = att_ref.shape
    t = place_ref[1]
    for i, k in enumerate(keep):
        x = sum_ref[i * share : (i + 1) * share, :]
        for a, m in enumerate(arrived):
            place = keep.index(k ^ m)
            x = x + got[a][place * share : (place + 1) * share, :].astype(f32)
        x = x + res_ref[pl.ds(pl.multiple_of((t ^ k) * share, share), share), :].astype(f32)
        if i == 0:
            att_ref[...] = x.astype(bf16)
        rows = slice(i * share, (i + 1) * share)
        msg_ref[rows, :width] = (x * gain_ref[...][None, :]).astype(bf16)
        left = jnp.sum(x * x, axis=1, keepdims=True)
        lane = lax.broadcasted_iota(jnp.int32, (share, TAIL), 1)
        tail = jnp.zeros((share, TAIL), f32)
        for piece in range(3):
            high = left.astype(bf16).astype(f32)
            tail = jnp.where(lane == piece, high, tail)
            left = left - high
        msg_ref[rows, width:] = tail.astype(bf16)


def stream(place, total, got, arrived, residual, gain, token, keep):
    rows, width = total.shape
    share = rows // len(keep)
    return pl.pallas_call(
        functools.partial(stream_kernel, keep, arrived),
        out_shape=[VM((share, width), bf16), jax.ShapeDtypeStruct((rows, width + TAIL), bf16)],
        in_specs=[SMEM_SPEC] + [VMEM_SPEC] * (len(got) + 4),
        out_specs=[VMEM_SPEC] * 2,
        compiler_params=pltpu.CompilerParams(vmem_limit_bytes=4 * MIB),
        name="residual_stream",
    )(place, total, *got, residual, gain, token)


def weights_kernel(owners, order, place_ref, routes_ref, given_ref, token_ref, out_ref):
    j, t = place_ref[0], place_ref[1]
    total = out_ref.shape[0]
    share = total // len(order)
    mine = jnp.where(routes_ref[...] == j // owners, given_ref[...], 0.0)
    mine = jnp.sum(mine, axis=0, keepdims=True)
    lane = lax.broadcasted_iota(jnp.int32, (share, total), 1)
    row = lax.broadcasted_iota(jnp.int32, (share, total), 0)
    for i, k in enumerate(order):
        picked = jnp.where(lane == (t ^ k) * share + row, mine, 0.0)
        out_ref[i * share : (i + 1) * share, :] = jnp.sum(picked, axis=1, keepdims=True)


def request_weights(place, routes, given, token, owners, order):
    return pl.pallas_call(
        functools.partial(weights_kernel, owners, order),
        out_shape=jax.ShapeDtypeStruct((routes.shape[1], 1), f32),
        in_specs=[SMEM_SPEC] + [VMEM_SPEC] * 3,
        out_specs=VMEM_SPEC,
        compiler_params=pltpu.CompilerParams(vmem_limit_bytes=4 * MIB),
        name="request_weights",
    )(place, routes, given, token)


def join(x_ref, parts, width):
    at = 0
    sq = []
    for p in parts:
        n = p.shape[0]
        x_ref[at : at + n, :] = p[:, :width]
        sq.append(jnp.sum(p[:, width:].astype(f32), axis=1, keepdims=True))
        at += n
    return jnp.concatenate(sq, axis=0)


def grow_kernel(first, odd, model, row_ks, ks, place_ref, *refs):
    last = odd is not None
    (a_ref, b_ref, gate, up), refs = refs[:4], refs[4:]
    if not first:
        (in_g, in_u, in_sq), refs = refs[:3], refs[3:]
    if last:
        weight, ready, refs = refs[0], refs[1 : 1 + len(odd)], refs[1 + len(odd) :]
    n = len(row_ks)
    mats, wd, refs = refs[:n], refs[n], refs[n + 1 :]
    if last:
        outs, h_ref, refs = refs[: len(odd)], refs[len(odd)], refs[len(odd) + 1 :]
    else:
        (acc_g, acc_u, sq_ref), refs = refs[:3], refs[3:]
    rows_loaded, loaded, (x_ref, row_sem, sem) = refs[:n], refs[n : n + len(ks)], refs[n + len(ks) :]
    loads = row_loads(place_ref, mats, row_ks, rows_loaded, row_sem) + col_loads(place_ref, wd, ks, loaded, sem)
    all_of(loads, "start")
    sq = join(x_ref, (a_ref, b_ref), x_ref.shape[1])
    if not first:
        sq = sq + in_sq[...]

    def columns(cols):
        g = jnp.dot(x_ref[...], gate[:, cols], preferred_element_type=f32)
        u = jnp.dot(x_ref[...], up[:, cols], preferred_element_type=f32)
        if not first:
            g, u = g + in_g[:, cols], u + in_u[:, cols]
        if last:
            scale = lax.rsqrt(sq / model + EPS)
            g, u = g * scale, u * (scale * weight[...])
            h_ref[:, cols] = (g / (1.0 + jnp.exp(-g)) * u).astype(bf16)
        else:
            acc_g[:, cols], acc_u[:, cols] = g, u

    hidden = gate.shape[1]
    if loads:

        @pl.loop(0, 2)
        def _(c):
            columns(pl.ds(pl.multiple_of(c * (hidden // 2), 128), hidden // 2))
    else:
        step = min(512, hidden)
        for lo in range(0, hidden, step):
            columns(slice(lo, lo + step))
    if last:
        for i in range(len(odd)):
            outs[i][...] = jnp.dot(h_ref[...], ready[i][...], preferred_element_type=f32).astype(bf16)
    else:
        sq_ref[...] = sq
    all_of(loads, "wait")


def grow(place, parts, gate, up, acc, ahead, down, ks, model, last):
    rows = parts[0].shape[0] + parts[1].shape[0]
    width, hidden = gate.shape
    args = [*parts, gate, up] + (list(acc) if acc is not None else [])
    odd = None
    if last is not None:
        weight, odd, ready = last
        args += [weight, *ready]
        outs = [jax.ShapeDtypeStruct((rows, width), bf16) for _ in odd] + [jax.ShapeDtypeStruct((rows, hidden), bf16)]
    else:
        outs = [jax.ShapeDtypeStruct((rows, n), f32) for n in (hidden, hidden, 1)]
    own = len(outs)
    res = pl.pallas_call(
        functools.partial(grow_kernel, acc is None, odd, model, [k for _, k in ahead], ks),
        out_shape=outs + [VM((width, hidden), bf16) for _ in ahead] + [VM((hidden, width), bf16) for _ in ks],
        in_specs=[SMEM_SPEC] + [VMEM_SPEC] * len(args) + [HBM_SPEC] * (len(ahead) + 1),
        out_specs=[VMEM_SPEC] * (own + len(ahead) + len(ks)),
        scratch_shapes=[VM((rows, width), bf16), pltpu.SemaphoreType.DMA((max(1, len(ahead)),)), pltpu.SemaphoreType.DMA((max(1, len(ks)),))],
        compiler_params=pltpu.CompilerParams(vmem_limit_bytes=4 * MIB),
        cost_estimate=cost(4 * width * hidden, 4 * rows * width * hidden),
        name="experts_last" if last is not None else "experts",
    )(place, *args, *[hbm(m) for m, _ in ahead], hbm(down))
    return res[:own], res[own : own + len(ahead)], res[own + len(ahead) :]


def back_kernel(n, place_ref, h_ref, *refs):
    adds, ready, outs = refs[:n], refs[n : 2 * n], refs[2 * n : 4 * n]
    half = outs[0].shape[0]
    for i in range(n):
        value = jnp.dot(h_ref[...], ready[i][...], preferred_element_type=f32) + adds[i][...].astype(f32)
        value = value.astype(bf16)
        outs[2 * i][...] = value[:half]
        outs[2 * i + 1][...] = value[half:]


def back(place, h, adds, ready):
    rows = h.shape[0]
    n, width = len(ready), ready[0].shape[1]
    res = pl.pallas_call(
        functools.partial(back_kernel, n),
        out_shape=[jax.ShapeDtypeStruct((rows // 2, width), bf16) for _ in range(2 * n)],
        in_specs=[SMEM_SPEC] + [VMEM_SPEC] * (1 + 2 * n),
        out_specs=[VMEM_SPEC] * (2 * n),
        compiler_params=pltpu.CompilerParams(vmem_limit_bytes=4 * MIB),
        name="back",
    )(place, h, *adds, *ready)
    return [res[2 * i : 2 * i + 2] for i in range(n)]


def own_kernel(place_ref, h_ref, add_ref, token_ref, wd, a_ref, b_ref, buf, sem):
    loads = col_loads(place_ref, wd, [0], [buf], sem)
    all_of(loads, "start")
    all_of(loads, "wait")
    half = a_ref.shape[0]
    value = jnp.dot(h_ref[...], buf[...], preferred_element_type=f32) + add_ref[...].astype(f32)
    a_ref[...] = value[:half]
    b_ref[...] = value[half:]


def own_block(place, h, add, token, down, width):
    rows, hidden = h.shape
    return pl.pallas_call(
        own_kernel,
        out_shape=[jax.ShapeDtypeStruct((rows // 2, width), f32)] * 2,
        in_specs=[SMEM_SPEC] + [VMEM_SPEC] * 3 + [HBM_SPEC],
        out_specs=[VMEM_SPEC] * 2,
        scratch_shapes=[VM((hidden, width), bf16), pltpu.SemaphoreType.DMA((1,))],
        compiler_params=pltpu.CompilerParams(vmem_limit_bytes=10 * MIB),
        cost_estimate=cost(2 * width * hidden, 2 * rows * width * hidden),
        name="own_block",
    )(place, h, add, token, hbm(down))


def gather_dp(x):
    n = lax.axis_size("dp")
    far = [swap(x, "dp", k) for k in range(2, n, 2)]
    out = [x, swap(x, "dp", 1)]
    for a in far:
        out += [a, swap(a, "dp", 1)]
    return out


def body(
    query,
    key_value_new,
    key_value_cache,
    cache_len,
    out_proj,
    residual,
    norm_gain,
    routes,
    route_weight,
    w_gate,
    w_up,
    w_down,
):
    n_dp = lax.axis_size("dp")
    n_tp = lax.axis_size("tp")
    j, t = lax.axis_index("dp"), lax.axis_index("tp")
    place = jnp.stack([j, t]).astype(jnp.int32)
    total, width = residual.shape
    share = total // n_tp
    keep, sent = list(range(0, n_tp, 2)), list(range(1, n_tp, 2))
    even, odd = list(range(2, n_dp, 2)), list(range(3, n_dp, 2))

    context, proj_weight = attend(place, query, key_value_new, key_value_cache, cache_len, out_proj)

    ctx = gather_dp(context)

    kept, parted = project(place, ctx, proj_weight, total, keep, sent)
    got = swap(parted, "tp", 1)
    (gate0,), token = fetch(place, parted, [(w_gate, 0)], width)
    sums, passed = add_up(kept, got, token)
    got = [swap(passed, "tp", k) for k in keep[1:]]
    (up0, gate1, up1, gate2), token = fetch(
        place, passed, [(w_up, 0), (w_gate, 1), (w_up, 1), (w_gate, 2)], width
    )
    attended, near = stream(place, sums, got, keep[1:], residual, norm_gain, token, keep)
    weight = request_weights(place, routes.T, route_weight.T, near, n_dp // EXPERTS, keep + sent)

    other = swap(near, "tp", 1)
    far_near = [swap(near, "dp", k) for k in even]
    (up2,), token = fetch(place, near, [(w_up, 2)], width)
    other = passed_on(other, token)
    core_near = swap(near, "dp", 1)
    far_other = [swap(other, "dp", k) for k in even]
    core_other = swap(other, "dp", 1)
    halves = [(near, other), (core_near, core_other)]
    for a, b in zip(far_near, far_other):
        halves += [(a, b), (swap(a, "dp", 1), swap(b, "dp", 1))]
    gates, ups = [gate0, gate1, gate2], [up0, up1, up2]
    odd = odd + [1]
    acc, ready = None, {}
    for i in range(n_dp):
        ahead = [(m, k) for m, at in ((w_gate, 0), (w_up, 1)) for k in range(3, n_dp) if i == at]
        downs = {2: odd, n_dp - 1: even}.get(i, [])
        last = (weight, odd, [ready[k] for k in odd]) if i == n_dp - 1 else None
        acc, late, loaded = grow(
            place, halves[i], gates[i], ups[i], acc, ahead, w_down, downs, w_gate.shape[0], last
        )
        for (m, _), v in zip(ahead, late):
            (gates if m is w_gate else ups).append(v)
        ready.update(zip(downs, loaded))
    out_odd, h = acc[:-1], acc[-1]

    crossed = [swap(o, "dp", 1) for o in out_odd]
    sums = back(place, h, crossed[:-1], [ready[k] for k in even])
    there = [swap(s[1], "dp", k) for s, k in zip(sums, even)]
    here = [swap(s[0], "dp", k) for s, k in zip(sums, even)]
    mix_a, mix_b = own_block(place, h, crossed[-1], sums[0][1], w_down, width)
    for x in there:
        mix_b = mix_b + x.astype(f32)
    got = swap(mix_b.astype(bf16), "tp", 1).astype(f32)
    for x in here:
        mix_a = mix_a + x.astype(f32)
    mix = mix_a + got
    result = mix[:share]
    for i, k in enumerate(keep[1:]):
        result = result + swap(mix[(i + 1) * share : (i + 2) * share].astype(bf16), "tp", k).astype(f32)
    return (attended, result.astype(bf16))


def solution(mesh):
    in_specs = (
        P(("grp", "dp"), "tp"),
        P(("grp", "dp"), "tp"),
        P(("grp", "dp"), None, "tp"),
        P(("grp", "dp")),
        P("tp", "dp"),
        P("grp", "dp"),
        P("dp"),
        P("grp", None),
        P("grp", None),
        P(None, ("dp", "tp")),
        P(None, ("dp", "tp")),
        P(("dp", "tp"), None),
    )
    out_specs = (P(("grp", "tp"), "dp"), P(("grp", "tp"), "dp"))
    return jax.shard_map(body, mesh=mesh, in_specs=in_specs, out_specs=out_specs, check_vma=False)
```

time: 261 us -> 86.9 us (0.33)
  local copies, waits for them, and re-layouts: 67.5 us -> 0.67 us
  Pallas kernels: 0 us -> 47.5 us
  waiting for transfers between devices: 59.1 us -> 15.6 us
  matrix products: 41.5 us -> 0 us
  other arithmetic: 42.2 us -> 0.82 us
  blocking collectives: 31.9 us -> 0 us
  starting transfers between devices: 3.61 us -> 21.2 us
  between operations: 14.3 us -> 0.86 us
    pallas_call x0 -> x15, Pallas kernels: none -> 47.5 us  [the longest x4 16.8 us: grow(): pl.pallas_call(functools.partial(grow_kernel, acc is None, odd, model, [k...]
    dot_general x6 -> x0, matrix products: 41.5 us -> none  [the longest x1 19.7 us: expert_ffn(): return jnp.dot(hidden, wd, preferred_element_type=jnp.float32)]
    unnamed x2 -> x0, other arithmetic: 34.6 us -> none
    psum x1 -> x0, waiting for transfers between devices: 24.4 us -> none  [body(): proj = lax.psum(partial_proj.astype(jnp.bfloat16), 'tp').astype(jnp.float32)]
    ppermute x0 -> x18, starting transfers between devices: none -> 21.2 us  [swap(): return lax.ppermute(x, axis, [(i, i ^ k) for i in range(n)])]
    reduce_scatter x1 -> x0, waiting for transfers between devices: 19 us -> none  [body(): lax.psum_scatter(combined.astype(jnp.bfloat16), 'tp', scatter_dimension=0...]
    all_to_all x1 -> x0, blocking collectives: 18.3 us -> none  [body(): lax.all_to_all(outgoing, 'dp', split_axis=0, concat_axis=2, tiled=True)[0]]
    slice x4 -> x1, local copies, waits for them, and re-layouts: 17.7 us -> 0.01 us  [body(): mix[(i + 1) * share:(i + 2) * share].astype(bf16)]
  transfers between devices with their start and end apart: 3 -> 18, of which waited for: 3 -> 8; matrix products, arithmetic and copies ran while one was open for 6% -> 1% of each run, Pallas kernels for 0% -> 39%
where the time goes in v2:
time: 86.9 us; the launch traced here: 86.6 us
  Pallas kernels  47.5 us (55%)
  starting transfers between devices  21.2 us (24%)
  waiting for transfers between devices  15.6 us (18%)
    ppermute x18, starting transfers between devices, swap(): return lax.ppermute(x, axis, [(i, i ^ k) for i in range(n)])  21.2 us
    pallas_call x4, Pallas kernels, grow(): pl.pallas_call(functools.partial(grow_kernel, acc is None, odd, model, [k...  16.8 us
    ppermute x18, waiting for transfers between devices, swap(): return lax.ppermute(x, axis, [(i, i ^ k) for i in range(n)])  15.6 us
    pallas_call x3, Pallas kernels, fetch(): pl.pallas_call(functools.partial(fetch_kernel, ks), out_shape=[VM((width,...  15.4 us
    pallas_call x1, Pallas kernels, attend(): pl.pallas_call(functools.partial(attend_kernel, kv, group, batch), out_sh...  6.56 us
    pallas_call x1, Pallas kernels, own_block(): pl.pallas_call(own_kernel, out_shape=[jax.ShapeDtypeStruct((rows // 2, wi...  4.36 us
  transfers between devices with their start and end apart: 18, of which 8 were waited for; matrix products, arithmetic and copies ran while one was open for 1% of the time, Pallas kernels for 39%

profile of v2, /device:TPU:0, one launch (start us, length us, event | category | flops | bytes accessed | tf_op | source)
XLA Modules:
  0.0 86.6 jit_solution(870505813514135113)
XLA Ops:
  0.6 0.1 pad_add_fusion._.place_ref
  0.7 6.6 %attention.1 = (bf16[32,1536]{1,0:T(8,128)(2,1)S(1)}, bf16[1536,1536]{1,0:T(8,128)(2,1)S(1)}) custom-call(s32[2]{0:T(128)S(1)} %pad_add_fusion._.place_ref, s32[32]{0:T(128)} %len_hbm.1, bf16[32,1536]{1,0:T(8,128)(2,1)} %q_hbm.1, bf16[32,512]{1,0:T(8,128)(2,1)} %new_hbm.1, bf16[32,160,512]{2,1,0:T(8,128)(2,1)} %cache_hbm.1, bf16[1536,1536]{1,0:T(8,128)(2,1)} %w_hbm.1), custom_call_target="tpu_custom_call" | custom-call | flops 62914560 | bytes 10485760 | tf_op jit(solution)/shard_map/attention/pallas_call | solution.py:126
  7.3 3.0 %collective-permute-start.1 = (bf16[32,1536]{1,0:T(8,128)(2,1)S(1)}, bf16[32,1536]{1,0:T(8,128)(2,1)S(1)}, u32[]{:S(2)}, u32[]{:S(2)}) collective-permute-start(bf16[32,1536]{1,0:T(8,128)(2,1)S(1)} %get-tuple-element.40.refs_0_), channel_id=1, source_target_pairs={{0,8},{4,12},{8,0},{12,4},{1,9},{5,13},{9,1},{13,5},{2,10},{6,14},... | collective-permute-start | bytes 294920 | tf_op jit(solution)/shard_map/ppermute | solution.py:26
  10.3 0.0 collective-permute-start
  10.3 2.8 %collective-permute-done.1.refs_2_ = bf16[32,1536]{1,0:T(8,128)(2,1)S(1)} collective-permute-done((bf16[32,1536]{1,0:T(8,128)(2,1)S(1)}, bf16[32,1536]{1,0:T(8,128)(2,1)S(1)}, u32[]{:S(2)}, u32[]{:S(2)}) %collective-permute-start.1) | collective-permute-done | bytes 98336 | tf_op jit(solution)/shard_map/ppermute | solution.py:26
  13.1 0.0 collective-permute-start.2
  13.1 0.0 collective-permute-done.refs_1_
  13.1 1.3 %collective-permute-done.2.refs_3_ = bf16[32,1536]{1,0:T(8,128)(2,1)S(1)} collective-permute-done((bf16[32,1536]{1,0:T(8,128)(2,1)S(1)}, bf16[32,1536]{1,0:T(8,128)(2,1)S(1)}, u32[]{:S(2)}, u32[]{:S(2)}) %collective-permute-start.2) | collective-permute-done | bytes 98336 | tf_op jit(solution)/shard_map/ppermute | solution.py:26
  14.4 1.4 %projection.1 = (f32[64,1536]{1,0:T(8,128)S(1)}, bf16[64,1536]{1,0:T(8,128)(2,1)S(1)}) custom-call(s32[2]{0:T(128)S(1)} %pad_add_fusion._.place_ref, bf16[32,1536]{1,0:T(8,128)(2,1)S(1)} %get-tuple-element.40.refs_0_, bf16[32,1536]{1,0:T(8,128)(2,1)S(1)} %collective-permute-done.refs_1_, bf16[32,1536]{1,0:T(8,128)(2,1)S(1)} %collective-permute-done.1.refs_2_, ...), custom_call_target="tpu_custom_call" | custom-call | flops 603979776 | bytes 4718592 | tf_op jit(solution)/shard_map/projection/pallas_call | solution.py:193
  15.8 1.9 %collective-permute-start.3 = (bf16[64,1536]{1,0:T(8,128)(2,1)S(1)}, bf16[64,1536]{1,0:T(8,128)(2,1)S(1)}, u32[]{:S(2)}, u32[]{:S(2)}) collective-permute-start(bf16[64,1536]{1,0:T(8,128)(2,1)S(1)} %get-tuple-element.43.token_ref), channel_id=1, source_target_pairs={{0,1},{1,0},{2,3},{3,2},{4,5},{5,4},{6,7},{7,6},{8,9},{9,8},{10,11... | collective-permute-start | bytes 589832 | tf_op jit(solution)/shard_map/ppermute | solution.py:26
  17.7 3.3 %fetch.3 = (bf16[1536,2048]{1,0:T(8,128)(2,1)S(1)}, bf16[8,128]{1,0:T(8,128)(2,1)S(1)}) custom-call(s32[2]{0:T(128)S(1)} %pad_add_fusion._.place_ref, bf16[64,1536]{1,0:T(8,128)(2,1)S(1)} %get-tuple-element.43.token_ref, bf16[6144,2048]{1,0:T(8,128)(2,1)} %refs_4_.1), custom_call_target="tpu_custom_call" | custom-call | bytes 6291456 | tf_op jit(solution)/shard_map/fetch/pallas_call | solution.py:159
  21.1 1.9 %collective-permute-done.3.got_ref = bf16[64,1536]{1,0:T(8,128)(2,1)S(1)} collective-permute-done((bf16[64,1536]{1,0:T(8,128)(2,1)S(1)}, bf16[64,1536]{1,0:T(8,128)(2,1)S(1)}, u32[]{:S(2)}, u32[]{:S(2)}) %collective-permute-start.3) | collective-permute-done | bytes 196640 | tf_op jit(solution)/shard_map/ppermute | solution.py:26
  23.0 0.1 pair_sum.1
  23.0 0.0 copy-start
  23.0 0.0 copy-start.1
  23.0 2.8 %collective-permute-start.4 = (bf16[64,1536]{1,0:T(8,128)(2,1)S(1)}, bf16[64,1536]{1,0:T(8,128)(2,1)S(1)}, u32[]{:S(2)}, u32[]{:S(2)}) collective-permute-start(bf16[64,1536]{1,0:T(8,128)(2,1)S(1)} %get-tuple-element.46.token_ref), channel_id=1, source_target_pairs={{0,2},{1,3},{2,0},{3,1},{4,6},{5,7},{6,4},{7,5},{8,10},{9,11},{10,... | collective-permute-start | bytes 589832 | tf_op jit(solution)/shard_map/ppermute | solution.py:26
  25.9 8.8 %fetch.4 = (bf16[1536,2048]{1,0:T(8,128)(2,1)S(1)}, bf16[1536,2048]{1,0:T(8,128)(2,1)S(1)}, bf16[1536,2048]{1,0:T(8,128)(2,1)S(1)}, bf16[1536,2048]{1,0:T(8,128)(2,1)S(1)}, bf16[8,128]{1,0:T(8,128)(2,1)S(1)}) custom-call(s32[2]{0:T(128)S(1)} %pad_add_fusion._.place_ref, bf16[64,1536]{1,0:T(8,128)(2,1)S(1)} %get-tuple-element.46.token_ref, ...), custom_call_target="tpu_custom_call" | custom-call | bytes 25165824 | tf_op jit(solution)/shard_map/fetch/pallas_call | solution.py:159
  34.6 0.0 collective-permute-done.4.refs_0_
  34.6 0.0 copy-done
  34.7 0.0 copy-done.1
  34.7 0.7 residual_stream.1
  35.4 0.0 copy-start.2
  35.4 0.0 copy-start.3
  35.4 1.6 %collective-permute-start.7 = (bf16[64,1664]{1,0:T(8,128)(2,1)S(1)}, bf16[64,1664]{1,0:T(8,128)(2,1)S(1)}, u32[]{:S(2)}, u32[]{:S(2)}) collective-permute-start(bf16[64,1664]{1,0:T(8,128)(2,1)S(1)} %get-tuple-element.49.token_ref.refs_0_), channel_id=1, source_target_pairs={{0,1},{1,0},{2,3},{3,2},{4,5},{5,4},{6,7},{7,6},{8,9},{9,8},{10,11... | collective-permute-start | bytes 638984 | tf_op jit(solution)/shard_map/ppermute | solution.py:26
  37.0 1.5 %collective-permute-start.5 = (bf16[64,1664]{1,0:T(8,128)(2,1)S(1)}, bf16[64,1664]{1,0:T(8,128)(2,1)S(1)}, u32[]{:S(2)}, u32[]{:S(2)}) collective-permute-start(bf16[64,1664]{1,0:T(8,128)(2,1)S(1)} %get-tuple-element.49.token_ref.refs_0_), channel_id=1, source_target_pairs={{0,8},{4,12},{8,0},{12,4},{1,9},{5,13},{9,1},{13,5},{2,10},{6,14},... | collective-permute-start | bytes 638984 | tf_op jit(solution)/shard_map/ppermute | solution.py:26
  38.6 3.3 %fetch.5 = (bf16[1536,2048]{1,0:T(8,128)(2,1)S(1)}, bf16[8,128]{1,0:T(8,128)(2,1)S(1)}) custom-call(s32[2]{0:T(128)S(1)} %pad_add_fusion._.place_ref, bf16[64,1664]{1,0:T(8,128)(2,1)S(1)} %get-tuple-element.49.token_ref.refs_0_, bf16[6144,2048]{1,0:T(8,128)(2,1)} %refs_7_.2), custom_call_target="tpu_custom_call" | custom-call | bytes 6291456 | tf_op jit(solution)/shard_map/fetch/pallas_call | solution.py:159
  41.9 0.0 collective-permute-done.7.x_ref
  41.9 1.3 %collective-permute-start.8 = (bf16[64,1664]{1,0:T(8,128)(2,1)S(1)}, bf16[64,1664]{1,0:T(8,128)(2,1)S(1)}, u32[]{:S(2)}, u32[]{:S(2)}) collective-permute-start(bf16[64,1664]{1,0:T(8,128)(2,1)S(1)} %passed_on.1.refs_1_), channel_id=1, source_target_pairs={{0,8},{4,12},{8,0},{12,4},{1,9},{5,13},{9,1},{13,5},{2,10},{6,14},... | collective-permute-start | bytes 638984 | tf_op jit(solution)/shard_map/ppermute | solution.py:26
  43.3 0.0 collective-permute-start.10
  43.3 0.5 collective-permute-start.11
  43.8 0.0 copy-done.2
  43.8 0.0 copy-done.3
  43.8 0.6 request_weights.1.refs_7_
  44.4 0.0 collective-permute-done.5.refs_0_
  44.4 0.1 collective-permute-start.6
  44.5 3.4 %experts.3 = (f32[128,2048]{1,0:T(8,128)S(1)}, f32[128,2048]{1,0:T(8,128)S(1)}, f32[128,1]{1,0:T(8,128)S(1)}, bf16[1536,2048]{1,0:T(8,128)(2,1)S(1)}) custom-call(s32[2]{0:T(128)S(1)} %pad_add_fusion._.place_ref, bf16[64,1664]{1,0:T(8,128)(2,1)S(1)} %get-tuple-element.49.token_ref.refs_0_, bf16[64,1664]{1,0:T(8,128)(2,1)S(1)} %passed_on.1.refs_1_, ...), custom_call_target="tpu_custom_call" | custom-call | flops 1610612736 | bytes 12582912 | tf_op jit(solution)/shard_map/experts/pallas_call | solution.py:375
  47.9 0.0 collective-permute-done.8.refs_1_
  47.9 0.6 collective-permute-start.9
  48.4 0.0 collective-permute-done.10.refs_0_
  48.4 0.0 collective-permute-done.11.refs_1_
  48.4 3.4 %experts.4 = (f32[128,2048]{1,0:T(8,128)S(1)}, f32[128,2048]{1,0:T(8,128)S(1)}, f32[128,1]{1,0:T(8,128)S(1)}, bf16[1536,2048]{1,0:T(8,128)(2,1)S(1)}) custom-call(s32[2]{0:T(128)S(1)} %pad_add_fusion._.place_ref, bf16[64,1664]{1,0:T(8,128)(2,1)S(1)} %collective-permute-done.10.refs_0_, bf16[64,1664]{1,0:T(8,128)(2,1)S(1)} %collective-permute-done.11.refs_1_, ...), custom_call_target="tpu_custom_call" | custom-call | flops 1610612736 | bytes 12582912 | tf_op jit(solution)/shard_map/experts/pallas_call | solution.py:375
  51.8 5.2 %experts.5 = (f32[128,2048]{1,0:T(8,128)S(1)}, f32[128,2048]{1,0:T(8,128)S(1)}, f32[128,1]{1,0:T(8,128)S(1)}, bf16[2048,1536]{1,0:T(8,128)(2,1)S(1)}, bf16[2048,1536]{1,0:T(8,128)(2,1)S(1)}) custom-call(s32[2]{0:T(128)S(1)} %pad_add_fusion._.place_ref, bf16[64,1664]{1,0:T(8,128)(2,1)S(1)} %collective-permute-done.5.refs_0_, ...), custom_call_target="tpu_custom_call" | custom-call | flops 1610612736 | bytes 12582912 | tf_op jit(solution)/shard_map/experts/pallas_call | solution.py:375
  57.0 0.0 collective-permute-done.6.refs_0_
  57.0 0.0 collective-permute-done.9.refs_1_
  57.0 4.9 %experts_last.1 = (bf16[128,1536]{1,0:T(8,128)(2,1)S(1)}, bf16[128,1536]{1,0:T(8,128)(2,1)S(1)}, bf16[128,2048]{1,0:T(8,128)(2,1)S(1)}, bf16[2048,1536]{1,0:T(8,128)(2,1)S(1)}) custom-call(s32[2]{0:T(128)S(1)} %pad_add_fusion._.place_ref, bf16[64,1664]{1,0:T(8,128)(2,1)S(1)} %collective-permute-done.6.refs_0_, ...), custom_call_target="tpu_custom_call" | custom-call | flops 1610612736 | bytes 12582912 | tf_op jit(solution)/shard_map/experts_last/pallas_call | solution.py:375
  61.9 0.1 collective-permute-start.13
  62.0 0.5 collective-permute-start.12
  62.5 1.2 %collective-permute-done.13.refs_0_ = bf16[128,1536]{1,0:T(8,128)(2,1)S(1)} collective-permute-done((bf16[128,1536]{1,0:T(8,128)(2,1)S(1)}, bf16[128,1536]{1,0:T(8,128)(2,1)S(1)}, u32[]{:S(2)}, u32[]{:S(2)}) %collective-permute-start.13) | collective-permute-done | bytes 393248 | tf_op jit(solution)/shard_map/ppermute | solution.py:26
  63.7 1.5 %back.1 = (bf16[64,1536]{1,0:T(8,128)(2,1)S(1)}, bf16[64,1536]{1,0:T(8,128)(2,1)S(1)}) custom-call(s32[2]{0:T(128)S(1)} %pad_add_fusion._.place_ref, bf16[128,2048]{1,0:T(8,128)(2,1)S(1)} %get-tuple-element.70.h_ref, bf16[128,1536]{1,0:T(8,128)(2,1)S(1)} %collective-permute-done.13.refs_0_, bf16[2048,1536]{1,0:T(8,128)(2,1)S(1)} %get-tuple-element.73.refs_1_), custom_call_target="tpu_custom_call" | custom-call | tf_op jit(solution)/shard_map/back/pallas_call | solution.py:401
  65.2 0.9 %collective-permute-start.15 = (bf16[64,1536]{1,0:T(8,128)(2,1)S(1)}, bf16[64,1536]{1,0:T(8,128)(2,1)S(1)}, u32[]{:S(2)}, u32[]{:S(2)}) collective-permute-start(bf16[64,1536]{1,0:T(8,128)(2,1)S(1)} %get-tuple-element.74.token_ref), channel_id=1, source_target_pairs={{0,8},{4,12},{8,0},{12,4},{1,9},{5,13},{9,1},{13,5},{2,10},{6,14},... | collective-permute-start | bytes 589832 | tf_op jit(solution)/shard_map/ppermute | solution.py:26
  66.1 1.2 %collective-permute-start.14 = (bf16[64,1536]{1,0:T(8,128)(2,1)S(1)}, bf16[64,1536]{1,0:T(8,128)(2,1)S(1)}, u32[]{:S(2)}, u32[]{:S(2)}) collective-permute-start(bf16[64,1536]{1,0:T(8,128)(2,1)S(1)} %get-tuple-element.76), channel_id=1, source_target_pairs={{0,8},{4,12},{8,0},{12,4},{1,9},{5,13},{9,1},{13,5},{2,10},{6,14},... | collective-permute-start | bytes 589832 | tf_op jit(solution)/shard_map/ppermute | solution.py:26
  67.3 0.0 collective-permute-done.12.add_ref
  67.3 4.4 %own_block.1 = (f32[64,1536]{1,0:T(8,128)S(1)}, f32[64,1536]{1,0:T(8,128)S(1)}) custom-call(s32[2]{0:T(128)S(1)} %pad_add_fusion._.place_ref, bf16[128,2048]{1,0:T(8,128)(2,1)S(1)} %get-tuple-element.70.h_ref, bf16[128,1536]{1,0:T(8,128)(2,1)S(1)} %collective-permute-done.12.add_ref, bf16[64,1536]{1,0:T(8,128)(2,1)S(1)} %get-tuple-element.74.token_ref, ...), custom_call_target="tpu_custom_call" | custom-call | flops 805306368 | bytes 6291456 | tf_op jit(solution)/shard_map/own_block/pallas_call | solution.py:424
  71.7 1.3 %collective-permute-done.15 = bf16[64,1536]{1,0:T(8,128)(2,1)S(1)} collective-permute-done((bf16[64,1536]{1,0:T(8,128)(2,1)S(1)}, bf16[64,1536]{1,0:T(8,128)(2,1)S(1)}, u32[]{:S(2)}, u32[]{:S(2)}) %collective-permute-start.15) | collective-permute-done | bytes 196640 | tf_op jit(solution)/shard_map/ppermute | solution.py:26
  73.1 1.7 %collective-permute-start.16 = (bf16[64,1536]{1,0:T(8,128)(2,1)S(1)}, bf16[64,1536]{1,0:T(8,128)(2,1)S(1)}, u32[]{:S(2)}, u32[]{:S(2)}) collective-permute-start(bf16[64,1536]{1,0:T(8,128)(2,1)S(1)} %add_convert_fusion), channel_id=1, source_target_pairs={{0,1},{1,0},{2,3},{3,2},{4,5},{5,4},{6,7},{7,6},{8,9},{9,8},{10,11... | collective-permute-start | bytes 589832 | tf_op jit(solution)/shard_map/ppermute | solution.py:26
  74.7 1.7 %collective-permute-done.14 = bf16[64,1536]{1,0:T(8,128)(2,1)S(1)} collective-permute-done((bf16[64,1536]{1,0:T(8,128)(2,1)S(1)}, bf16[64,1536]{1,0:T(8,128)(2,1)S(1)}, u32[]{:S(2)}, u32[]{:S(2)}) %collective-permute-start.14) | collective-permute-done | bytes 196640 | tf_op jit(solution)/shard_map/ppermute | solution.py:26
  76.5 2.4 %collective-permute-done.16 = bf16[64,1536]{1,0:T(8,128)(2,1)S(1)} collective-permute-done((bf16[64,1536]{1,0:T(8,128)(2,1)S(1)}, bf16[64,1536]{1,0:T(8,128)(2,1)S(1)}, u32[]{:S(2)}, u32[]{:S(2)}) %collective-permute-start.16) | collective-permute-done | bytes 196640 | tf_op jit(solution)/shard_map/ppermute | solution.py:26
  78.8 0.1 convert_add_fusion
  78.9 3.4 %collective-permute-start.17 = (bf16[32,1536]{1,0:T(8,128)(2,1)S(1)}, bf16[32,1536]{1,0:T(8,128)(2,1)S(1)}, u32[]{:S(2)}, u32[]{:S(2)}) collective-permute-start(bf16[32,1536]{1,0:T(8,128)(2,1)S(1)} %slice.15), channel_id=1, source_target_pairs={{0,2},{1,3},{2,0},{3,1},{4,6},{5,7},{6,4},{7,5},{8,10},{9,11},{10,... | collective-permute-start | bytes 294920 | tf_op jit(solution)/shard_map/ppermute | solution.py:26
  82.3 0.6 copy.14
  83.0 3.0 %collective-permute-done.17 = bf16[32,1536]{1,0:T(8,128)(2,1)S(1)} collective-permute-done((bf16[32,1536]{1,0:T(8,128)(2,1)S(1)}, bf16[32,1536]{1,0:T(8,128)(2,1)S(1)}, u32[]{:S(2)}, u32[]{:S(2)}) %collective-permute-start.17) | collective-permute-done | bytes 98336 | tf_op jit(solution)/shard_map/ppermute | solution.py:26
  86.0 0.7 fusion
  (3 shorter events, 0.1 us)
Async XLA Ops:
  7.3 5.8 %collective-permute-start.1 = (bf16[32,1536]{1,0:T(8,128)(2,1)S(1)}, bf16[32,1536]{1,0:T(8,128)(2,1)S(1)}, u32[]{:S(2)}, u32[]{:S(2)}) collective-permute-start(bf16[32,1536]{1,0:T(8,128)(2,1)S(1)} %get-tuple-element.40.refs_0_), channel_id=1, source_target_pairs={{0,8},{4,12},{8,0},{12,4},{1,9},{5,13},{9,1},{13,5},{2,10},{6,14},... | collective-permute-start | bytes 294920 | tf_op jit(solution)/shard_map/ppermute | solution.py:26
  10.3 2.8 %collective-permute-start = (bf16[32,1536]{1,0:T(8,128)(2,1)S(1)}, bf16[32,1536]{1,0:T(8,128)(2,1)S(1)}, u32[]{:S(2)}, u32[]{:S(2)}) collective-permute-start(bf16[32,1536]{1,0:T(8,128)(2,1)S(1)} %get-tuple-element.40.refs_0_), channel_id=1, source_target_pairs={{0,4},{4,0},{8,12},{12,8},{1,5},{5,1},{9,13},{13,9},{2,6},{6,2},{1... | collective-permute-start | bytes 294920 | tf_op jit(solution)/shard_map/ppermute | solution.py:26
  13.1 1.3 %collective-permute-start.2 = (bf16[32,1536]{1,0:T(8,128)(2,1)S(1)}, bf16[32,1536]{1,0:T(8,128)(2,1)S(1)}, u32[]{:S(2)}, u32[]{:S(2)}) collective-permute-start(bf16[32,1536]{1,0:T(8,128)(2,1)S(1)} %collective-permute-done.1.refs_2_), channel_id=1, source_target_pairs={{0,4},{4,0},{8,12},{12,8},{1,5},{5,1},{9,13},{13,9},{2,6},{6,2},{1... | collective-permute-start | bytes 294920 | tf_op jit(solution)/shard_map/ppermute | solution.py:26
  15.8 7.2 %collective-permute-start.3 = (bf16[64,1536]{1,0:T(8,128)(2,1)S(1)}, bf16[64,1536]{1,0:T(8,128)(2,1)S(1)}, u32[]{:S(2)}, u32[]{:S(2)}) collective-permute-start(bf16[64,1536]{1,0:T(8,128)(2,1)S(1)} %get-tuple-element.43.token_ref), channel_id=1, source_target_pairs={{0,1},{1,0},{2,3},{3,2},{4,5},{5,4},{6,7},{7,6},{8,9},{9,8},{10,11... | collective-permute-start | bytes 589832 | tf_op jit(solution)/shard_map/ppermute | solution.py:26
  23.0 11.6 %copy-start = (bf16[128,1536]{1,0:T(8,128)(2,1)S(1)}, bf16[128,1536]{1,0:T(8,128)(2,1)}, u32[]{:S(2)}) copy-start(bf16[128,1536]{1,0:T(8,128)(2,1)} %refs_1_.3) | copy-start | bytes 1179652
  23.0 11.6 %copy-start.1 = (f32[1536]{0:T(1024)S(1)}, f32[1536]{0:T(1024)}, u32[]{:S(2)}) copy-start(f32[1536]{0:T(1024)} %refs_2_.3) | copy-start | bytes 18436
  23.0 11.6 %collective-permute-start.4 = (bf16[64,1536]{1,0:T(8,128)(2,1)S(1)}, bf16[64,1536]{1,0:T(8,128)(2,1)S(1)}, u32[]{:S(2)}, u32[]{:S(2)}) collective-permute-start(bf16[64,1536]{1,0:T(8,128)(2,1)S(1)} %get-tuple-element.46.token_ref), channel_id=1, source_target_pairs={{0,2},{1,3},{2,0},{3,1},{4,6},{5,7},{6,4},{7,5},{8,10},{9,11},{10,... | collective-permute-start | bytes 589832 | tf_op jit(solution)/shard_map/ppermute | solution.py:26
  35.4 8.4 %copy-start.2 = (s32[128,2]{0,1:T(2,128)S(1)}, s32[128,2]{0,1:T(2,128)}, u32[]{:S(2)}) copy-start(s32[128,2]{0,1:T(2,128)} %param.19) | copy-start | bytes 3076
  35.4 8.4 %copy-start.3 = (f32[128,2]{0,1:T(2,128)S(1)}, f32[128,2]{0,1:T(2,128)}, u32[]{:S(2)}) copy-start(f32[128,2]{0,1:T(2,128)} %param.20) | copy-start | bytes 3076
  35.4 6.5 %collective-permute-start.7 = (bf16[64,1664]{1,0:T(8,128)(2,1)S(1)}, bf16[64,1664]{1,0:T(8,128)(2,1)S(1)}, u32[]{:S(2)}, u32[]{:S(2)}) collective-permute-start(bf16[64,1664]{1,0:T(8,128)(2,1)S(1)} %get-tuple-element.49.token_ref.refs_0_), channel_id=1, source_target_pairs={{0,1},{1,0},{2,3},{3,2},{4,5},{5,4},{6,7},{7,6},{8,9},{9,8},{10,11... | collective-permute-start | bytes 638984 | tf_op jit(solution)/shard_map/ppermute | solution.py:26
  37.0 7.4 %collective-permute-start.5 = (bf16[64,1664]{1,0:T(8,128)(2,1)S(1)}, bf16[64,1664]{1,0:T(8,128)(2,1)S(1)}, u32[]{:S(2)}, u32[]{:S(2)}) collective-permute-start(bf16[64,1664]{1,0:T(8,128)(2,1)S(1)} %get-tuple-element.49.token_ref.refs_0_), channel_id=1, source_target_pairs={{0,8},{4,12},{8,0},{12,4},{1,9},{5,13},{9,1},{13,5},{2,10},{6,14},... | collective-permute-start | bytes 638984 | tf_op jit(solution)/shard_map/ppermute | solution.py:26
  41.9 5.9 %collective-permute-start.8 = (bf16[64,1664]{1,0:T(8,128)(2,1)S(1)}, bf16[64,1664]{1,0:T(8,128)(2,1)S(1)}, u32[]{:S(2)}, u32[]{:S(2)}) collective-permute-start(bf16[64,1664]{1,0:T(8,128)(2,1)S(1)} %passed_on.1.refs_1_), channel_id=1, source_target_pairs={{0,8},{4,12},{8,0},{12,4},{1,9},{5,13},{9,1},{13,5},{2,10},{6,14},... | collective-permute-start | bytes 638984 | tf_op jit(solution)/shard_map/ppermute | solution.py:26
  43.3 5.2 %collective-permute-start.10 = (bf16[64,1664]{1,0:T(8,128)(2,1)S(1)}, bf16[64,1664]{1,0:T(8,128)(2,1)S(1)}, u32[]{:S(2)}, u32[]{:S(2)}) collective-permute-start(bf16[64,1664]{1,0:T(8,128)(2,1)S(1)} %get-tuple-element.49.token_ref.refs_0_), channel_id=1, source_target_pairs={{0,4},{4,0},{8,12},{12,8},{1,5},{5,1},{9,13},{13,9},{2,6},{6,2},{1... | collective-permute-start | bytes 638984 | tf_op jit(solution)/shard_map/ppermute | solution.py:26
  43.3 5.2 %collective-permute-start.11 = (bf16[64,1664]{1,0:T(8,128)(2,1)S(1)}, bf16[64,1664]{1,0:T(8,128)(2,1)S(1)}, u32[]{:S(2)}, u32[]{:S(2)}) collective-permute-start(bf16[64,1664]{1,0:T(8,128)(2,1)S(1)} %passed_on.1.refs_1_), channel_id=1, source_target_pairs={{0,4},{4,0},{8,12},{12,8},{1,5},{5,1},{9,13},{13,9},{2,6},{6,2},{1... | collective-permute-start | bytes 638984 | tf_op jit(solution)/shard_map/ppermute | solution.py:26
  44.4 12.6 %collective-permute-start.6 = (bf16[64,1664]{1,0:T(8,128)(2,1)S(1)}, bf16[64,1664]{1,0:T(8,128)(2,1)S(1)}, u32[]{:S(2)}, u32[]{:S(2)}) collective-permute-start(bf16[64,1664]{1,0:T(8,128)(2,1)S(1)} %collective-permute-done.5.refs_0_), channel_id=1, source_target_pairs={{0,4},{4,0},{8,12},{12,8},{1,5},{5,1},{9,13},{13,9},{2,6},{6,2},{1... | collective-permute-start | bytes 638984 | tf_op jit(solution)/shard_map/ppermute | solution.py:26
  47.9 9.1 %collective-permute-start.9 = (bf16[64,1664]{1,0:T(8,128)(2,1)S(1)}, bf16[64,1664]{1,0:T(8,128)(2,1)S(1)}, u32[]{:S(2)}, u32[]{:S(2)}) collective-permute-start(bf16[64,1664]{1,0:T(8,128)(2,1)S(1)} %collective-permute-done.8.refs_1_), channel_id=1, source_target_pairs={{0,4},{4,0},{8,12},{12,8},{1,5},{5,1},{9,13},{13,9},{2,6},{6,2},{1... | collective-permute-start | bytes 638984 | tf_op jit(solution)/shard_map/ppermute | solution.py:26
  61.9 1.8 %collective-permute-start.13 = (bf16[128,1536]{1,0:T(8,128)(2,1)S(1)}, bf16[128,1536]{1,0:T(8,128)(2,1)S(1)}, u32[]{:S(2)}, u32[]{:S(2)}) collective-permute-start(bf16[128,1536]{1,0:T(8,128)(2,1)S(1)} %get-tuple-element.72), channel_id=1, source_target_pairs={{0,4},{4,0},{8,12},{12,8},{1,5},{5,1},{9,13},{13,9},{2,6},{6,2},{1... | collective-permute-start | bytes 1179656 | tf_op jit(solution)/shard_map/ppermute | solution.py:26
  62.0 5.3 %collective-permute-start.12 = (bf16[128,1536]{1,0:T(8,128)(2,1)S(1)}, bf16[128,1536]{1,0:T(8,128)(2,1)S(1)}, u32[]{:S(2)}, u32[]{:S(2)}) collective-permute-start(bf16[128,1536]{1,0:T(8,128)(2,1)S(1)} %get-tuple-element.71), channel_id=1, source_target_pairs={{0,4},{4,0},{8,12},{12,8},{1,5},{5,1},{9,13},{13,9},{2,6},{6,2},{1... | collective-permute-start | bytes 1179656 | tf_op jit(solution)/shard_map/ppermute | solution.py:26
  65.2 7.8 %collective-permute-start.15 = (bf16[64,1536]{1,0:T(8,128)(2,1)S(1)}, bf16[64,1536]{1,0:T(8,128)(2,1)S(1)}, u32[]{:S(2)}, u32[]{:S(2)}) collective-permute-start(bf16[64,1536]{1,0:T(8,128)(2,1)S(1)} %get-tuple-element.74.token_ref), channel_id=1, source_target_pairs={{0,8},{4,12},{8,0},{12,4},{1,9},{5,13},{9,1},{13,5},{2,10},{6,14},... | collective-permute-start | bytes 589832 | tf_op jit(solution)/shard_map/ppermute | solution.py:26
  66.1 10.3 %collective-permute-start.14 = (bf16[64,1536]{1,0:T(8,128)(2,1)S(1)}, bf16[64,1536]{1,0:T(8,128)(2,1)S(1)}, u32[]{:S(2)}, u32[]{:S(2)}) collective-permute-start(bf16[64,1536]{1,0:T(8,128)(2,1)S(1)} %get-tuple-element.76), channel_id=1, source_target_pairs={{0,8},{4,12},{8,0},{12,4},{1,9},{5,13},{9,1},{13,5},{2,10},{6,14},... | collective-permute-start | bytes 589832 | tf_op jit(solution)/shard_map/ppermute | solution.py:26
  73.1 5.7 %collective-permute-start.16 = (bf16[64,1536]{1,0:T(8,128)(2,1)S(1)}, bf16[64,1536]{1,0:T(8,128)(2,1)S(1)}, u32[]{:S(2)}, u32[]{:S(2)}) collective-permute-start(bf16[64,1536]{1,0:T(8,128)(2,1)S(1)} %add_convert_fusion), channel_id=1, source_target_pairs={{0,1},{1,0},{2,3},{3,2},{4,5},{5,4},{6,7},{7,6},{8,9},{9,8},{10,11... | collective-permute-start | bytes 589832 | tf_op jit(solution)/shard_map/ppermute | solution.py:26
  78.9 7.1 %collective-permute-start.17 = (bf16[32,1536]{1,0:T(8,128)(2,1)S(1)}, bf16[32,1536]{1,0:T(8,128)(2,1)S(1)}, u32[]{:S(2)}, u32[]{:S(2)}) collective-permute-start(bf16[32,1536]{1,0:T(8,128)(2,1)S(1)} %slice.15), channel_id=1, source_target_pairs={{0,2},{1,3},{2,0},{3,1},{4,6},{5,7},{6,4},{7,5},{8,10},{9,11},{10,... | collective-permute-start | bytes 294920 | tf_op jit(solution)/shard_map/ppermute | solution.py:26

commit v3 on v2

--- a/solution.py
+++ b/solution.py
@@ -58,7 +58,7 @@
 
 
 def attend_kernel(kv, group, batch, _, len_hbm, q_hbm, new_hbm, cache_hbm, w_hbm, *refs):
-    out_ref, w_ref, len_ref, q_ref, new_ref, cache, q_scr, sem, w_sem, small_sem = refs
+    out_ref, w_ref, len_ref, q_ref, new_ref, cache, q_scr, new_scr, sem, w_sem, small_sem = refs
     rows, slots = cache.shape[0], cache.shape[1]
     small = [
         pltpu.make_async_copy(a, b, small_sem.at[i])
@@ -77,40 +77,39 @@
         for g in range(group):
             lo = (h * group + g) * HEAD_SIZE
             q_scr[h, :, g, :] = q_ref[:, lo : lo + HEAD_SIZE].astype(f32)
-    pos = lax.broadcasted_iota(jnp.int32, (1, 8, slots), 2)
-    new = new_ref[...].astype(f32)
-    for i, p in enumerate(parts):
-        base = i * batch
-        valid = jnp.concatenate([pos < len_ref[base + b] for b in range(batch)], axis=0)
-        loads[i].wait()
+    new_scr[...] = new_ref[...].astype(f32)
+    lane = lax.broadcasted_iota(jnp.int32, (HEAD_SIZE, HEAD_SIZE), 1)
+    row = lax.broadcasted_iota(jnp.int32, (slots + 16, HEAD_SIZE), 0)
+
+    @pl.loop(0, len(parts))
+    def _(i):
+        base = pl.multiple_of(i * batch, batch)
+        p = pl.ds(base, batch)
+        length = jnp.zeros((1, HEAD_SIZE), jnp.int32)
+        for b in range(batch):
+            length = jnp.where(lane[:1] // 8 == b, len_ref[base + b], length)
+        valid = (row < length) | (row == slots)
+        new = new_scr[p, :]
+        pltpu.make_async_copy(cache_hbm.at[p], cache.at[p], sem.at[i]).wait()
         for h in range(kv):
             lo = 2 * h * HEAD_SIZE
-
-            def spread(col):
-                return jnp.concatenate(
-                    [
-                        jnp.broadcast_to(new[base + b : base + b + 1, col : col + HEAD_SIZE][None], (1, 8, HEAD_SIZE))
-                        for b in range(batch)
-                    ],
-                    axis=0,
+            hi = lo + HEAD_SIZE
+            q = q_scr[h, p].reshape(batch * 8, HEAD_SIZE).T.astype(bf16)
+            wide = jnp.concatenate([jnp.where(lane // 8 == b, q, jnp.zeros_like(q)) for b in range(batch)], axis=0)
+            keys = jnp.concatenate([cache[base + b, :, lo:hi] for b in range(batch)], axis=1)
+            fresh = jnp.concatenate([new[b : b + 1, lo:hi] for b in range(batch)], axis=1)
+            fresh = jnp.broadcast_to(fresh, (16, batch * HEAD_SIZE)).astype(bf16)
+            s = jnp.dot(jnp.concatenate([keys, fresh], axis=0), wide, preferred_element_type=f32)
+            s = jnp.where(valid, s * scale, -jnp.inf)
+            e = jnp.exp(s - jnp.max(s, axis=0, keepdims=True))
+            probs = (e * (1.0 / jnp.sum(e, axis=0, keepdims=True))).T
+            for b in range(batch):
+                new_v = jnp.broadcast_to(new[b : b + 1, hi : hi + HEAD_SIZE], (16, HEAD_SIZE)).astype(bf16)
+                vals = jnp.concatenate([cache[base + b, :, hi : hi + HEAD_SIZE], new_v], axis=0)
+                q_scr[h, base + b] = jnp.dot(
+                    probs[b * 8 : b * 8 + 8].astype(bf16), vals, preferred_element_type=f32
                 )
 
-            q = q_scr[h, p]
-            keys = cache[p, :, lo : lo + HEAD_SIZE]
-            vals = cache[p, :, lo + HEAD_SIZE : lo + 2 * HEAD_SIZE]
-            s = lax.dot_general(
-                q.astype(bf16), keys, (((2,), (2,)), ((0,), (0,))), preferred_element_type=f32
-            )
-            s = jnp.where(valid, s * scale, -jnp.inf)
-            s_new = jnp.sum(q * spread(lo), axis=2, keepdims=True) * scale
-            top = jnp.maximum(jnp.max(s, axis=2, keepdims=True), s_new)
-            e = jnp.exp(s - top)
-            e_new = jnp.exp(s_new - top)
-            inv = 1.0 / (jnp.sum(e, axis=2, keepdims=True) + e_new)
-            probs = (e * inv).astype(bf16)
-            p_new = (e_new * inv).astype(bf16).astype(f32)
-            ctx = lax.dot_general(probs, vals, (((2,), (1,)), ((0,), (0,))), preferred_element_type=f32)
-            q_scr[h, p] = ctx + p_new * spread(lo + HEAD_SIZE)
     for h in range(kv):
         for g in range(group):
             lo = (h * group + g) * HEAD_SIZE
@@ -122,7 +121,7 @@
     rows, slots, width = cache.shape
     kv = width // (2 * HEAD_SIZE)
     group = QUERY_HEADS // KEY_VALUE_HEADS
-    batch = 8
+    batch = HEAD_SIZE // 8
     return pl.pallas_call(
         functools.partial(attend_kernel, kv, group, batch),
         out_shape=[jax.ShapeDtypeStruct(query.shape, bf16), VM(out_proj.shape, bf16)],
@@ -134,6 +133,7 @@
             VM(key_value_new.shape, bf16),
             VM(cache.shape, bf16),
             VM((kv, rows, 8, HEAD_SIZE), f32),
+            VM(key_value_new.shape, f32),
             pltpu.SemaphoreType.DMA((rows // batch,)),
             pltpu.SemaphoreType.DMA,
             pltpu.SemaphoreType.DMA((3,)),
@@ -205,36 +205,37 @@
     )(place, *ctx, out_proj)
 
 
-def sum_kernel(own_ref, got_ref, token_ref, sum_ref, pass_ref):
+def sum_kernel(own_ref, got_ref, *refs):
+    sum_ref, pass_ref = refs[-2:]
     total = own_ref[...] + got_ref[...].astype(f32)
     sum_ref[...] = total
     pass_ref[...] = total.astype(bf16)
 
 
-def pass_kernel(x_ref, token_ref, out_ref):
-    out_ref[...] = x_ref[...]
-
-
-def passed_on(x, token):
+def pass_kernel(x_ref, *refs):
+    refs[-1][...] = x_ref[...]
+
+
+def passed_on(x, *tokens):
     return pl.pallas_call(
         pass_kernel,
         out_shape=jax.ShapeDtypeStruct(x.shape, x.dtype),
-        in_specs=[VMEM_SPEC] * 2,
+        in_specs=[VMEM_SPEC] * (1 + len(tokens)),
         out_specs=VMEM_SPEC,
         compiler_params=pltpu.CompilerParams(vmem_limit_bytes=2 * MIB),
         name="passed_on",
-    )(x, token)
-
-
-def add_up(own, got, token):
+    )(x, *tokens)
+
+
+def add_up(own, got, *tokens):
     return pl.pallas_call(
         sum_kernel,
         out_shape=[jax.ShapeDtypeStruct(own.shape, f32), jax.ShapeDtypeStruct(own.shape, bf16)],
-        in_specs=[VMEM_SPEC] * 3,
+        in_specs=[VMEM_SPEC] * (2 + len(tokens)),
         out_specs=[VMEM_SPEC] * 2,
         compiler_params=pltpu.CompilerParams(vmem_limit_bytes=4 * MIB),
         name="pair_sum",
-    )(own, got, token)
+    )(own, got, *tokens)
 
 
 def stream_kernel(keep, arrived, place_ref, sum_ref, *refs):
@@ -310,79 +311,112 @@
     return jnp.concatenate(sq, axis=0)
 
 
-def grow_kernel(first, odd, model, row_ks, ks, place_ref, *refs):
-    last = odd is not None
+def products(x_refs, gates, ups, cols):
+    g = sum(jnp.dot(x[...], w[:, cols], preferred_element_type=f32) for x, w in zip(x_refs, gates))
+    u = sum(jnp.dot(x[...], w[:, cols], preferred_element_type=f32) for x, w in zip(x_refs, ups))
+    return g, u
+
+
+def halves_of(hidden, work):
+    @pl.loop(0, 2)
+    def _(c):
+        work(pl.ds(pl.multiple_of(c * (hidden // 2), 128), hidden // 2))
+
+
+def grow_kernel(first, row_ks, ks, place_ref, *refs):
+    r, m = len(row_ks), len(ks)
     (a_ref, b_ref, gate, up), refs = refs[:4], refs[4:]
     if not first:
         (in_g, in_u, in_sq), refs = refs[:3], refs[3:]
-    if last:
-        weight, ready, refs = refs[0], refs[1 : 1 + len(odd)], refs[1 + len(odd) :]
-    n = len(row_ks)
-    mats, wd, refs = refs[:n], refs[n], refs[n + 1 :]
-    if last:
-        outs, h_ref, refs = refs[: len(odd)], refs[len(odd)], refs[len(odd) + 1 :]
-    else:
-        (acc_g, acc_u, sq_ref), refs = refs[:3], refs[3:]
-    rows_loaded, loaded, (x_ref, row_sem, sem) = refs[:n], refs[n : n + len(ks)], refs[n + len(ks) :]
-    loads = row_loads(place_ref, mats, row_ks, rows_loaded, row_sem) + col_loads(place_ref, wd, ks, loaded, sem)
+    mats, wd, (acc_g, acc_u, sq_ref), refs = refs[:r], refs[r], refs[r + 1 : r + 4], refs[r + 4 :]
+    row_loaded, loaded, (x_ref, row_sem, sem) = refs[:r], refs[r : r + m], refs[r + m :]
+    loads = row_loads(place_ref, mats, row_ks, row_loaded, row_sem) + col_loads(place_ref, wd, ks, loaded, sem)
     all_of(loads, "start")
     sq = join(x_ref, (a_ref, b_ref), x_ref.shape[1])
-    if not first:
-        sq = sq + in_sq[...]
-
-    def columns(cols):
-        g = jnp.dot(x_ref[...], gate[:, cols], preferred_element_type=f32)
-        u = jnp.dot(x_ref[...], up[:, cols], preferred_element_type=f32)
-        if not first:
-            g, u = g + in_g[:, cols], u + in_u[:, cols]
-        if last:
-            scale = lax.rsqrt(sq / model + EPS)
-            g, u = g * scale, u * (scale * weight[...])
-            h_ref[:, cols] = (g / (1.0 + jnp.exp(-g)) * u).astype(bf16)
-        else:
-            acc_g[:, cols], acc_u[:, cols] = g, u
-
-    hidden = gate.shape[1]
-    if loads:
-
-        @pl.loop(0, 2)
-        def _(c):
-            columns(pl.ds(pl.multiple_of(c * (hidden // 2), 128), hidden // 2))
-    else:
-        step = min(512, hidden)
-        for lo in range(0, hidden, step):
-            columns(slice(lo, lo + step))
-    if last:
-        for i in range(len(odd)):
-            outs[i][...] = jnp.dot(h_ref[...], ready[i][...], preferred_element_type=f32).astype(bf16)
-    else:
-        sq_ref[...] = sq
+    sq_ref[...] = sq if first else sq + in_sq[...]
+
+    def work(cols):
+        g, u = products([x_ref], [gate], [up], cols)
+        acc_g[:, cols] = g if first else g + in_g[:, cols]
+        acc_u[:, cols] = u if first else u + in_u[:, cols]
+
+    halves_of(acc_g.shape[1], work)
     all_of(loads, "wait")
 
 
-def grow(place, parts, gate, up, acc, ahead, down, ks, model, last):
+def grow(place, parts, gate, up, acc, ahead, down, ks):
     rows = parts[0].shape[0] + parts[1].shape[0]
     width, hidden = gate.shape
+    r, m = len(ahead), len(ks)
     args = [*parts, gate, up] + (list(acc) if acc is not None else [])
-    odd = None
-    if last is not None:
-        weight, odd, ready = last
-        args += [weight, *ready]
-        outs = [jax.ShapeDtypeStruct((rows, width), bf16) for _ in odd] + [jax.ShapeDtypeStruct((rows, hidden), bf16)]
-    else:
-        outs = [jax.ShapeDtypeStruct((rows, n), f32) for n in (hidden, hidden, 1)]
-    own = len(outs)
     res = pl.pallas_call(
-        functools.partial(grow_kernel, acc is None, odd, model, [k for _, k in ahead], ks),
-        out_shape=outs + [VM((width, hidden), bf16) for _ in ahead] + [VM((hidden, width), bf16) for _ in ks],
-        in_specs=[SMEM_SPEC] + [VMEM_SPEC] * len(args) + [HBM_SPEC] * (len(ahead) + 1),
-        out_specs=[VMEM_SPEC] * (own + len(ahead) + len(ks)),
-        scratch_shapes=[VM((rows, width), bf16), pltpu.SemaphoreType.DMA((max(1, len(ahead)),)), pltpu.SemaphoreType.DMA((max(1, len(ks)),))],
+        functools.partial(grow_kernel, acc is None, [k for _, k in ahead], ks),
+        out_shape=[jax.ShapeDtypeStruct((rows, c), f32) for c in (hidden, hidden, 1)]
+        + [VM((width, hidden), bf16) for _ in ahead]
+        + [VM((hidden, width), bf16) for _ in ks],
+        in_specs=[SMEM_SPEC] + [VMEM_SPEC] * len(args) + [HBM_SPEC] * (r + 1),
+        out_specs=[VMEM_SPEC] * (3 + r + m),
+        scratch_shapes=[
+            VM((rows, width), bf16),
+            pltpu.SemaphoreType.DMA((max(1, r),)),
+            pltpu.SemaphoreType.DMA((max(1, m),)),
+        ],
         compiler_params=pltpu.CompilerParams(vmem_limit_bytes=4 * MIB),
         cost_estimate=cost(4 * width * hidden, 4 * rows * width * hidden),
-        name="experts_last" if last is not None else "experts",
+        name="experts",
     )(place, *args, *[hbm(m) for m, _ in ahead], hbm(down))
-    return res[:own], res[own : own + len(ahead)], res[own + len(ahead) :]
+    return res[:3], res[3 : 3 + r], res[3 + r :]
+
+
+def last_kernel(n, a, late, even, model, place_ref, *refs):
+    parts, gates, ups, refs = refs[: 2 * n], refs[2 * n : 3 * n], refs[3 * n : 4 * n], refs[4 * n :]
+    (in_g, in_u, in_sq, weight), downs, wd, refs = refs[:4], refs[4 : 3 + a], refs[3 + a], refs[4 + a :]
+    b = len(even)
+    outs, h_ref, loaded, (x_ref, down, sem, late_sem) = refs[:a], refs[a], refs[a + 1 : a + 1 + b], refs[a + 1 + b :]
+    late_load = col_loads(place_ref, wd, [late], [down], late_sem)
+    loads = col_loads(place_ref, wd, even, loaded, sem)
+    all_of(late_load + loads, "start")
+    xs = [x_ref.at[i] for i in range(n)]
+    sq = in_sq[...] + sum(join(xs[i], parts[2 * i : 2 * i + 2], x_ref.shape[2]) for i in range(n))
+    scale = lax.rsqrt(sq / model + EPS)
+    up_scale = scale * weight[...]
+
+    def work(cols):
+        g, u = products(xs, gates, ups, cols)
+        g = (g + in_g[:, cols]) * scale
+        u = (u + in_u[:, cols]) * up_scale
+        h_ref[:, cols] = (g / (1.0 + jnp.exp(-g)) * u).astype(bf16)
+
+    halves_of(h_ref.shape[1], work)
+    for i, w in enumerate([*downs, down]):
+        if w is down:
+            all_of(late_load, "wait")
+        outs[i][...] = jnp.dot(h_ref[...], w[...], preferred_element_type=f32).astype(bf16)
+    all_of(loads, "wait")
+
+
+def last_blocks(place, parts, gates, ups, acc, weight, downs, down, late, even):
+    n, a = len(gates), len(downs) + 1
+    rows = parts[0].shape[0] + parts[1].shape[0]
+    width, hidden = gates[0].shape
+    res = pl.pallas_call(
+        functools.partial(last_kernel, n, a, late, even, down.shape[1]),
+        out_shape=[jax.ShapeDtypeStruct((rows, width), bf16) for _ in range(a)]
+        + [jax.ShapeDtypeStruct((rows, hidden), bf16)]
+        + [VM((hidden, width), bf16) for _ in even],
+        in_specs=[SMEM_SPEC] + [VMEM_SPEC] * (4 * n + 3 + a) + [HBM_SPEC],
+        out_specs=[VMEM_SPEC] * (a + 1 + len(even)),
+        scratch_shapes=[
+            VM((n, rows, width), bf16),
+            VM((hidden, width), bf16),
+            pltpu.SemaphoreType.DMA((len(even),)),
+            pltpu.SemaphoreType.DMA((1,)),
+        ],
+        compiler_params=pltpu.CompilerParams(vmem_limit_bytes=10 * MIB),
+        cost_estimate=cost(4 * n * width * hidden, 4 * n * rows * width * hidden),
+        name="experts_last",
+    )(place, *parts, *gates, *ups, *acc, weight, *downs, hbm(down))
+    return res[:a], res[a], res[a + 1 :]
 
 
 def back_kernel(n, place_ref, h_ref, *refs):
@@ -472,41 +506,33 @@
     kept, parted = project(place, ctx, proj_weight, total, keep, sent)
     got = swap(parted, "tp", 1)
     (gate0,), token = fetch(place, parted, [(w_gate, 0)], width)
-    sums, passed = add_up(kept, got, token)
+    weight = request_weights(place, routes.T, route_weight.T, token, n_dp // EXPERTS, keep + sent)
+    sums, passed = add_up(kept, got, token, weight)
     got = [swap(passed, "tp", k) for k in keep[1:]]
-    (up0, gate1, up1, gate2), token = fetch(
-        place, passed, [(w_up, 0), (w_gate, 1), (w_up, 1), (w_gate, 2)], width
+    (up0, gate1, up1, *gates), token = fetch(
+        place, passed, [(w_up, 0), (w_gate, 1), (w_up, 1)] + [(w_gate, k) for k in even], width
     )
     attended, near = stream(place, sums, got, keep[1:], residual, norm_gain, token, keep)
-    weight = request_weights(place, routes.T, route_weight.T, near, n_dp // EXPERTS, keep + sent)
 
     other = swap(near, "tp", 1)
     far_near = [swap(near, "dp", k) for k in even]
-    (up2,), token = fetch(place, near, [(w_up, 2)], width)
+    ups, token = fetch(place, near, [(w_up, k) for k in even], width)
     other = passed_on(other, token)
     core_near = swap(near, "dp", 1)
     far_other = [swap(other, "dp", k) for k in even]
     core_other = swap(other, "dp", 1)
-    halves = [(near, other), (core_near, core_other)]
-    for a, b in zip(far_near, far_other):
-        halves += [(a, b), (swap(a, "dp", 1), swap(b, "dp", 1))]
-    gates, ups = [gate0, gate1, gate2], [up0, up1, up2]
-    odd = odd + [1]
-    acc, ready = None, {}
-    for i in range(n_dp):
-        ahead = [(m, k) for m, at in ((w_gate, 0), (w_up, 1)) for k in range(3, n_dp) if i == at]
-        downs = {2: odd, n_dp - 1: even}.get(i, [])
-        last = (weight, odd, [ready[k] for k in odd]) if i == n_dp - 1 else None
-        acc, late, loaded = grow(
-            place, halves[i], gates[i], ups[i], acc, ahead, w_down, downs, w_gate.shape[0], last
-        )
-        for (m, _), v in zip(ahead, late):
-            (gates if m is w_gate else ups).append(v)
-        ready.update(zip(downs, loaded))
-    out_odd, h = acc[:-1], acc[-1]
+    acc, odd_gates, _ = grow(place, (passed_on(near, *far_near), other), gate0, up0, None, [(w_gate, k) for k in odd], w_down, [])
+    acc, odd_ups, _ = grow(place, (core_near, core_other), gate1, up1, acc, [(w_up, k) for k in odd], w_down, [])
+    far_other = [passed_on(x, acc[2]) for x in far_other]
+    last, downs = [], []
+    for i, (a, b) in enumerate(zip(far_near, far_other)):
+        last += [swap(a, "dp", 1), swap(b, "dp", 1)]
+        acc, _, loaded = grow(place, (a, b), gates[i], ups[i], acc, [], w_down, odd if i == 0 else [])
+        downs += loaded
+    out_odd, h, ready = last_blocks(place, last, odd_gates, odd_ups, acc, weight, downs, w_down, 1, even)
 
     crossed = [swap(o, "dp", 1) for o in out_odd]
-    sums = back(place, h, crossed[:-1], [ready[k] for k in even])
+    sums = back(place, h, crossed[:-1], ready)
     there = [swap(s[1], "dp", k) for s, k in zip(sums, even)]
     here = [swap(s[0], "dp", k) for s, k in zip(sums, even)]
     mix_a, mix_b = own_block(place, h, crossed[-1], sums[0][1], w_down, width)

time: 86.9 us -> 82.2 us (0.946)
  Pallas kernels: 47.5 us -> 45.1 us
  waiting for transfers between devices: 15.6 us -> 14.1 us
  starting transfers between devices: 21.2 us -> 20.3 us
    ppermute x18, waiting for transfers between devices: 15.6 us -> 14.1 us  [swap(): return lax.ppermute(x, axis, [(i, i ^ k) for i in range(n)])]
    pallas_call x4, Pallas kernels: 16.8 us -> 15.3 us  [the longest x3 10.1 us: grow(): pl.pallas_call(functools.partial(grow_kernel, acc is None, [k for _, k in...]
    pallas_call x1, Pallas kernels: 6.56 us -> 5.61 us  [attend(): pl.pallas_call(functools.partial(attend_kernel, kv, group, batch), out_sh...]
where the time goes in v3:
time: 82.2 us; the launch traced here: 81.9 us
  Pallas kernels  45.1 us (55%)
  starting transfers between devices  20.3 us (25%)
  waiting for transfers between devices  14.1 us (17%)
  between operations  0.94 us (1%)
    ppermute x18, starting transfers between devices, swap(): return lax.ppermute(x, axis, [(i, i ^ k) for i in range(n)])  20.3 us
    pallas_call x3, Pallas kernels, fetch(): pl.pallas_call(functools.partial(fetch_kernel, ks), out_shape=[VM((width,...  15.4 us
    ppermute x18, waiting for transfers between devices, swap(): return lax.ppermute(x, axis, [(i, i ^ k) for i in range(n)])  14.1 us
    pallas_call x3, Pallas kernels, grow(): pl.pallas_call(functools.partial(grow_kernel, acc is None, [k for _, k in...  10.1 us
    pallas_call x1, Pallas kernels, attend(): pl.pallas_call(functools.partial(attend_kernel, kv, group, batch), out_sh...  5.61 us
    pallas_call x1, Pallas kernels, last_blocks(): pl.pallas_call(functools.partial(last_kernel, n, a, late, even, down.shap...  5.19 us
    pallas_call x1, Pallas kernels, own_block(): pl.pallas_call(own_kernel, out_shape=[jax.ShapeDtypeStruct((rows // 2, wi...  4.36 us
  transfers between devices with their start and end apart: 18, of which 8 were waited for; matrix products, arithmetic and copies ran while one was open for 1% of the time, Pallas kernels for 39%

profile of v3, /device:TPU:0, one launch (start us, length us, event | category | flops | bytes accessed | tf_op | source)
XLA Modules:
  0.0 81.9 jit_solution(15293502655344770611)
XLA Ops:
  0.6 0.1 pad_add_fusion._.place_ref
  0.7 5.6 %attention.1 = (bf16[32,1536]{1,0:T(8,128)(2,1)S(1)}, bf16[1536,1536]{1,0:T(8,128)(2,1)S(1)}) custom-call(s32[2]{0:T(128)S(1)} %pad_add_fusion._.place_ref, s32[32]{0:T(128)} %len_hbm.1, bf16[32,1536]{1,0:T(8,128)(2,1)} %q_hbm.1, bf16[32,512]{1,0:T(8,128)(2,1)} %new_hbm.1, bf16[32,160,512]{2,1,0:T(8,128)(2,1)} %cache_hbm.1, bf16[1536,1536]{1,0:T(8,128)(2,1)} %w_hbm.1), custom_call_target="tpu_custom_call" | custom-call | flops 62914560 | bytes 10485760 | tf_op jit(solution)/shard_map/attention/pallas_call | solution.py:125
  6.3 3.0 %collective-permute-start.1 = (bf16[32,1536]{1,0:T(8,128)(2,1)S(1)}, bf16[32,1536]{1,0:T(8,128)(2,1)S(1)}, u32[]{:S(2)}, u32[]{:S(2)}) collective-permute-start(bf16[32,1536]{1,0:T(8,128)(2,1)S(1)} %get-tuple-element.39.refs_0_), channel_id=1, source_target_pairs={{0,8},{4,12},{8,0},{12,4},{1,9},{5,13},{9,1},{13,5},{2,10},{6,14},... | collective-permute-start | bytes 294920 | tf_op jit(solution)/shard_map/ppermute | solution.py:26
  9.4 0.0 collective-permute-start
  9.4 2.8 %collective-permute-done.1.refs_2_ = bf16[32,1536]{1,0:T(8,128)(2,1)S(1)} collective-permute-done((bf16[32,1536]{1,0:T(8,128)(2,1)S(1)}, bf16[32,1536]{1,0:T(8,128)(2,1)S(1)}, u32[]{:S(2)}, u32[]{:S(2)}) %collective-permute-start.1) | collective-permute-done | bytes 98336 | tf_op jit(solution)/shard_map/ppermute | solution.py:26
  12.2 0.0 collective-permute-start.2
  12.2 0.0 collective-permute-done.refs_1_
  12.2 1.3 %collective-permute-done.2.refs_3_ = bf16[32,1536]{1,0:T(8,128)(2,1)S(1)} collective-permute-done((bf16[32,1536]{1,0:T(8,128)(2,1)S(1)}, bf16[32,1536]{1,0:T(8,128)(2,1)S(1)}, u32[]{:S(2)}, u32[]{:S(2)}) %collective-permute-start.2) | collective-permute-done | bytes 98336 | tf_op jit(solution)/shard_map/ppermute | solution.py:26
  13.5 1.4 %projection.1 = (f32[64,1536]{1,0:T(8,128)S(1)}, bf16[64,1536]{1,0:T(8,128)(2,1)S(1)}) custom-call(s32[2]{0:T(128)S(1)} %pad_add_fusion._.place_ref, bf16[32,1536]{1,0:T(8,128)(2,1)S(1)} %get-tuple-element.39.refs_0_, bf16[32,1536]{1,0:T(8,128)(2,1)S(1)} %collective-permute-done.refs_1_, bf16[32,1536]{1,0:T(8,128)(2,1)S(1)} %collective-permute-done.1.refs_2_, ...), custom_call_target="tpu_custom_call" | custom-call | flops 603979776 | bytes 4718592 | tf_op jit(solution)/shard_map/projection/pallas_call | solution.py:193
  14.8 0.0 copy-start.3
  14.9 0.0 copy-start.4
  14.9 1.9 %collective-permute-start.3 = (bf16[64,1536]{1,0:T(8,128)(2,1)S(1)}, bf16[64,1536]{1,0:T(8,128)(2,1)S(1)}, u32[]{:S(2)}, u32[]{:S(2)}) collective-permute-start(bf16[64,1536]{1,0:T(8,128)(2,1)S(1)} %get-tuple-element.42.token_ref), channel_id=1, source_target_pairs={{0,1},{1,0},{2,3},{3,2},{4,5},{5,4},{6,7},{7,6},{8,9},{9,8},{10,11... | collective-permute-start | bytes 589832 | tf_op jit(solution)/shard_map/ppermute | solution.py:26
  16.8 3.3 %fetch.3 = (bf16[1536,2048]{1,0:T(8,128)(2,1)S(1)}, bf16[8,128]{1,0:T(8,128)(2,1)S(1)}) custom-call(s32[2]{0:T(128)S(1)} %pad_add_fusion._.place_ref, bf16[64,1536]{1,0:T(8,128)(2,1)S(1)} %get-tuple-element.42.token_ref, bf16[6144,2048]{1,0:T(8,128)(2,1)} %refs_4_.1), custom_call_target="tpu_custom_call" | custom-call | bytes 6291456 | tf_op jit(solution)/shard_map/fetch/pallas_call | solution.py:159
  20.2 0.0 copy-done.3
  20.2 0.0 copy-done.4
  20.2 0.6 request_weights.1.refs_1_.refs_7_
  20.8 1.2 %collective-permute-done.3.got_ref = bf16[64,1536]{1,0:T(8,128)(2,1)S(1)} collective-permute-done((bf16[64,1536]{1,0:T(8,128)(2,1)S(1)}, bf16[64,1536]{1,0:T(8,128)(2,1)S(1)}, u32[]{:S(2)}, u32[]{:S(2)}) %collective-permute-start.3) | collective-permute-done | bytes 196640 | tf_op jit(solution)/shard_map/ppermute | solution.py:26
  22.0 0.1 pair_sum.1
  22.1 0.0 copy-start.1
  22.1 0.0 copy-start.2
  22.1 2.8 %collective-permute-start.4 = (bf16[64,1536]{1,0:T(8,128)(2,1)S(1)}, bf16[64,1536]{1,0:T(8,128)(2,1)S(1)}, u32[]{:S(2)}, u32[]{:S(2)}) collective-permute-start(bf16[64,1536]{1,0:T(8,128)(2,1)S(1)} %get-tuple-element.45.token_ref), channel_id=1, source_target_pairs={{0,2},{1,3},{2,0},{3,1},{4,6},{5,7},{6,4},{7,5},{8,10},{9,11},{10,... | collective-permute-start | bytes 589832 | tf_op jit(solution)/shard_map/ppermute | solution.py:26
  24.9 8.8 %fetch.4 = (bf16[1536,2048]{1,0:T(8,128)(2,1)S(1)}, bf16[1536,2048]{1,0:T(8,128)(2,1)S(1)}, bf16[1536,2048]{1,0:T(8,128)(2,1)S(1)}, bf16[1536,2048]{1,0:T(8,128)(2,1)S(1)}, bf16[8,128]{1,0:T(8,128)(2,1)S(1)}) custom-call(s32[2]{0:T(128)S(1)} %pad_add_fusion._.place_ref, bf16[64,1536]{1,0:T(8,128)(2,1)S(1)} %get-tuple-element.45.token_ref, ...), custom_call_target="tpu_custom_call" | custom-call | bytes 25165824 | tf_op jit(solution)/shard_map/fetch/pallas_call | solution.py:159
  33.7 0.0 copy-start
  33.7 0.0 collective-permute-done.4.refs_0_
  33.7 0.7 residual_stream.1
  34.5 1.6 %collective-permute-start.7 = (bf16[64,1664]{1,0:T(8,128)(2,1)S(1)}, bf16[64,1664]{1,0:T(8,128)(2,1)S(1)}, u32[]{:S(2)}, u32[]{:S(2)}) collective-permute-start(bf16[64,1664]{1,0:T(8,128)(2,1)S(1)} %get-tuple-element.48.token_ref.x_ref), channel_id=1, source_target_pairs={{0,1},{1,0},{2,3},{3,2},{4,5},{5,4},{6,7},{7,6},{8,9},{9,8},{10,11... | collective-permute-start | bytes 638984 | tf_op jit(solution)/shard_map/ppermute | solution.py:26
  36.1 1.5 %collective-permute-start.5 = (bf16[64,1664]{1,0:T(8,128)(2,1)S(1)}, bf16[64,1664]{1,0:T(8,128)(2,1)S(1)}, u32[]{:S(2)}, u32[]{:S(2)}) collective-permute-start(bf16[64,1664]{1,0:T(8,128)(2,1)S(1)} %get-tuple-element.48.token_ref.x_ref), channel_id=1, source_target_pairs={{0,8},{4,12},{8,0},{12,4},{1,9},{5,13},{9,1},{13,5},{2,10},{6,14},... | collective-permute-start | bytes 638984 | tf_op jit(solution)/shard_map/ppermute | solution.py:26
  37.6 3.3 %fetch.5 = (bf16[1536,2048]{1,0:T(8,128)(2,1)S(1)}, bf16[8,128]{1,0:T(8,128)(2,1)S(1)}) custom-call(s32[2]{0:T(128)S(1)} %pad_add_fusion._.place_ref, bf16[64,1664]{1,0:T(8,128)(2,1)S(1)} %get-tuple-element.48.token_ref.x_ref, bf16[6144,2048]{1,0:T(8,128)(2,1)} %refs_7_.2), custom_call_target="tpu_custom_call" | custom-call | bytes 6291456 | tf_op jit(solution)/shard_map/fetch/pallas_call | solution.py:159
  41.0 0.1 collective-permute-start.9
  41.0 0.0 collective-permute-done.7.x_ref
  41.1 0.0 slice-start
  41.1 0.5 collective-permute-start.10
  41.6 0.8 collective-permute-start.8
  42.4 0.0 collective-permute-done.5.refs_0_
  42.4 0.0 slice-start.1
  42.4 3.4 %experts.3 = (f32[128,2048]{1,0:T(8,128)S(1)}, f32[128,2048]{1,0:T(8,128)S(1)}, f32[128,1]{1,0:T(8,128)S(1)}, bf16[1536,2048]{1,0:T(8,128)(2,1)S(1)}) custom-call(s32[2]{0:T(128)S(1)} %pad_add_fusion._.place_ref, bf16[64,1664]{1,0:T(8,128)(2,1)S(1)} %passed_on.4.refs_0_, bf16[64,1664]{1,0:T(8,128)(2,1)S(1)} %passed_on.3.refs_1_, ...), custom_call_target="tpu_custom_call" | custom-call | flops 1610612736 | bytes 12582912 | tf_op jit(solution)/shard_map/experts/pallas_call | solution.py:352
  45.8 0.4 collective-permute-start.6
  46.3 0.0 collective-permute-done.9.refs_0_
  46.3 0.0 collective-permute-done.10.refs_1_
  46.3 0.0 slice-done
  46.3 3.4 %experts.4 = (f32[128,2048]{1,0:T(8,128)S(1)}, f32[128,2048]{1,0:T(8,128)S(1)}, f32[128,1]{1,0:T(8,128)S(1)}, bf16[1536,2048]{1,0:T(8,128)(2,1)S(1)}) custom-call(s32[2]{0:T(128)S(1)} %pad_add_fusion._.place_ref, bf16[64,1664]{1,0:T(8,128)(2,1)S(1)} %collective-permute-done.9.refs_0_, bf16[64,1664]{1,0:T(8,128)(2,1)S(1)} %collective-permute-done.10.refs_1_, ...), custom_call_target="tpu_custom_call" | custom-call | flops 1610612736 | bytes 12582912 | tf_op jit(solution)/shard_map/experts/pallas_call | solution.py:352
  49.7 0.0 collective-permute-done.8.x_ref
  49.7 0.2 collective-permute-start.11
  49.9 3.3 %experts.5 = (f32[128,2048]{1,0:T(8,128)S(1)}, f32[128,2048]{1,0:T(8,128)S(1)}, f32[128,1]{1,0:T(8,128)S(1)}, bf16[2048,1536]{1,0:T(8,128)(2,1)S(1)}) custom-call(s32[2]{0:T(128)S(1)} %pad_add_fusion._.place_ref, bf16[64,1664]{1,0:T(8,128)(2,1)S(1)} %collective-permute-done.5.refs_0_, bf16[64,1664]{1,0:T(8,128)(2,1)S(1)} %passed_on.5.refs_1_, ...), custom_call_target="tpu_custom_call" | custom-call | flops 1610612736 | bytes 12582912 | tf_op jit(solution)/shard_map/experts/pallas_call | solution.py:352
  53.3 0.0 collective-permute-done.6.refs_0_
  53.3 0.0 collective-permute-done.11.refs_1_
  53.3 5.2 %experts_last.1 = (bf16[128,1536]{1,0:T(8,128)(2,1)S(1)}, bf16[128,1536]{1,0:T(8,128)(2,1)S(1)}, bf16[128,2048]{1,0:T(8,128)(2,1)S(1)}, bf16[2048,1536]{1,0:T(8,128)(2,1)S(1)}) custom-call(s32[2]{0:T(128)S(1)} %pad_add_fusion._.place_ref, bf16[64,1664]{1,0:T(8,128)(2,1)S(1)} %collective-permute-done.6.refs_0_, ...), custom_call_target="tpu_custom_call" | custom-call | flops 1610612736 | bytes 12582912 | tf_op jit(solution)/shard_map/experts_last/pallas_call | solution.py:402
  58.5 0.4 collective-permute-start.13
  58.9 0.1 collective-permute-start.12
  59.1 1.2 %collective-permute-done.13.refs_0_ = bf16[128,1536]{1,0:T(8,128)(2,1)S(1)} collective-permute-done((bf16[128,1536]{1,0:T(8,128)(2,1)S(1)}, bf16[128,1536]{1,0:T(8,128)(2,1)S(1)}, u32[]{:S(2)}, u32[]{:S(2)}) %collective-permute-start.13) | collective-permute-done | bytes 393248 | tf_op jit(solution)/shard_map/ppermute | solution.py:26
  60.3 1.5 %back.1 = (bf16[64,1536]{1,0:T(8,128)(2,1)S(1)}, bf16[64,1536]{1,0:T(8,128)(2,1)S(1)}) custom-call(s32[2]{0:T(128)S(1)} %pad_add_fusion._.place_ref, bf16[128,2048]{1,0:T(8,128)(2,1)S(1)} %get-tuple-element.68.h_ref, bf16[128,1536]{1,0:T(8,128)(2,1)S(1)} %collective-permute-done.13.refs_0_, bf16[2048,1536]{1,0:T(8,128)(2,1)S(1)} %get-tuple-element.71.refs_1_), custom_call_target="tpu_custom_call" | custom-call | tf_op jit(solution)/shard_map/back/pallas_call | solution.py:435
  61.8 1.3 %collective-permute-start.15 = (bf16[64,1536]{1,0:T(8,128)(2,1)S(1)}, bf16[64,1536]{1,0:T(8,128)(2,1)S(1)}, u32[]{:S(2)}, u32[]{:S(2)}) collective-permute-start(bf16[64,1536]{1,0:T(8,128)(2,1)S(1)} %get-tuple-element.72.token_ref), channel_id=1, source_target_pairs={{0,8},{4,12},{8,0},{12,4},{1,9},{5,13},{9,1},{13,5},{2,10},{6,14},... | collective-permute-start | bytes 589832 | tf_op jit(solution)/shard_map/ppermute | solution.py:26
  63.1 0.8 collective-permute-start.14
  63.9 0.0 collective-permute-done.12.add_ref
  63.9 4.4 %own_block.1 = (f32[64,1536]{1,0:T(8,128)S(1)}, f32[64,1536]{1,0:T(8,128)S(1)}) custom-call(s32[2]{0:T(128)S(1)} %pad_add_fusion._.place_ref, bf16[128,2048]{1,0:T(8,128)(2,1)S(1)} %get-tuple-element.68.h_ref, bf16[128,1536]{1,0:T(8,128)(2,1)S(1)} %collective-permute-done.12.add_ref, bf16[64,1536]{1,0:T(8,128)(2,1)S(1)} %get-tuple-element.72.token_ref, ...), custom_call_target="tpu_custom_call" | custom-call | flops 805306368 | bytes 6291456 | tf_op jit(solution)/shard_map/own_block/pallas_call | solution.py:458
  68.3 1.3 %collective-permute-done.15 = bf16[64,1536]{1,0:T(8,128)(2,1)S(1)} collective-permute-done((bf16[64,1536]{1,0:T(8,128)(2,1)S(1)}, bf16[64,1536]{1,0:T(8,128)(2,1)S(1)}, u32[]{:S(2)}, u32[]{:S(2)}) %collective-permute-start.15) | collective-permute-done | bytes 196640 | tf_op jit(solution)/shard_map/ppermute | solution.py:26
  69.7 1.6 %collective-permute-start.16 = (bf16[64,1536]{1,0:T(8,128)(2,1)S(1)}, bf16[64,1536]{1,0:T(8,128)(2,1)S(1)}, u32[]{:S(2)}, u32[]{:S(2)}) collective-permute-start(bf16[64,1536]{1,0:T(8,128)(2,1)S(1)} %add_convert_fusion), channel_id=1, source_target_pairs={{0,1},{1,0},{2,3},{3,2},{4,5},{5,4},{6,7},{7,6},{8,9},{9,8},{10,11... | collective-permute-start | bytes 589832 | tf_op jit(solution)/shard_map/ppermute | solution.py:26
  71.3 2.0 %collective-permute-done.14 = bf16[64,1536]{1,0:T(8,128)(2,1)S(1)} collective-permute-done((bf16[64,1536]{1,0:T(8,128)(2,1)S(1)}, bf16[64,1536]{1,0:T(8,128)(2,1)S(1)}, u32[]{:S(2)}, u32[]{:S(2)}) %collective-permute-start.14) | collective-permute-done | bytes 196640 | tf_op jit(solution)/shard_map/ppermute | solution.py:26
  73.3 2.3 %collective-permute-done.16 = bf16[64,1536]{1,0:T(8,128)(2,1)S(1)} collective-permute-done((bf16[64,1536]{1,0:T(8,128)(2,1)S(1)}, bf16[64,1536]{1,0:T(8,128)(2,1)S(1)}, u32[]{:S(2)}, u32[]{:S(2)}) %collective-permute-start.16) | collective-permute-done | bytes 196640 | tf_op jit(solution)/shard_map/ppermute | solution.py:26
  75.6 0.1 convert_add_fusion
  75.6 3.0 %collective-permute-start.17 = (bf16[32,1536]{1,0:T(8,128)(2,1)S(1)}, bf16[32,1536]{1,0:T(8,128)(2,1)S(1)}, u32[]{:S(2)}, u32[]{:S(2)}) collective-permute-start(bf16[32,1536]{1,0:T(8,128)(2,1)S(1)} %slice.15), channel_id=1, source_target_pairs={{0,2},{1,3},{2,0},{3,1},{4,6},{5,7},{6,4},{7,5},{8,10},{9,11},{10,... | collective-permute-start | bytes 294920 | tf_op jit(solution)/shard_map/ppermute | solution.py:26
  78.7 0.6 copy.14
  79.3 2.0 %collective-permute-done.17 = bf16[32,1536]{1,0:T(8,128)(2,1)S(1)} collective-permute-done((bf16[32,1536]{1,0:T(8,128)(2,1)S(1)}, bf16[32,1536]{1,0:T(8,128)(2,1)S(1)}, u32[]{:S(2)}, u32[]{:S(2)}) %collective-permute-start.17) | collective-permute-done | bytes 98336 | tf_op jit(solution)/shard_map/ppermute | solution.py:26
  81.3 0.7 fusion
  (10 shorter events, 0.1 us)
Async XLA Ops:
  6.3 5.8 %collective-permute-start.1 = (bf16[32,1536]{1,0:T(8,128)(2,1)S(1)}, bf16[32,1536]{1,0:T(8,128)(2,1)S(1)}, u32[]{:S(2)}, u32[]{:S(2)}) collective-permute-start(bf16[32,1536]{1,0:T(8,128)(2,1)S(1)} %get-tuple-element.39.refs_0_), channel_id=1, source_target_pairs={{0,8},{4,12},{8,0},{12,4},{1,9},{5,13},{9,1},{13,5},{2,10},{6,14},... | collective-permute-start | bytes 294920 | tf_op jit(solution)/shard_map/ppermute | solution.py:26
  9.4 2.8 %collective-permute-start = (bf16[32,1536]{1,0:T(8,128)(2,1)S(1)}, bf16[32,1536]{1,0:T(8,128)(2,1)S(1)}, u32[]{:S(2)}, u32[]{:S(2)}) collective-permute-start(bf16[32,1536]{1,0:T(8,128)(2,1)S(1)} %get-tuple-element.39.refs_0_), channel_id=1, source_target_pairs={{0,4},{4,0},{8,12},{12,8},{1,5},{5,1},{9,13},{13,9},{2,6},{6,2},{1... | collective-permute-start | bytes 294920 | tf_op jit(solution)/shard_map/ppermute | solution.py:26
  12.2 1.3 %collective-permute-start.2 = (bf16[32,1536]{1,0:T(8,128)(2,1)S(1)}, bf16[32,1536]{1,0:T(8,128)(2,1)S(1)}, u32[]{:S(2)}, u32[]{:S(2)}) collective-permute-start(bf16[32,1536]{1,0:T(8,128)(2,1)S(1)} %collective-permute-done.1.refs_2_), channel_id=1, source_target_pairs={{0,4},{4,0},{8,12},{12,8},{1,5},{5,1},{9,13},{13,9},{2,6},{6,2},{1... | collective-permute-start | bytes 294920 | tf_op jit(solution)/shard_map/ppermute | solution.py:26
  14.8 5.3 %copy-start.3 = (s32[128,2]{0,1:T(2,128)S(1)}, s32[128,2]{0,1:T(2,128)}, u32[]{:S(2)}) copy-start(s32[128,2]{0,1:T(2,128)} %param.19) | copy-start | bytes 3076
  14.9 5.3 %copy-start.4 = (f32[128,2]{0,1:T(2,128)S(1)}, f32[128,2]{0,1:T(2,128)}, u32[]{:S(2)}) copy-start(f32[128,2]{0,1:T(2,128)} %param.20) | copy-start | bytes 3076
  14.9 7.2 %collective-permute-start.3 = (bf16[64,1536]{1,0:T(8,128)(2,1)S(1)}, bf16[64,1536]{1,0:T(8,128)(2,1)S(1)}, u32[]{:S(2)}, u32[]{:S(2)}) collective-permute-start(bf16[64,1536]{1,0:T(8,128)(2,1)S(1)} %get-tuple-element.42.token_ref), channel_id=1, source_target_pairs={{0,1},{1,0},{2,3},{3,2},{4,5},{5,4},{6,7},{7,6},{8,9},{9,8},{10,11... | collective-permute-start | bytes 589832 | tf_op jit(solution)/shard_map/ppermute | solution.py:26
  22.1 11.6 %copy-start.1 = (bf16[128,1536]{1,0:T(8,128)(2,1)S(1)}, bf16[128,1536]{1,0:T(8,128)(2,1)}, u32[]{:S(2)}) copy-start(bf16[128,1536]{1,0:T(8,128)(2,1)} %refs_1_.3) | copy-start | bytes 1179652
  22.1 11.6 %copy-start.2 = (f32[1536]{0:T(1024)S(1)}, f32[1536]{0:T(1024)}, u32[]{:S(2)}) copy-start(f32[1536]{0:T(1024)} %refs_2_.3) | copy-start | bytes 18436
  22.1 11.6 %collective-permute-start.4 = (bf16[64,1536]{1,0:T(8,128)(2,1)S(1)}, bf16[64,1536]{1,0:T(8,128)(2,1)S(1)}, u32[]{:S(2)}, u32[]{:S(2)}) collective-permute-start(bf16[64,1536]{1,0:T(8,128)(2,1)S(1)} %get-tuple-element.45.token_ref), channel_id=1, source_target_pairs={{0,2},{1,3},{2,0},{3,1},{4,6},{5,7},{6,4},{7,5},{8,10},{9,11},{10,... | collective-permute-start | bytes 589832 | tf_op jit(solution)/shard_map/ppermute | solution.py:26
  33.7 7.3 %copy-start = (bf16[1536,2048]{1,0:T(8,128)(2,1)}, bf16[1536,2048]{1,0:T(8,128)(2,1)S(1)}, u32[]{:S(2)}) copy-start(bf16[1536,2048]{1,0:T(8,128)(2,1)S(1)} %get-tuple-element.50.refs_2_) | copy-start | bytes 18874372
  34.5 6.6 %collective-permute-start.7 = (bf16[64,1664]{1,0:T(8,128)(2,1)S(1)}, bf16[64,1664]{1,0:T(8,128)(2,1)S(1)}, u32[]{:S(2)}, u32[]{:S(2)}) collective-permute-start(bf16[64,1664]{1,0:T(8,128)(2,1)S(1)} %get-tuple-element.48.token_ref.x_ref), channel_id=1, source_target_pairs={{0,1},{1,0},{2,3},{3,2},{4,5},{5,4},{6,7},{7,6},{8,9},{9,8},{10,11... | collective-permute-start | bytes 638984 | tf_op jit(solution)/shard_map/ppermute | solution.py:26
  36.1 6.3 %collective-permute-start.5 = (bf16[64,1664]{1,0:T(8,128)(2,1)S(1)}, bf16[64,1664]{1,0:T(8,128)(2,1)S(1)}, u32[]{:S(2)}, u32[]{:S(2)}) collective-permute-start(bf16[64,1664]{1,0:T(8,128)(2,1)S(1)} %get-tuple-element.48.token_ref.x_ref), channel_id=1, source_target_pairs={{0,8},{4,12},{8,0},{12,4},{1,9},{5,13},{9,1},{13,5},{2,10},{6,14},... | collective-permute-start | bytes 638984 | tf_op jit(solution)/shard_map/ppermute | solution.py:26
  41.0 5.3 %collective-permute-start.9 = (bf16[64,1664]{1,0:T(8,128)(2,1)S(1)}, bf16[64,1664]{1,0:T(8,128)(2,1)S(1)}, u32[]{:S(2)}, u32[]{:S(2)}) collective-permute-start(bf16[64,1664]{1,0:T(8,128)(2,1)S(1)} %get-tuple-element.48.token_ref.x_ref), channel_id=1, source_target_pairs={{0,4},{4,0},{8,12},{12,8},{1,5},{5,1},{9,13},{13,9},{2,6},{6,2},{1... | collective-permute-start | bytes 638984 | tf_op jit(solution)/shard_map/ppermute | solution.py:26
  41.1 5.2 %slice-start = ((s8[6291456]{0:T(1024)(128)(4,1)}), s8[4194304]{0:T(1024)(128)(4,1)S(1)}, s32[]{:S(2)}) async-start(s8[6291456]{0:T(1024)(128)(4,1)} %bitcast.4), calls=%async_computation | async-start | bytes 8388608
  41.1 5.2 %collective-permute-start.10 = (bf16[64,1664]{1,0:T(8,128)(2,1)S(1)}, bf16[64,1664]{1,0:T(8,128)(2,1)S(1)}, u32[]{:S(2)}, u32[]{:S(2)}) collective-permute-start(bf16[64,1664]{1,0:T(8,128)(2,1)S(1)} %passed_on.3.refs_1_), channel_id=1, source_target_pairs={{0,4},{4,0},{8,12},{12,8},{1,5},{5,1},{9,13},{13,9},{2,6},{6,2},{1... | collective-permute-start | bytes 638984 | tf_op jit(solution)/shard_map/ppermute | solution.py:26
  41.6 8.0 %collective-permute-start.8 = (bf16[64,1664]{1,0:T(8,128)(2,1)S(1)}, bf16[64,1664]{1,0:T(8,128)(2,1)S(1)}, u32[]{:S(2)}, u32[]{:S(2)}) collective-permute-start(bf16[64,1664]{1,0:T(8,128)(2,1)S(1)} %passed_on.3.refs_1_), channel_id=1, source_target_pairs={{0,8},{4,12},{8,0},{12,4},{1,9},{5,13},{9,1},{13,5},{2,10},{6,14},... | collective-permute-start | bytes 638984 | tf_op jit(solution)/shard_map/ppermute | solution.py:26
  42.4 3.9 %slice-start.1 = ((s8[6291456]{0:T(1024)(128)(4,1)}), s8[2097152]{0:T(1024)(128)(4,1)S(1)}, s32[]{:S(2)}) async-start(s8[6291456]{0:T(1024)(128)(4,1)} %bitcast.4), calls=%async_computation.1 | async-start | bytes 4194304
  45.8 7.4 %collective-permute-start.6 = (bf16[64,1664]{1,0:T(8,128)(2,1)S(1)}, bf16[64,1664]{1,0:T(8,128)(2,1)S(1)}, u32[]{:S(2)}, u32[]{:S(2)}) collective-permute-start(bf16[64,1664]{1,0:T(8,128)(2,1)S(1)} %collective-permute-done.5.refs_0_), channel_id=1, source_target_pairs={{0,4},{4,0},{8,12},{12,8},{1,5},{5,1},{9,13},{13,9},{2,6},{6,2},{1... | collective-permute-start | bytes 638984 | tf_op jit(solution)/shard_map/ppermute | solution.py:26
  49.7 3.6 %collective-permute-start.11 = (bf16[64,1664]{1,0:T(8,128)(2,1)S(1)}, bf16[64,1664]{1,0:T(8,128)(2,1)S(1)}, u32[]{:S(2)}, u32[]{:S(2)}) collective-permute-start(bf16[64,1664]{1,0:T(8,128)(2,1)S(1)} %passed_on.5.refs_1_), channel_id=1, source_target_pairs={{0,4},{4,0},{8,12},{12,8},{1,5},{5,1},{9,13},{13,9},{2,6},{6,2},{1... | collective-permute-start | bytes 638984 | tf_op jit(solution)/shard_map/ppermute | solution.py:26
  58.5 1.8 %collective-permute-start.13 = (bf16[128,1536]{1,0:T(8,128)(2,1)S(1)}, bf16[128,1536]{1,0:T(8,128)(2,1)S(1)}, u32[]{:S(2)}, u32[]{:S(2)}) collective-permute-start(bf16[128,1536]{1,0:T(8,128)(2,1)S(1)} %get-tuple-element.70), channel_id=1, source_target_pairs={{0,4},{4,0},{8,12},{12,8},{1,5},{5,1},{9,13},{13,9},{2,6},{6,2},{1... | collective-permute-start | bytes 1179656 | tf_op jit(solution)/shard_map/ppermute | solution.py:26
  58.9 5.0 %collective-permute-start.12 = (bf16[128,1536]{1,0:T(8,128)(2,1)S(1)}, bf16[128,1536]{1,0:T(8,128)(2,1)S(1)}, u32[]{:S(2)}, u32[]{:S(2)}) collective-permute-start(bf16[128,1536]{1,0:T(8,128)(2,1)S(1)} %get-tuple-element.69), channel_id=1, source_target_pairs={{0,4},{4,0},{8,12},{12,8},{1,5},{5,1},{9,13},{13,9},{2,6},{6,2},{1... | collective-permute-start | bytes 1179656 | tf_op jit(solution)/shard_map/ppermute | solution.py:26
  61.8 7.8 %collective-permute-start.15 = (bf16[64,1536]{1,0:T(8,128)(2,1)S(1)}, bf16[64,1536]{1,0:T(8,128)(2,1)S(1)}, u32[]{:S(2)}, u32[]{:S(2)}) collective-permute-start(bf16[64,1536]{1,0:T(8,128)(2,1)S(1)} %get-tuple-element.72.token_ref), channel_id=1, source_target_pairs={{0,8},{4,12},{8,0},{12,4},{1,9},{5,13},{9,1},{13,5},{2,10},{6,14},... | collective-permute-start | bytes 589832 | tf_op jit(solution)/shard_map/ppermute | solution.py:26
  63.1 10.2 %collective-permute-start.14 = (bf16[64,1536]{1,0:T(8,128)(2,1)S(1)}, bf16[64,1536]{1,0:T(8,128)(2,1)S(1)}, u32[]{:S(2)}, u32[]{:S(2)}) collective-permute-start(bf16[64,1536]{1,0:T(8,128)(2,1)S(1)} %get-tuple-element.74), channel_id=1, source_target_pairs={{0,8},{4,12},{8,0},{12,4},{1,9},{5,13},{9,1},{13,5},{2,10},{6,14},... | collective-permute-start | bytes 589832 | tf_op jit(solution)/shard_map/ppermute | solution.py:26
  69.7 5.9 %collective-permute-start.16 = (bf16[64,1536]{1,0:T(8,128)(2,1)S(1)}, bf16[64,1536]{1,0:T(8,128)(2,1)S(1)}, u32[]{:S(2)}, u32[]{:S(2)}) collective-permute-start(bf16[64,1536]{1,0:T(8,128)(2,1)S(1)} %add_convert_fusion), channel_id=1, source_target_pairs={{0,1},{1,0},{2,3},{3,2},{4,5},{5,4},{6,7},{7,6},{8,9},{9,8},{10,11... | collective-permute-start | bytes 589832 | tf_op jit(solution)/shard_map/ppermute | solution.py:26
  75.6 5.6 %collective-permute-start.17 = (bf16[32,1536]{1,0:T(8,128)(2,1)S(1)}, bf16[32,1536]{1,0:T(8,128)(2,1)S(1)}, u32[]{:S(2)}, u32[]{:S(2)}) collective-permute-start(bf16[32,1536]{1,0:T(8,128)(2,1)S(1)} %slice.15), channel_id=1, source_target_pairs={{0,2},{1,3},{2,0},{3,1},{4,6},{5,7},{6,4},{7,5},{8,10},{9,11},{10,... | collective-permute-start | bytes 294920 | tf_op jit(solution)/shard_map/ppermute | solution.py:26

commit v4 on v3

--- a/solution.py
+++ b/solution.py
@@ -419,27 +419,43 @@
     return res[:a], res[a], res[a + 1 :]
 
 
-def back_kernel(n, place_ref, h_ref, *refs):
-    adds, ready, outs = refs[:n], refs[n : 2 * n], refs[2 * n : 4 * n]
+def down_kernel(n, h_ref, *refs):
+    for w, out in zip(refs[:n], refs[n:]):
+        out[...] = jnp.dot(h_ref[...], w[...], preferred_element_type=f32).astype(out.dtype)
+
+
+def down_blocks(h, downs, types):
+    n, rows, (hidden, width) = len(downs), h.shape[0], downs[0].shape
+    return pl.pallas_call(
+        functools.partial(down_kernel, n),
+        out_shape=[jax.ShapeDtypeStruct((rows, width), t) for t in types],
+        in_specs=[VMEM_SPEC] * (1 + n),
+        out_specs=[VMEM_SPEC] * n,
+        compiler_params=pltpu.CompilerParams(vmem_limit_bytes=4 * MIB),
+        cost_estimate=cost(2 * n * width * hidden, 2 * n * rows * width * hidden),
+        name="down",
+    )(h, *downs)
+
+
+def back_kernel(n, *refs):
+    own, adds, outs = refs[:n], refs[n : 2 * n], refs[2 * n :]
     half = outs[0].shape[0]
     for i in range(n):
-        value = jnp.dot(h_ref[...], ready[i][...], preferred_element_type=f32) + adds[i][...].astype(f32)
-        value = value.astype(bf16)
-        outs[2 * i][...] = value[:half]
-        outs[2 * i + 1][...] = value[half:]
-
-
-def back(place, h, adds, ready):
-    rows = h.shape[0]
-    n, width = len(ready), ready[0].shape[1]
+        for part in range(2):
+            rows = slice(part * half, (part + 1) * half)
+            outs[2 * i + part][...] = (own[i][rows, :] + adds[i][rows, :].astype(f32)).astype(bf16)
+
+
+def back(own, adds):
+    n, (rows, width) = len(own), own[0].shape
     res = pl.pallas_call(
         functools.partial(back_kernel, n),
         out_shape=[jax.ShapeDtypeStruct((rows // 2, width), bf16) for _ in range(2 * n)],
-        in_specs=[SMEM_SPEC] + [VMEM_SPEC] * (1 + 2 * n),
+        in_specs=[VMEM_SPEC] * (2 * n),
         out_specs=[VMEM_SPEC] * (2 * n),
         compiler_params=pltpu.CompilerParams(vmem_limit_bytes=4 * MIB),
         name="back",
-    )(place, h, *adds, *ready)
+    )(*own, *adds)
     return [res[2 * i : 2 * i + 2] for i in range(n)]
 
 
@@ -532,7 +548,7 @@
     out_odd, h, ready = last_blocks(place, last, odd_gates, odd_ups, acc, weight, downs, w_down, 1, even)
 
     crossed = [swap(o, "dp", 1) for o in out_odd]
-    sums = back(place, h, crossed[:-1], ready)
+    sums = back(down_blocks(h, ready, [f32] * len(even)), crossed[:-1])
     there = [swap(s[1], "dp", k) for s, k in zip(sums, even)]
     here = [swap(s[0], "dp", k) for s, k in zip(sums, even)]
     mix_a, mix_b = own_block(place, h, crossed[-1], sums[0][1], w_down, width)

time: 82.2 us -> 80.8 us (0.983)
  waiting for transfers between devices: 14.1 us -> 13.1 us
    pallas_call x1, Pallas kernels: 1.54 us -> 0.07 us  [back(): pl.pallas_call(functools.partial(back_kernel, n), out_shape=[jax.ShapeDty...]
    ppermute x18, waiting for transfers between devices: 14.1 us -> 13.1 us  [swap(): return lax.ppermute(x, axis, [(i, i ^ k) for i in range(n)])]
    pallas_call x0 -> x1, Pallas kernels: none -> 0.99 us  [down_blocks(): pl.pallas_call(functools.partial(down_kernel, n), out_shape=[jax.ShapeDty...]
where the time goes in v4:
time: 80.8 us; the launch traced here: 80.5 us
  Pallas kernels  44.6 us (55%)
  starting transfers between devices  20.4 us (25%)
  waiting for transfers between devices  13.1 us (16%)
  between operations  0.94 us (1%)
  other arithmetic  0.82 us (1%)
    ppermute x18, starting transfers between devices, swap(): return lax.ppermute(x, axis, [(i, i ^ k) for i in range(n)])  20.4 us
    pallas_call x3, Pallas kernels, fetch(): pl.pallas_call(functools.partial(fetch_kernel, ks), out_shape=[VM((width,...  15.4 us
    ppermute x18, waiting for transfers between devices, swap(): return lax.ppermute(x, axis, [(i, i ^ k) for i in range(n)])  13.1 us
    pallas_call x3, Pallas kernels, grow(): pl.pallas_call(functools.partial(grow_kernel, acc is None, [k for _, k in...  10.1 us
    pallas_call x1, Pallas kernels, attend(): pl.pallas_call(functools.partial(attend_kernel, kv, group, batch), out_sh...  5.61 us
    pallas_call x1, Pallas kernels, last_blocks(): pl.pallas_call(functools.partial(last_kernel, n, a, late, even, down.shap...  5.19 us
    pallas_call x1, Pallas kernels, own_block(): pl.pallas_call(own_kernel, out_shape=[jax.ShapeDtypeStruct((rows // 2, wi...  4.36 us
  transfers between devices with their start and end apart: 18, of which 8 were waited for; matrix products, arithmetic and copies ran while one was open for 1% of the time, Pallas kernels for 39%

profile of v4, /device:TPU:0, one launch (start us, length us, event | category | flops | bytes accessed | tf_op | source)
XLA Modules:
  0.0 80.5 jit_solution(11546125378354052924)
XLA Ops:
  0.6 0.1 pad_add_fusion._.place_ref
  0.7 5.6 %attention.1 = (bf16[32,1536]{1,0:T(8,128)(2,1)S(1)}, bf16[1536,1536]{1,0:T(8,128)(2,1)S(1)}) custom-call(s32[2]{0:T(128)S(1)} %pad_add_fusion._.place_ref, s32[32]{0:T(128)} %len_hbm.1, bf16[32,1536]{1,0:T(8,128)(2,1)} %q_hbm.1, bf16[32,512]{1,0:T(8,128)(2,1)} %new_hbm.1, bf16[32,160,512]{2,1,0:T(8,128)(2,1)} %cache_hbm.1, bf16[1536,1536]{1,0:T(8,128)(2,1)} %w_hbm.1), custom_call_target="tpu_custom_call" | custom-call | flops 62914560 | bytes 10485760 | tf_op jit(solution)/shard_map/attention/pallas_call | solution.py:125
  6.3 3.0 %collective-permute-start.1 = (bf16[32,1536]{1,0:T(8,128)(2,1)S(1)}, bf16[32,1536]{1,0:T(8,128)(2,1)S(1)}, u32[]{:S(2)}, u32[]{:S(2)}) collective-permute-start(bf16[32,1536]{1,0:T(8,128)(2,1)S(1)} %get-tuple-element.39.refs_0_), channel_id=1, source_target_pairs={{0,8},{4,12},{8,0},{12,4},{1,9},{5,13},{9,1},{13,5},{2,10},{6,14},... | collective-permute-start | bytes 294920 | tf_op jit(solution)/shard_map/ppermute | solution.py:26
  9.4 0.0 collective-permute-start
  9.4 2.8 %collective-permute-done.1.refs_2_ = bf16[32,1536]{1,0:T(8,128)(2,1)S(1)} collective-permute-done((bf16[32,1536]{1,0:T(8,128)(2,1)S(1)}, bf16[32,1536]{1,0:T(8,128)(2,1)S(1)}, u32[]{:S(2)}, u32[]{:S(2)}) %collective-permute-start.1) | collective-permute-done | bytes 98336 | tf_op jit(solution)/shard_map/ppermute | solution.py:26
  12.2 0.0 collective-permute-start.2
  12.2 0.0 collective-permute-done.refs_1_
  12.2 1.3 %collective-permute-done.2.refs_3_ = bf16[32,1536]{1,0:T(8,128)(2,1)S(1)} collective-permute-done((bf16[32,1536]{1,0:T(8,128)(2,1)S(1)}, bf16[32,1536]{1,0:T(8,128)(2,1)S(1)}, u32[]{:S(2)}, u32[]{:S(2)}) %collective-permute-start.2) | collective-permute-done | bytes 98336 | tf_op jit(solution)/shard_map/ppermute | solution.py:26
  13.5 1.4 %projection.1 = (f32[64,1536]{1,0:T(8,128)S(1)}, bf16[64,1536]{1,0:T(8,128)(2,1)S(1)}) custom-call(s32[2]{0:T(128)S(1)} %pad_add_fusion._.place_ref, bf16[32,1536]{1,0:T(8,128)(2,1)S(1)} %get-tuple-element.39.refs_0_, bf16[32,1536]{1,0:T(8,128)(2,1)S(1)} %collective-permute-done.refs_1_, bf16[32,1536]{1,0:T(8,128)(2,1)S(1)} %collective-permute-done.1.refs_2_, ...), custom_call_target="tpu_custom_call" | custom-call | flops 603979776 | bytes 4718592 | tf_op jit(solution)/shard_map/projection/pallas_call | solution.py:193
  14.8 0.0 copy-start.3
  14.9 0.0 copy-start.4
  14.9 1.9 %collective-permute-start.3 = (bf16[64,1536]{1,0:T(8,128)(2,1)S(1)}, bf16[64,1536]{1,0:T(8,128)(2,1)S(1)}, u32[]{:S(2)}, u32[]{:S(2)}) collective-permute-start(bf16[64,1536]{1,0:T(8,128)(2,1)S(1)} %get-tuple-element.42.token_ref), channel_id=1, source_target_pairs={{0,1},{1,0},{2,3},{3,2},{4,5},{5,4},{6,7},{7,6},{8,9},{9,8},{10,11... | collective-permute-start | bytes 589832 | tf_op jit(solution)/shard_map/ppermute | solution.py:26
  16.8 3.3 %fetch.3 = (bf16[1536,2048]{1,0:T(8,128)(2,1)S(1)}, bf16[8,128]{1,0:T(8,128)(2,1)S(1)}) custom-call(s32[2]{0:T(128)S(1)} %pad_add_fusion._.place_ref, bf16[64,1536]{1,0:T(8,128)(2,1)S(1)} %get-tuple-element.42.token_ref, bf16[6144,2048]{1,0:T(8,128)(2,1)} %refs_4_.1), custom_call_target="tpu_custom_call" | custom-call | bytes 6291456 | tf_op jit(solution)/shard_map/fetch/pallas_call | solution.py:159
  20.2 0.0 copy-done.3
  20.2 0.0 copy-done.4
  20.2 0.6 request_weights.1.refs_1_.refs_7_
  20.8 1.2 %collective-permute-done.3.got_ref = bf16[64,1536]{1,0:T(8,128)(2,1)S(1)} collective-permute-done((bf16[64,1536]{1,0:T(8,128)(2,1)S(1)}, bf16[64,1536]{1,0:T(8,128)(2,1)S(1)}, u32[]{:S(2)}, u32[]{:S(2)}) %collective-permute-start.3) | collective-permute-done | bytes 196640 | tf_op jit(solution)/shard_map/ppermute | solution.py:26
  22.0 0.1 pair_sum.1
  22.1 0.0 copy-start.1
  22.1 0.0 copy-start.2
  22.1 2.8 %collective-permute-start.4 = (bf16[64,1536]{1,0:T(8,128)(2,1)S(1)}, bf16[64,1536]{1,0:T(8,128)(2,1)S(1)}, u32[]{:S(2)}, u32[]{:S(2)}) collective-permute-start(bf16[64,1536]{1,0:T(8,128)(2,1)S(1)} %get-tuple-element.45.token_ref), channel_id=1, source_target_pairs={{0,2},{1,3},{2,0},{3,1},{4,6},{5,7},{6,4},{7,5},{8,10},{9,11},{10,... | collective-permute-start | bytes 589832 | tf_op jit(solution)/shard_map/ppermute | solution.py:26
  24.9 8.8 %fetch.4 = (bf16[1536,2048]{1,0:T(8,128)(2,1)S(1)}, bf16[1536,2048]{1,0:T(8,128)(2,1)S(1)}, bf16[1536,2048]{1,0:T(8,128)(2,1)S(1)}, bf16[1536,2048]{1,0:T(8,128)(2,1)S(1)}, bf16[8,128]{1,0:T(8,128)(2,1)S(1)}) custom-call(s32[2]{0:T(128)S(1)} %pad_add_fusion._.place_ref, bf16[64,1536]{1,0:T(8,128)(2,1)S(1)} %get-tuple-element.45.token_ref, ...), custom_call_target="tpu_custom_call" | custom-call | bytes 25165824 | tf_op jit(solution)/shard_map/fetch/pallas_call | solution.py:159
  33.7 0.0 collective-permute-done.4.refs_0_
  33.7 0.0 copy-done.1
  33.7 0.7 residual_stream.1
  34.5 1.6 %collective-permute-start.7 = (bf16[64,1664]{1,0:T(8,128)(2,1)S(1)}, bf16[64,1664]{1,0:T(8,128)(2,1)S(1)}, u32[]{:S(2)}, u32[]{:S(2)}) collective-permute-start(bf16[64,1664]{1,0:T(8,128)(2,1)S(1)} %get-tuple-element.48.token_ref.x_ref), channel_id=1, source_target_pairs={{0,1},{1,0},{2,3},{3,2},{4,5},{5,4},{6,7},{7,6},{8,9},{9,8},{10,11... | collective-permute-start | bytes 638984 | tf_op jit(solution)/shard_map/ppermute | solution.py:26
  36.1 1.5 %collective-permute-start.5 = (bf16[64,1664]{1,0:T(8,128)(2,1)S(1)}, bf16[64,1664]{1,0:T(8,128)(2,1)S(1)}, u32[]{:S(2)}, u32[]{:S(2)}) collective-permute-start(bf16[64,1664]{1,0:T(8,128)(2,1)S(1)} %get-tuple-element.48.token_ref.x_ref), channel_id=1, source_target_pairs={{0,8},{4,12},{8,0},{12,4},{1,9},{5,13},{9,1},{13,5},{2,10},{6,14},... | collective-permute-start | bytes 638984 | tf_op jit(solution)/shard_map/ppermute | solution.py:26
  37.6 3.3 %fetch.5 = (bf16[1536,2048]{1,0:T(8,128)(2,1)S(1)}, bf16[8,128]{1,0:T(8,128)(2,1)S(1)}) custom-call(s32[2]{0:T(128)S(1)} %pad_add_fusion._.place_ref, bf16[64,1664]{1,0:T(8,128)(2,1)S(1)} %get-tuple-element.48.token_ref.x_ref, bf16[6144,2048]{1,0:T(8,128)(2,1)} %refs_7_.2), custom_call_target="tpu_custom_call" | custom-call | bytes 6291456 | tf_op jit(solution)/shard_map/fetch/pallas_call | solution.py:159
  41.0 0.1 collective-permute-start.9
  41.0 0.0 collective-permute-done.7.x_ref
  41.1 0.0 slice-start
  41.1 0.5 collective-permute-start.10
  41.6 0.8 collective-permute-start.8
  42.4 0.0 collective-permute-done.5.refs_0_
  42.4 0.0 slice-start.1
  42.4 3.4 %experts.3 = (f32[128,2048]{1,0:T(8,128)S(1)}, f32[128,2048]{1,0:T(8,128)S(1)}, f32[128,1]{1,0:T(8,128)S(1)}, bf16[1536,2048]{1,0:T(8,128)(2,1)S(1)}) custom-call(s32[2]{0:T(128)S(1)} %pad_add_fusion._.place_ref, bf16[64,1664]{1,0:T(8,128)(2,1)S(1)} %passed_on.4.refs_0_, bf16[64,1664]{1,0:T(8,128)(2,1)S(1)} %passed_on.3.refs_1_, ...), custom_call_target="tpu_custom_call" | custom-call | flops 1610612736 | bytes 12582912 | tf_op jit(solution)/shard_map/experts/pallas_call | solution.py:352
  45.8 0.4 collective-permute-start.6
  46.3 0.0 collective-permute-done.9.refs_0_
  46.3 0.0 collective-permute-done.10.refs_1_
  46.3 3.4 %experts.4 = (f32[128,2048]{1,0:T(8,128)S(1)}, f32[128,2048]{1,0:T(8,128)S(1)}, f32[128,1]{1,0:T(8,128)S(1)}, bf16[1536,2048]{1,0:T(8,128)(2,1)S(1)}) custom-call(s32[2]{0:T(128)S(1)} %pad_add_fusion._.place_ref, bf16[64,1664]{1,0:T(8,128)(2,1)S(1)} %collective-permute-done.9.refs_0_, bf16[64,1664]{1,0:T(8,128)(2,1)S(1)} %collective-permute-done.10.refs_1_, ...), custom_call_target="tpu_custom_call" | custom-call | flops 1610612736 | bytes 12582912 | tf_op jit(solution)/shard_map/experts/pallas_call | solution.py:352
  49.7 0.0 collective-permute-done.8.x_ref
  49.7 0.2 collective-permute-start.11
  49.9 3.3 %experts.5 = (f32[128,2048]{1,0:T(8,128)S(1)}, f32[128,2048]{1,0:T(8,128)S(1)}, f32[128,1]{1,0:T(8,128)S(1)}, bf16[2048,1536]{1,0:T(8,128)(2,1)S(1)}) custom-call(s32[2]{0:T(128)S(1)} %pad_add_fusion._.place_ref, bf16[64,1664]{1,0:T(8,128)(2,1)S(1)} %collective-permute-done.5.refs_0_, bf16[64,1664]{1,0:T(8,128)(2,1)S(1)} %passed_on.5.refs_1_, ...), custom_call_target="tpu_custom_call" | custom-call | flops 1610612736 | bytes 12582912 | tf_op jit(solution)/shard_map/experts/pallas_call | solution.py:352
  53.3 0.0 collective-permute-done.6.refs_0_
  53.3 0.0 collective-permute-done.11.refs_1_
  53.3 5.2 %experts_last.1 = (bf16[128,1536]{1,0:T(8,128)(2,1)S(1)}, bf16[128,1536]{1,0:T(8,128)(2,1)S(1)}, bf16[128,2048]{1,0:T(8,128)(2,1)S(1)}, bf16[2048,1536]{1,0:T(8,128)(2,1)S(1)}) custom-call(s32[2]{0:T(128)S(1)} %pad_add_fusion._.place_ref, bf16[64,1664]{1,0:T(8,128)(2,1)S(1)} %collective-permute-done.6.refs_0_, ...), custom_call_target="tpu_custom_call" | custom-call | flops 1610612736 | bytes 12582912 | tf_op jit(solution)/shard_map/experts_last/pallas_call | solution.py:402
  58.5 0.4 collective-permute-start.13
  58.9 0.1 collective-permute-start.12
  59.1 1.0 %down.1.refs_0_ = f32[128,1536]{1,0:T(8,128)S(1)} custom-call(bf16[128,2048]{1,0:T(8,128)(2,1)S(1)} %get-tuple-element.68.h_ref, bf16[2048,1536]{1,0:T(8,128)(2,1)S(1)} %get-tuple-element.70.refs_0_), custom_call_target="tpu_custom_call" | custom-call | flops 805306368 | bytes 6291456 | tf_op jit(solution)/shard_map/down/pallas_call | solution.py:429
  60.1 0.2 collective-permute-done.13.refs_1_
  60.3 0.1 back.1
  60.4 1.3 %collective-permute-start.15 = (bf16[64,1536]{1,0:T(8,128)(2,1)S(1)}, bf16[64,1536]{1,0:T(8,128)(2,1)S(1)}, u32[]{:S(2)}, u32[]{:S(2)}) collective-permute-start(bf16[64,1536]{1,0:T(8,128)(2,1)S(1)} %get-tuple-element.72.token_ref), channel_id=1, source_target_pairs={{0,8},{4,12},{8,0},{12,4},{1,9},{5,13},{9,1},{13,5},{2,10},{6,14},... | collective-permute-start | bytes 589832 | tf_op jit(solution)/shard_map/ppermute | solution.py:26
  61.7 0.8 collective-permute-start.14
  62.5 0.0 collective-permute-done.12.add_ref
  62.5 4.4 %own_block.1 = (f32[64,1536]{1,0:T(8,128)S(1)}, f32[64,1536]{1,0:T(8,128)S(1)}) custom-call(s32[2]{0:T(128)S(1)} %pad_add_fusion._.place_ref, bf16[128,2048]{1,0:T(8,128)(2,1)S(1)} %get-tuple-element.68.h_ref, bf16[128,1536]{1,0:T(8,128)(2,1)S(1)} %collective-permute-done.12.add_ref, bf16[64,1536]{1,0:T(8,128)(2,1)S(1)} %get-tuple-element.72.token_ref, ...), custom_call_target="tpu_custom_call" | custom-call | flops 805306368 | bytes 6291456 | tf_op jit(solution)/shard_map/own_block/pallas_call | solution.py:474
  66.8 1.3 %collective-permute-done.15 = bf16[64,1536]{1,0:T(8,128)(2,1)S(1)} collective-permute-done((bf16[64,1536]{1,0:T(8,128)(2,1)S(1)}, bf16[64,1536]{1,0:T(8,128)(2,1)S(1)}, u32[]{:S(2)}, u32[]{:S(2)}) %collective-permute-start.15) | collective-permute-done | bytes 196640 | tf_op jit(solution)/shard_map/ppermute | solution.py:26
  68.2 1.6 %collective-permute-start.16 = (bf16[64,1536]{1,0:T(8,128)(2,1)S(1)}, bf16[64,1536]{1,0:T(8,128)(2,1)S(1)}, u32[]{:S(2)}, u32[]{:S(2)}) collective-permute-start(bf16[64,1536]{1,0:T(8,128)(2,1)S(1)} %add_convert_fusion), channel_id=1, source_target_pairs={{0,1},{1,0},{2,3},{3,2},{4,5},{5,4},{6,7},{7,6},{8,9},{9,8},{10,11... | collective-permute-start | bytes 589832 | tf_op jit(solution)/shard_map/ppermute | solution.py:26
  69.8 2.0 %collective-permute-done.14 = bf16[64,1536]{1,0:T(8,128)(2,1)S(1)} collective-permute-done((bf16[64,1536]{1,0:T(8,128)(2,1)S(1)}, bf16[64,1536]{1,0:T(8,128)(2,1)S(1)}, u32[]{:S(2)}, u32[]{:S(2)}) %collective-permute-start.14) | collective-permute-done | bytes 196640 | tf_op jit(solution)/shard_map/ppermute | solution.py:26
  71.8 2.3 %collective-permute-done.16 = bf16[64,1536]{1,0:T(8,128)(2,1)S(1)} collective-permute-done((bf16[64,1536]{1,0:T(8,128)(2,1)S(1)}, bf16[64,1536]{1,0:T(8,128)(2,1)S(1)}, u32[]{:S(2)}, u32[]{:S(2)}) %collective-permute-start.16) | collective-permute-done | bytes 196640 | tf_op jit(solution)/shard_map/ppermute | solution.py:26
  74.1 0.1 convert_add_fusion
  74.1 3.1 %collective-permute-start.17 = (bf16[32,1536]{1,0:T(8,128)(2,1)S(1)}, bf16[32,1536]{1,0:T(8,128)(2,1)S(1)}, u32[]{:S(2)}, u32[]{:S(2)}) collective-permute-start(bf16[32,1536]{1,0:T(8,128)(2,1)S(1)} %slice.15), channel_id=1, source_target_pairs={{0,2},{1,3},{2,0},{3,1},{4,6},{5,7},{6,4},{7,5},{8,10},{9,11},{10,... | collective-permute-start | bytes 294920 | tf_op jit(solution)/shard_map/ppermute | solution.py:26
  77.2 0.6 copy.14
  77.8 2.0 %collective-permute-done.17 = bf16[32,1536]{1,0:T(8,128)(2,1)S(1)} collective-permute-done((bf16[32,1536]{1,0:T(8,128)(2,1)S(1)}, bf16[32,1536]{1,0:T(8,128)(2,1)S(1)}, u32[]{:S(2)}, u32[]{:S(2)}) %collective-permute-start.17) | collective-permute-done | bytes 98336 | tf_op jit(solution)/shard_map/ppermute | solution.py:26
  79.8 0.7 fusion
  (11 shorter events, 0.1 us)
Async XLA Ops:
  6.3 5.8 %collective-permute-start.1 = (bf16[32,1536]{1,0:T(8,128)(2,1)S(1)}, bf16[32,1536]{1,0:T(8,128)(2,1)S(1)}, u32[]{:S(2)}, u32[]{:S(2)}) collective-permute-start(bf16[32,1536]{1,0:T(8,128)(2,1)S(1)} %get-tuple-element.39.refs_0_), channel_id=1, source_target_pairs={{0,8},{4,12},{8,0},{12,4},{1,9},{5,13},{9,1},{13,5},{2,10},{6,14},... | collective-permute-start | bytes 294920 | tf_op jit(solution)/shard_map/ppermute | solution.py:26
  9.4 2.8 %collective-permute-start = (bf16[32,1536]{1,0:T(8,128)(2,1)S(1)}, bf16[32,1536]{1,0:T(8,128)(2,1)S(1)}, u32[]{:S(2)}, u32[]{:S(2)}) collective-permute-start(bf16[32,1536]{1,0:T(8,128)(2,1)S(1)} %get-tuple-element.39.refs_0_), channel_id=1, source_target_pairs={{0,4},{4,0},{8,12},{12,8},{1,5},{5,1},{9,13},{13,9},{2,6},{6,2},{1... | collective-permute-start | bytes 294920 | tf_op jit(solution)/shard_map/ppermute | solution.py:26
  12.2 1.3 %collective-permute-start.2 = (bf16[32,1536]{1,0:T(8,128)(2,1)S(1)}, bf16[32,1536]{1,0:T(8,128)(2,1)S(1)}, u32[]{:S(2)}, u32[]{:S(2)}) collective-permute-start(bf16[32,1536]{1,0:T(8,128)(2,1)S(1)} %collective-permute-done.1.refs_2_), channel_id=1, source_target_pairs={{0,4},{4,0},{8,12},{12,8},{1,5},{5,1},{9,13},{13,9},{2,6},{6,2},{1... | collective-permute-start | bytes 294920 | tf_op jit(solution)/shard_map/ppermute | solution.py:26
  14.8 5.3 %copy-start.3 = (s32[128,2]{0,1:T(2,128)S(1)}, s32[128,2]{0,1:T(2,128)}, u32[]{:S(2)}) copy-start(s32[128,2]{0,1:T(2,128)} %param.19) | copy-start | bytes 3076
  14.9 5.3 %copy-start.4 = (f32[128,2]{0,1:T(2,128)S(1)}, f32[128,2]{0,1:T(2,128)}, u32[]{:S(2)}) copy-start(f32[128,2]{0,1:T(2,128)} %param.20) | copy-start | bytes 3076
  14.9 7.2 %collective-permute-start.3 = (bf16[64,1536]{1,0:T(8,128)(2,1)S(1)}, bf16[64,1536]{1,0:T(8,128)(2,1)S(1)}, u32[]{:S(2)}, u32[]{:S(2)}) collective-permute-start(bf16[64,1536]{1,0:T(8,128)(2,1)S(1)} %get-tuple-element.42.token_ref), channel_id=1, source_target_pairs={{0,1},{1,0},{2,3},{3,2},{4,5},{5,4},{6,7},{7,6},{8,9},{9,8},{10,11... | collective-permute-start | bytes 589832 | tf_op jit(solution)/shard_map/ppermute | solution.py:26
  22.1 11.6 %copy-start.1 = (bf16[128,1536]{1,0:T(8,128)(2,1)S(1)}, bf16[128,1536]{1,0:T(8,128)(2,1)}, u32[]{:S(2)}) copy-start(bf16[128,1536]{1,0:T(8,128)(2,1)} %refs_1_.3) | copy-start | bytes 1179652
  22.1 11.6 %copy-start.2 = (f32[1536]{0:T(1024)S(1)}, f32[1536]{0:T(1024)}, u32[]{:S(2)}) copy-start(f32[1536]{0:T(1024)} %refs_2_.3) | copy-start | bytes 18436
  22.1 11.6 %collective-permute-start.4 = (bf16[64,1536]{1,0:T(8,128)(2,1)S(1)}, bf16[64,1536]{1,0:T(8,128)(2,1)S(1)}, u32[]{:S(2)}, u32[]{:S(2)}) collective-permute-start(bf16[64,1536]{1,0:T(8,128)(2,1)S(1)} %get-tuple-element.45.token_ref), channel_id=1, source_target_pairs={{0,2},{1,3},{2,0},{3,1},{4,6},{5,7},{6,4},{7,5},{8,10},{9,11},{10,... | collective-permute-start | bytes 589832 | tf_op jit(solution)/shard_map/ppermute | solution.py:26
  33.7 7.3 %copy-start = (bf16[1536,2048]{1,0:T(8,128)(2,1)}, bf16[1536,2048]{1,0:T(8,128)(2,1)S(1)}, u32[]{:S(2)}) copy-start(bf16[1536,2048]{1,0:T(8,128)(2,1)S(1)} %get-tuple-element.50.refs_2_) | copy-start | bytes 18874372
  34.5 6.6 %collective-permute-start.7 = (bf16[64,1664]{1,0:T(8,128)(2,1)S(1)}, bf16[64,1664]{1,0:T(8,128)(2,1)S(1)}, u32[]{:S(2)}, u32[]{:S(2)}) collective-permute-start(bf16[64,1664]{1,0:T(8,128)(2,1)S(1)} %get-tuple-element.48.token_ref.x_ref), channel_id=1, source_target_pairs={{0,1},{1,0},{2,3},{3,2},{4,5},{5,4},{6,7},{7,6},{8,9},{9,8},{10,11... | collective-permute-start | bytes 638984 | tf_op jit(solution)/shard_map/ppermute | solution.py:26
  36.1 6.3 %collective-permute-start.5 = (bf16[64,1664]{1,0:T(8,128)(2,1)S(1)}, bf16[64,1664]{1,0:T(8,128)(2,1)S(1)}, u32[]{:S(2)}, u32[]{:S(2)}) collective-permute-start(bf16[64,1664]{1,0:T(8,128)(2,1)S(1)} %get-tuple-element.48.token_ref.x_ref), channel_id=1, source_target_pairs={{0,8},{4,12},{8,0},{12,4},{1,9},{5,13},{9,1},{13,5},{2,10},{6,14},... | collective-permute-start | bytes 638984 | tf_op jit(solution)/shard_map/ppermute | solution.py:26
  41.0 5.3 %collective-permute-start.9 = (bf16[64,1664]{1,0:T(8,128)(2,1)S(1)}, bf16[64,1664]{1,0:T(8,128)(2,1)S(1)}, u32[]{:S(2)}, u32[]{:S(2)}) collective-permute-start(bf16[64,1664]{1,0:T(8,128)(2,1)S(1)} %get-tuple-element.48.token_ref.x_ref), channel_id=1, source_target_pairs={{0,4},{4,0},{8,12},{12,8},{1,5},{5,1},{9,13},{13,9},{2,6},{6,2},{1... | collective-permute-start | bytes 638984 | tf_op jit(solution)/shard_map/ppermute | solution.py:26
  41.1 5.2 %slice-start = ((s8[6291456]{0:T(1024)(128)(4,1)}), s8[4194304]{0:T(1024)(128)(4,1)S(1)}, s32[]{:S(2)}) async-start(s8[6291456]{0:T(1024)(128)(4,1)} %bitcast.4), calls=%async_computation | async-start | bytes 8388608
  41.1 5.2 %collective-permute-start.10 = (bf16[64,1664]{1,0:T(8,128)(2,1)S(1)}, bf16[64,1664]{1,0:T(8,128)(2,1)S(1)}, u32[]{:S(2)}, u32[]{:S(2)}) collective-permute-start(bf16[64,1664]{1,0:T(8,128)(2,1)S(1)} %passed_on.3.refs_1_), channel_id=1, source_target_pairs={{0,4},{4,0},{8,12},{12,8},{1,5},{5,1},{9,13},{13,9},{2,6},{6,2},{1... | collective-permute-start | bytes 638984 | tf_op jit(solution)/shard_map/ppermute | solution.py:26
  41.6 8.0 %collective-permute-start.8 = (bf16[64,1664]{1,0:T(8,128)(2,1)S(1)}, bf16[64,1664]{1,0:T(8,128)(2,1)S(1)}, u32[]{:S(2)}, u32[]{:S(2)}) collective-permute-start(bf16[64,1664]{1,0:T(8,128)(2,1)S(1)} %passed_on.3.refs_1_), channel_id=1, source_target_pairs={{0,8},{4,12},{8,0},{12,4},{1,9},{5,13},{9,1},{13,5},{2,10},{6,14},... | collective-permute-start | bytes 638984 | tf_op jit(solution)/shard_map/ppermute | solution.py:26
  42.4 3.9 %slice-start.1 = ((s8[6291456]{0:T(1024)(128)(4,1)}), s8[2097152]{0:T(1024)(128)(4,1)S(1)}, s32[]{:S(2)}) async-start(s8[6291456]{0:T(1024)(128)(4,1)} %bitcast.4), calls=%async_computation.1 | async-start | bytes 4194304
  45.8 7.4 %collective-permute-start.6 = (bf16[64,1664]{1,0:T(8,128)(2,1)S(1)}, bf16[64,1664]{1,0:T(8,128)(2,1)S(1)}, u32[]{:S(2)}, u32[]{:S(2)}) collective-permute-start(bf16[64,1664]{1,0:T(8,128)(2,1)S(1)} %collective-permute-done.5.refs_0_), channel_id=1, source_target_pairs={{0,4},{4,0},{8,12},{12,8},{1,5},{5,1},{9,13},{13,9},{2,6},{6,2},{1... | collective-permute-start | bytes 638984 | tf_op jit(solution)/shard_map/ppermute | solution.py:26
  49.7 3.6 %collective-permute-start.11 = (bf16[64,1664]{1,0:T(8,128)(2,1)S(1)}, bf16[64,1664]{1,0:T(8,128)(2,1)S(1)}, u32[]{:S(2)}, u32[]{:S(2)}) collective-permute-start(bf16[64,1664]{1,0:T(8,128)(2,1)S(1)} %passed_on.5.refs_1_), channel_id=1, source_target_pairs={{0,4},{4,0},{8,12},{12,8},{1,5},{5,1},{9,13},{13,9},{2,6},{6,2},{1... | collective-permute-start | bytes 638984 | tf_op jit(solution)/shard_map/ppermute | solution.py:26
  58.5 1.8 %collective-permute-start.13 = (bf16[128,1536]{1,0:T(8,128)(2,1)S(1)}, bf16[128,1536]{1,0:T(8,128)(2,1)S(1)}, u32[]{:S(2)}, u32[]{:S(2)}) collective-permute-start(bf16[128,1536]{1,0:T(8,128)(2,1)S(1)} %get-tuple-element.71), channel_id=1, source_target_pairs={{0,4},{4,0},{8,12},{12,8},{1,5},{5,1},{9,13},{13,9},{2,6},{6,2},{1... | collective-permute-start | bytes 1179656 | tf_op jit(solution)/shard_map/ppermute | solution.py:26
  58.9 3.5 %collective-permute-start.12 = (bf16[128,1536]{1,0:T(8,128)(2,1)S(1)}, bf16[128,1536]{1,0:T(8,128)(2,1)S(1)}, u32[]{:S(2)}, u32[]{:S(2)}) collective-permute-start(bf16[128,1536]{1,0:T(8,128)(2,1)S(1)} %get-tuple-element.69), channel_id=1, source_target_pairs={{0,4},{4,0},{8,12},{12,8},{1,5},{5,1},{9,13},{13,9},{2,6},{6,2},{1... | collective-permute-start | bytes 1179656 | tf_op jit(solution)/shard_map/ppermute | solution.py:26
  60.4 7.8 %collective-permute-start.15 = (bf16[64,1536]{1,0:T(8,128)(2,1)S(1)}, bf16[64,1536]{1,0:T(8,128)(2,1)S(1)}, u32[]{:S(2)}, u32[]{:S(2)}) collective-permute-start(bf16[64,1536]{1,0:T(8,128)(2,1)S(1)} %get-tuple-element.72.token_ref), channel_id=1, source_target_pairs={{0,8},{4,12},{8,0},{12,4},{1,9},{5,13},{9,1},{13,5},{2,10},{6,14},... | collective-permute-start | bytes 589832 | tf_op jit(solution)/shard_map/ppermute | solution.py:26
  61.7 10.1 %collective-permute-start.14 = (bf16[64,1536]{1,0:T(8,128)(2,1)S(1)}, bf16[64,1536]{1,0:T(8,128)(2,1)S(1)}, u32[]{:S(2)}, u32[]{:S(2)}) collective-permute-start(bf16[64,1536]{1,0:T(8,128)(2,1)S(1)} %get-tuple-element.74), channel_id=1, source_target_pairs={{0,8},{4,12},{8,0},{12,4},{1,9},{5,13},{9,1},{13,5},{2,10},{6,14},... | collective-permute-start | bytes 589832 | tf_op jit(solution)/shard_map/ppermute | solution.py:26
  68.2 5.9 %collective-permute-start.16 = (bf16[64,1536]{1,0:T(8,128)(2,1)S(1)}, bf16[64,1536]{1,0:T(8,128)(2,1)S(1)}, u32[]{:S(2)}, u32[]{:S(2)}) collective-permute-start(bf16[64,1536]{1,0:T(8,128)(2,1)S(1)} %add_convert_fusion), channel_id=1, source_target_pairs={{0,1},{1,0},{2,3},{3,2},{4,5},{5,4},{6,7},{7,6},{8,9},{9,8},{10,11... | collective-permute-start | bytes 589832 | tf_op jit(solution)/shard_map/ppermute | solution.py:26
  74.1 5.7 %collective-permute-start.17 = (bf16[32,1536]{1,0:T(8,128)(2,1)S(1)}, bf16[32,1536]{1,0:T(8,128)(2,1)S(1)}, u32[]{:S(2)}, u32[]{:S(2)}) collective-permute-start(bf16[32,1536]{1,0:T(8,128)(2,1)S(1)} %slice.15), channel_id=1, source_target_pairs={{0,2},{1,3},{2,0},{3,1},{4,6},{5,7},{6,4},{7,5},{8,10},{9,11},{10,... | collective-permute-start | bytes 294920 | tf_op jit(solution)/shard_map/ppermute | solution.py:26
